TPU v7x, 32 devices: a whole 2x2x4 slice. The times are simulated.
32 devices in a mesh: sens: 2 (over y), par: 16 (over z, x, core).
Axes of the slice: x: 2, y: 2, z: 4, core: 2. Of those that a mesh axis runs over, the one named last changes fastest.
Arguments:
- probes: bfloat16 [2, 256, 512], P(None, 'sens', 'par'), may hold values from -6 to 6
- green_blocks: bfloat16 [2, 16384, 256], P(None, 'par', 'sens'), may hold values from -0.375 to 0.375
- noise_table: float32 [4, 8], replicated, may hold values from 0.3 to 4
- station_class: int32 [256], P('sens'), may hold values from 0 to 7
- kappa_table: float32 [16], replicated, may hold values from 0.1 to 4
- coeff_index: int32 [4096], replicated, may hold values from 0 to 15
Outputs:
- hess_probes: float32 [2, 256, 512], P(None, 'sens', 'par')
All inputs are finite; a program needn't handle non-finite values.
Results may differ from a plain program's by a relative error of at most 0.003.
Values may be sent and summed in bfloat16 or wider, within the bound.
No kernel may reach another device: no remote copies, remote signals or barrier semaphores. Data moves between devices by JAX's collectives and lax.ppermute only.
A program may use at most 64 MiB of HBM per device.

v0:
```python
import jax
import jax.numpy as jnp
from jax import lax
from jax.sharding import PartitionSpec as P

SPLIT = 4
DIP = 32


def shortened(value):
    return jax.tree.map(lambda a: a.astype(jnp.bfloat16) if a.dtype == jnp.float32 else a, value)


def shifted(block, axis, distance):
    devices = range(lax.axis_size(axis))
    route = [(i - distance, i) for i in devices if i - distance in devices]
    return lax.ppermute(block, axis, route)


def swapped(value, axis, apart):
    return lax.ppermute(value, axis, [(i, i ^ 1 << apart) for i in range(lax.axis_size(axis))])


def neighbours(values, nfreq):
    left_rim = shifted(shortened(values[:, -1:]), "par", nfreq)
    right_rim = shifted(shortened(values[:, :1]), "par", -nfreq)
    along = jnp.concatenate([left_rim, values[:, :-1]], axis=1) + jnp.concatenate(
        [values[:, 1:], right_rim], axis=1
    )
    dipped = jnp.pad(values, ((0, 0), (0, 0), (1, 1), (0, 0)))
    return along + dipped[:, :, 2:] + dipped[:, :, :-2]


def sweeps(source, diagonal, nfreq):
    first_sweep = source / diagonal
    second_sweep = (source + neighbours(first_sweep, nfreq)) / diagonal
    return ((source + neighbours(second_sweep, nfreq)) / diagonal).astype(jnp.bfloat16)


def adjoint(green_part, probe_part):
    real_src = jnp.dot(green_part[0], probe_part[0], preferred_element_type=jnp.float32) + jnp.dot(
        green_part[1], probe_part[1], preferred_element_type=jnp.float32
    )
    imag_src = jnp.dot(green_part[0], probe_part[1], preferred_element_type=jnp.float32) - jnp.dot(
        green_part[1], probe_part[0], preferred_element_type=jnp.float32
    )
    return jnp.stack([real_src, imag_src])


def forward(green_part, slip_all):
    form = "cs,cr->sr"
    real_data = jnp.einsum(
        form, green_part[0], slip_all[0], preferred_element_type=jnp.float32
    ) - jnp.einsum(form, green_part[1], slip_all[1], preferred_element_type=jnp.float32)
    imag_data = jnp.einsum(
        form, green_part[0], slip_all[1], preferred_element_type=jnp.float32
    ) + jnp.einsum(form, green_part[1], slip_all[0], preferred_element_type=jnp.float32)
    return jnp.stack([real_data, imag_data])


def shards(probes, green_blocks, noise_table, station_class, kappa_table, coeff_index):
    cells_dev = green_blocks.shape[1]
    rows_dev = probes.shape[2]
    probe_count = rows_dev * SPLIT
    strike_dev = cells_dev // DIP
    nfreq = noise_table.shape[0]
    bit_count = SPLIT.bit_length() - 1
    bit_base = nfreq.bit_length() - 1
    highest = lax.Precision.HIGHEST
    par_index = lax.axis_index("par")
    freq_index = par_index % nfreq
    local_part = par_index // nfreq
    groups = noise_table.shape[1]
    station_hot = (station_class[:, None] == jnp.arange(groups, dtype=jnp.int32)[None, :]).astype(
        jnp.float32
    )
    variance = jnp.dot(station_hot, noise_table.T, precision=highest)
    weight = 1.0 / jnp.sqrt(variance)
    freq_hot = (jnp.arange(nfreq, dtype=jnp.int32) == freq_index).astype(jnp.float32)
    weight_col = jnp.dot(weight, freq_hot, precision=highest)
    joined = (weight_col[None, :, None] * probes.astype(jnp.float32)).astype(jnp.bfloat16)
    for bit_pos in range(bit_count):
        partner = swapped(joined, "par", bit_base + bit_pos)
        upper_side = par_index // 2 ** (bit_base + bit_pos) % 2 == 1
        joined = jnp.where(
            upper_side,
            jnp.concatenate([partner, joined], axis=2),
            jnp.concatenate([joined, partner], axis=2),
        )
    classes = kappa_table.shape[0]
    own_index = lax.dynamic_slice_in_dim(coeff_index, local_part * cells_dev, cells_dev, 0)
    class_hot = (own_index[:, None] == jnp.arange(classes, dtype=jnp.int32)[None, :]).astype(
        jnp.float32
    )
    kappa_cell = jnp.dot(class_hot, kappa_table, precision=highest)
    diagonal = (4.0 + kappa_cell).reshape(1, strike_dev, DIP, 1)
    green_all, probe_all = (
        lax.all_gather(green_blocks, "sens", axis=2, tiled=True),
        lax.all_gather(joined, "sens", axis=1, tiled=True),
    )
    source = adjoint(green_all, probe_all)
    slip_tile = sweeps(source.reshape(2, strike_dev, DIP, probe_count), diagonal, nfreq)
    slip_all = slip_tile.reshape(2, cells_dev, probe_count)
    partial_data = forward(green_blocks, slip_all)
    totals = partial_data
    for bit_pos in range(bit_count):
        totals = totals + swapped(totals, "par", bit_base + bit_pos)
    own_rows = lax.dynamic_slice_in_dim(totals, local_part * rows_dev, rows_dev, 2)
    return weight_col[None, :, None] * own_rows


def solution(mesh):
    in_specs = (P(None, "sens", "par"), P(None, "par", "sens"), P(), P("sens"), P(), P())
    out_specs = P(None, "sens", "par")
    return jax.shard_map(shards, mesh=mesh, in_specs=in_specs, out_specs=out_specs, check_vma=False)
```

profile of v0, /device:TPU:0, one launch (start us, length us, event | category | flops | bytes accessed | tf_op | source)
XLA Modules:
  0.0 79.2 jit_solution(4576016123673162143)
XLA Ops:
  6.5 0.7 all-gather.2.cloned.1.call-update
  7.3 0.9 %convolution_rsqrt_fusion = f32[128,4]{1,0:T(8,128)S(1)} fusion(f32[4,8]{1,0:T(4,128)S(1)} %copy-done, s32[128]{0:T(128)} %param.9), kind=kOutput, calls=%fused_computation.8 | convolution fusion | flops 50176 | bytes 2688 | tf_op jit(solution)/shard_map/dot_general | solution.py:77
  8.3 0.8 multiply_convert_fusion
  9.1 3.0 %collective-permute-start = (bf16[2,128,32]{1,2,0:T(8,128)(2,1)S(1)}, bf16[2,128,32]{1,2,0:T(8,128)(2,1)S(1)}, u32[]{:S(2)}, u32[]{:S(2)}) collective-permute-start(bf16[2,128,32]{1,2,0:T(8,128)(2,1)S(1)} %multiply_convert_fusion), channel_id=1, source_target_pairs={{0,4},{1,5},{2,6},{3,7},{4,0},{5,1},{6,2},{7,3},{8,12},{9,13},{10,... | collective-permute-start | bytes 49160 | tf_op jit(solution)/shard_map/ppermute | solution.py:21
  12.1 0.7 dynamic_slice.6
  12.8 1.1 %fusion.14 = f32[1,1024]{1,0:T(1,128)S(1)} fusion(s32[1024]{0:T(1024)S(1)} %dynamic_slice.6, f32[16]{0:T(128)} %param.10), kind=kOutput, calls=%fused_computation.30 | convolution fusion | flops 212992 | bytes 8256 | tf_op jit(solution)/shard_map/dot_general | solution.py:95
  13.9 3.0 %collective-permute-start.1 = (bf16[2,128,64]{1,2,0:T(8,128)(2,1)S(1)}, bf16[2,128,64]{1,2,0:T(8,128)(2,1)S(1)}, u32[]{:S(2)}, u32[]{:S(2)}) collective-permute-start(bf16[2,128,64]{1,2,0:T(8,128)(2,1)S(1)} %maximum_select_fusion.1), channel_id=1, source_target_pairs={{0,8},{1,9},{2,10},{3,11},{4,12},{5,13},{6,14},{7,15},{8,0},{9,1},... | collective-permute-start | bytes 98312 | tf_op jit(solution)/shard_map/ppermute | solution.py:21
  17.0 1.8 %collective-permute-done.1 = bf16[2,128,64]{1,2,0:T(8,128)(2,1)S(1)} collective-permute-done((bf16[2,128,64]{1,2,0:T(8,128)(2,1)S(1)}, bf16[2,128,64]{1,2,0:T(8,128)(2,1)S(1)}, u32[]{:S(2)}, u32[]{:S(2)}) %collective-permute-start.1) | collective-permute-done | bytes 32800 | tf_op jit(solution)/shard_map/ppermute | solution.py:21
  18.9 6.2 %all_gather.6 = bf16[2,256,128]{1,2,0:T(8,128)(2,1)S(1)} all-gather(bf16[2,128,128]{1,2,0:T(8,128)(2,1)S(1)} %maximum_select_fusion), channel_id=1, replica_groups=mesh['sens'=2,'par'=16] {'sens'}, dimensions={1}, use_global_device_ids=true | all-gather | bytes 196608 | tf_op jit(solution)/shard_map/all_gather | solution.py:99
  25.0 8.6 %all-gather.2.cloned.1.call-done = bf16[2,1024,256]{2,1,0:T(8,128)(2,1)} async-done(((bf16[2,1024,128]{2,1,0:T(8,128)(2,1)}), bf16[2,1024,256]{2,1,0:T(8,128)(2,1)}) %all-gather.2.cloned.1.call-update) | async-done | bytes 1048592 | tf_op jit(solution)/shard_map/all_gather | solution.py:98
  33.6 1.4 %fusion.15 = f32[128,1024]{1,0:T(8,128)S(1)} fusion(bf16[2,1024,256]{2,1,0:T(8,128)(2,1)} %all-gather.2.cloned.1.call-done, bf16[2,256,128]{1,2,0:T(8,128)(2,1)S(1)} %all_gather.6), kind=kOutput, calls=%fused_computation.31 | convolution fusion | flops 67108864 | bytes 1114112 | tf_op jit(solution)/shard_map/dot_general | solution.py:44
  35.1 0.3 fusion
  35.6 0.3 fusion.16
  35.9 0.3 fusion.1
  36.4 0.3 fusion.38
  36.7 3.4 %collective-permute-start.2 = (bf16[2,1,32,128]{3,2,1,0:T(8,128)(2,1)S(1)}, bf16[2,1,32,128]{3,2,1,0:T(8,128)(2,1)S(1)}, u32[]{:S(2)}, u32[]{:S(2)}) collective-permute-start(bf16[2,1,32,128]{3,2,1,0:T(8,128)(2,1)S(1)} %get-tuple-element.17), channel_id=1, source_target_pairs={{0,4},{1,5},{2,6},{3,7},{4,8},{5,9},{6,10},{7,11},{8,12},{9,13},{1... | collective-permute-start | bytes 49160 | tf_op jit(solution)/shard_map/ppermute | solution.py:17
  40.1 1.3 %collective-permute-start.3 = (bf16[2,1,32,128]{3,2,1,0:T(8,128)(2,1)S(1)}, bf16[2,1,32,128]{3,2,1,0:T(8,128)(2,1)S(1)}, u32[]{:S(2)}, u32[]{:S(2)}) collective-permute-start(bf16[2,1,32,128]{3,2,1,0:T(8,128)(2,1)S(1)} %get-tuple-element.18), channel_id=1, source_target_pairs={{4,0},{5,1},{6,2},{7,3},{8,4},{9,5},{10,6},{11,7},{12,8},{13,9},{1... | collective-permute-start | bytes 49160 | tf_op jit(solution)/shard_map/ppermute | solution.py:17
  41.7 4.0 %collective-permute-done.3 = bf16[2,1,32,128]{3,2,1,0:T(8,128)(2,1)S(1)} collective-permute-done((bf16[2,1,32,128]{3,2,1,0:T(8,128)(2,1)S(1)}, bf16[2,1,32,128]{3,2,1,0:T(8,128)(2,1)S(1)}, u32[]{:S(2)}, u32[]{:S(2)}) %collective-permute-start.3) | collective-permute-done | bytes 16416 | tf_op jit(solution)/shard_map/ppermute | solution.py:17
  45.7 0.7 fusion.36
  46.4 3.4 %collective-permute-start.4 = (bf16[2,1,32,128]{3,2,1,0:T(8,128)(2,1)S(1)}, bf16[2,1,32,128]{3,2,1,0:T(8,128)(2,1)S(1)}, u32[]{:S(2)}, u32[]{:S(2)}) collective-permute-start(bf16[2,1,32,128]{3,2,1,0:T(8,128)(2,1)S(1)} %get-tuple-element.15), channel_id=1, source_target_pairs={{0,4},{1,5},{2,6},{3,7},{4,8},{5,9},{6,10},{7,11},{8,12},{9,13},{1... | collective-permute-start | bytes 49160 | tf_op jit(solution)/shard_map/ppermute | solution.py:17
  49.8 1.3 %collective-permute-start.5 = (bf16[2,1,32,128]{3,2,1,0:T(8,128)(2,1)S(1)}, bf16[2,1,32,128]{3,2,1,0:T(8,128)(2,1)S(1)}, u32[]{:S(2)}, u32[]{:S(2)}) collective-permute-start(bf16[2,1,32,128]{3,2,1,0:T(8,128)(2,1)S(1)} %get-tuple-element.16), channel_id=1, source_target_pairs={{4,0},{5,1},{6,2},{7,3},{8,4},{9,5},{10,6},{11,7},{12,8},{13,9},{1... | collective-permute-start | bytes 49160 | tf_op jit(solution)/shard_map/ppermute | solution.py:17
  51.4 4.0 %collective-permute-done.5 = bf16[2,1,32,128]{3,2,1,0:T(8,128)(2,1)S(1)} collective-permute-done((bf16[2,1,32,128]{3,2,1,0:T(8,128)(2,1)S(1)}, bf16[2,1,32,128]{3,2,1,0:T(8,128)(2,1)S(1)}, u32[]{:S(2)}, u32[]{:S(2)}) %collective-permute-start.5) | collective-permute-done | bytes 16416 | tf_op jit(solution)/shard_map/ppermute | solution.py:17
  55.4 0.7 fusion.12
  56.2 1.0 %copy-done.1 = bf16[2,1024,128]{2,1,0:T(8,128)(2,1)S(1)} copy-done((bf16[2,1024,128]{2,1,0:T(8,128)(2,1)S(1)}, bf16[2,1024,128]{2,1,0:T(8,128)(2,1)}, u32[]{:S(2)}) %copy-start.1) | copy-done | bytes 524312
  57.2 0.3 fusion.19
  57.4 0.3 fusion.21
  57.7 0.3 fusion.2
  58.0 0.3 fusion.3
  58.3 1.6 %collective-permute-start.6 = (f32[2,128,128]{1,2,0:T(8,128)S(1)}, f32[2,128,128]{1,2,0:T(8,128)S(1)}, u32[]{:S(2)}, u32[]{:S(2)}) collective-permute-start(f32[2,128,128]{1,2,0:T(8,128)S(1)} %pad_maximum_fusion.1), channel_id=1, source_target_pairs={{0,4},{1,5},{2,6},{3,7},{4,0},{5,1},{6,2},{7,3},{8,12},{9,13},{10,... | collective-permute-start | bytes 393224 | tf_op jit(solution)/shard_map/ppermute | solution.py:21
  59.8 4.5 %collective-permute-done.6 = f32[2,128,128]{1,2,0:T(8,128)S(1)} collective-permute-done((f32[2,128,128]{1,2,0:T(8,128)S(1)}, f32[2,128,128]{1,2,0:T(8,128)S(1)}, u32[]{:S(2)}, u32[]{:S(2)}) %collective-permute-start.6) | collective-permute-done | bytes 131104 | tf_op jit(solution)/shard_map/ppermute | solution.py:21
  64.5 7.2 %collective-permute-done.7 = f32[2,128,128]{1,2,0:T(8,128)S(1)} collective-permute-done((f32[2,128,128]{1,2,0:T(8,128)S(1)}, f32[2,128,128]{1,2,0:T(8,128)S(1)}, u32[]{:S(2)}, u32[]{:S(2)}) %collective-permute-start.7) | collective-permute-done | bytes 131104 | tf_op jit(solution)/shard_map/ppermute | solution.py:21
  71.7 0.6 fusion.28
  (28 shorter events, 1.3 us)
Async XLA Ops:
  6.5 0.7 copy-start
  6.5 27.1 %all-gather.2.cloned.1.call-start = ((), (), s32[]{:S(2)}) async-start(), calls=%async_computation | async-start | bytes 1572864 | tf_op jit(solution)/shard_map/all_gather | solution.py:98
  9.1 4.8 %collective-permute-start = (bf16[2,128,32]{1,2,0:T(8,128)(2,1)S(1)}, bf16[2,128,32]{1,2,0:T(8,128)(2,1)S(1)}, u32[]{:S(2)}, u32[]{:S(2)}) collective-permute-start(bf16[2,128,32]{1,2,0:T(8,128)(2,1)S(1)} %multiply_convert_fusion), channel_id=1, source_target_pairs={{0,4},{1,5},{2,6},{3,7},{4,0},{5,1},{6,2},{7,3},{8,12},{9,13},{10,... | collective-permute-start | bytes 49160 | tf_op jit(solution)/shard_map/ppermute | solution.py:21
  13.9 4.9 %collective-permute-start.1 = (bf16[2,128,64]{1,2,0:T(8,128)(2,1)S(1)}, bf16[2,128,64]{1,2,0:T(8,128)(2,1)S(1)}, u32[]{:S(2)}, u32[]{:S(2)}) collective-permute-start(bf16[2,128,64]{1,2,0:T(8,128)(2,1)S(1)} %maximum_select_fusion.1), channel_id=1, source_target_pairs={{0,8},{1,9},{2,10},{3,11},{4,12},{5,13},{6,14},{7,15},{8,0},{9,1},... | collective-permute-start | bytes 98312 | tf_op jit(solution)/shard_map/ppermute | solution.py:21
  33.6 1.4 %copy-start.2 = (bf16[2,1024,256]{2,1,0:T(8,128)(2,1)S(1)}, bf16[2,1024,256]{2,1,0:T(8,128)(2,1)}, u32[]{:S(2)}) copy-start(bf16[2,1024,256]{2,1,0:T(8,128)(2,1)} %all-gather.2.cloned.1.call-done) | copy-start | bytes 3145732
  36.7 5.0 %collective-permute-start.2 = (bf16[2,1,32,128]{3,2,1,0:T(8,128)(2,1)S(1)}, bf16[2,1,32,128]{3,2,1,0:T(8,128)(2,1)S(1)}, u32[]{:S(2)}, u32[]{:S(2)}) collective-permute-start(bf16[2,1,32,128]{3,2,1,0:T(8,128)(2,1)S(1)} %get-tuple-element.17), channel_id=1, source_target_pairs={{0,4},{1,5},{2,6},{3,7},{4,8},{5,9},{6,10},{7,11},{8,12},{9,13},{1... | collective-permute-start | bytes 49160 | tf_op jit(solution)/shard_map/ppermute | solution.py:17
  40.1 5.6 %collective-permute-start.3 = (bf16[2,1,32,128]{3,2,1,0:T(8,128)(2,1)S(1)}, bf16[2,1,32,128]{3,2,1,0:T(8,128)(2,1)S(1)}, u32[]{:S(2)}, u32[]{:S(2)}) collective-permute-start(bf16[2,1,32,128]{3,2,1,0:T(8,128)(2,1)S(1)} %get-tuple-element.18), channel_id=1, source_target_pairs={{4,0},{5,1},{6,2},{7,3},{8,4},{9,5},{10,6},{11,7},{12,8},{13,9},{1... | collective-permute-start | bytes 49160 | tf_op jit(solution)/shard_map/ppermute | solution.py:17
  46.4 5.0 %collective-permute-start.4 = (bf16[2,1,32,128]{3,2,1,0:T(8,128)(2,1)S(1)}, bf16[2,1,32,128]{3,2,1,0:T(8,128)(2,1)S(1)}, u32[]{:S(2)}, u32[]{:S(2)}) collective-permute-start(bf16[2,1,32,128]{3,2,1,0:T(8,128)(2,1)S(1)} %get-tuple-element.15), channel_id=1, source_target_pairs={{0,4},{1,5},{2,6},{3,7},{4,8},{5,9},{6,10},{7,11},{8,12},{9,13},{1... | collective-permute-start | bytes 49160 | tf_op jit(solution)/shard_map/ppermute | solution.py:17
  49.8 5.6 %collective-permute-start.5 = (bf16[2,1,32,128]{3,2,1,0:T(8,128)(2,1)S(1)}, bf16[2,1,32,128]{3,2,1,0:T(8,128)(2,1)S(1)}, u32[]{:S(2)}, u32[]{:S(2)}) collective-permute-start(bf16[2,1,32,128]{3,2,1,0:T(8,128)(2,1)S(1)} %get-tuple-element.16), channel_id=1, source_target_pairs={{4,0},{5,1},{6,2},{7,3},{8,4},{9,5},{10,6},{11,7},{12,8},{13,9},{1... | collective-permute-start | bytes 49160 | tf_op jit(solution)/shard_map/ppermute | solution.py:17
  56.1 1.0 %copy-start.1 = (bf16[2,1024,128]{2,1,0:T(8,128)(2,1)S(1)}, bf16[2,1024,128]{2,1,0:T(8,128)(2,1)}, u32[]{:S(2)}) copy-start(bf16[2,1024,128]{2,1,0:T(8,128)(2,1)} %param.7) | copy-start | bytes 1572868
  58.3 6.1 %collective-permute-start.6 = (f32[2,128,128]{1,2,0:T(8,128)S(1)}, f32[2,128,128]{1,2,0:T(8,128)S(1)}, u32[]{:S(2)}, u32[]{:S(2)}) collective-permute-start(f32[2,128,128]{1,2,0:T(8,128)S(1)} %pad_maximum_fusion.1), channel_id=1, source_target_pairs={{0,4},{1,5},{2,6},{3,7},{4,0},{5,1},{6,2},{7,3},{8,12},{9,13},{10,... | collective-permute-start | bytes 393224 | tf_op jit(solution)/shard_map/ppermute | solution.py:21
  64.4 7.3 %collective-permute-start.7 = (f32[2,128,128]{1,2,0:T(8,128)S(1)}, f32[2,128,128]{1,2,0:T(8,128)S(1)}, u32[]{:S(2)}, u32[]{:S(2)}) collective-permute-start(f32[2,128,128]{1,2,0:T(8,128)S(1)} %fusion.35), channel_id=1, source_target_pairs={{0,8},{1,9},{2,10},{3,11},{4,12},{5,13},{6,14},{7,15},{8,0},{9,1},... | collective-permute-start | bytes 393224 | tf_op jit(solution)/shard_map/ppermute | solution.py:21
Sparse Core Ops, SparseCore 0:
  8.9 24.6 all-gather.1
where the time goes:
time: 79.6 us; the launch traced here: 79.2 us
  waiting for transfers between devices  31 us (39%)
  starting transfers between devices  17 us (21%)
  between operations  13.7 us (17%)
  blocking collectives  6.18 us (8%)
  matrix products  5.54 us (7%)
  other arithmetic  3.1 us (4%)
  local copies, waits for them, and re-layouts  2.7 us (3%)
    ppermute x4, waiting for transfers between devices, swapped(): lax.ppermute(value, axis, [(i, i ^ 1 << apart) for i in range(lax.axis_si...  13.6 us
    ppermute x4, starting transfers between devices, shifted(): return lax.ppermute(block, axis, route)  9.38 us
    all_gather x1, waiting for transfers between devices, shards(): lax.all_gather(green_blocks, 'sens', axis=2, tiled=True)  8.56 us
    ppermute x4, waiting for transfers between devices, shifted(): return lax.ppermute(block, axis, route)  8.09 us
    ppermute x4, starting transfers between devices, swapped(): lax.ppermute(value, axis, [(i, i ^ 1 << apart) for i in range(lax.axis_si...  7.65 us
    all_gather x1, blocking collectives, shards(): lax.all_gather(joined, 'sens', axis=1, tiled=True)  6.18 us
  transfers between devices with their start and end apart: 9, of which 6 were waited for; matrix products, arithmetic and copies ran while one was open for 5% of the time, Pallas kernels for 0%

commit v1 on v0

v1 whole, which is shorter than its diff:
```python
import functools

import jax
import jax.numpy as jnp
from jax import lax
from jax.experimental import pallas as pl
from jax.experimental.pallas import tpu as pltpu
from jax.sharding import PartitionSpec as P

SPLIT = 4
DIP = 32
LANES = 128
REACH = 2 * DIP
F32 = jnp.float32
BF16 = jnp.bfloat16


def swapped(value, axis, mask):
    return lax.ppermute(value, axis, [(i, i ^ mask) for i in range(lax.axis_size(axis))])


def turned(value, axis, step):
    size = lax.axis_size(axis)
    return lax.ppermute(value, axis, [(i, (i + step) % size) for i in range(size)])


def shifted(value, axis, step):
    size = lax.axis_size(axis)
    return lax.ppermute(value, axis, [(i, i + step) for i in range(size) if 0 <= i + step < size])


def dot(a, b, form=((1,), (0,))):
    return lax.dot_general(a, b, (form, ((), ())), preferred_element_type=F32)


def chosen(table, index, count, place):
    value = jnp.zeros(index.shape, F32)
    for k in range(count):
        value = jnp.where(index == k, place(table, k), value)
    return value


def stencil():
    row = lax.broadcasted_iota(jnp.int32, (4 * LANES, 2 * LANES), 0)
    col = lax.broadcasted_iota(jnp.int32, (4 * LANES, 2 * LANES), 1)
    away = row - LANES - col
    dip = lax.rem(col, DIP)
    hit = (away == DIP) | (away == -DIP)
    hit = hit | ((away == 1) & (dip != DIP - 1)) | ((away == -1) & (dip != 0))
    return hit.astype(F32).astype(BF16)


def local_kernel(nsens, nfreq, nclass, ngroup, noise, kappa, coeff, *refs):
    stations, refs = refs[:nsens], refs[nsens:]
    probes, refs = refs[:nsens], refs[nsens:]
    greens, refs = refs[:nsens], refs[nsens:]
    low, high, keep, send = refs
    par = lax.axis_index("par")
    freq = lax.rem(par, nfreq)
    part = lax.div(par, nfreq)
    cells = greens[0].shape[1]
    blocks = cells // LANES
    rows = probes[0].shape[0] * probes[0].shape[2]
    parts = coeff.shape[0] // blocks

    def weight(station):
        variance = chosen(noise, station[...], ngroup, lambda t, k: t[freq, k])
        return 1.0 / jnp.sqrt(variance)

    def inverse(index):
        return 1.0 / (4.0 + chosen(kappa, index, nclass, lambda t, k: t[k]))

    own = inverse(coeff[pl.ds(part * blocks, blocks), :])
    before = inverse(coeff[pl.ds(jnp.maximum(part * blocks - 1, 0), 1), :])
    after = inverse(coeff[pl.ds(jnp.minimum((part + 1) * blocks, parts * blocks - 1), 1), :])
    inv = [jnp.where(part > 0, before, 0.0)]
    inv += [own[b : b + 1] for b in range(blocks)]
    inv += [jnp.where(part < parts - 1, after, 0.0)]

    weights = [weight(s) for s in stations]
    lhs = []
    for w, p in zip(weights, probes):
        z = (w[None, None] * p[...].astype(F32)).astype(BF16)
        zr, zi = z[:, 0].reshape(rows, LANES), z[:, 1].reshape(rows, LANES)
        top = jnp.concatenate([zr, zi], axis=1)
        bottom = jnp.concatenate([zi, -zr], axis=1)
        lhs.append(jnp.concatenate([top, bottom], axis=0))

    def both(ref, b, n):
        return jnp.concatenate([ref[0, b : b + n], ref[1, b : b + n]], axis=1)

    wide = 2 * LANES
    source = []
    for b in range(0, cells, wide):
        total = dot(lhs[0], both(greens[0], b, wide), ((1,), (1,)))
        for a, g in zip(lhs[1:], greens[1:]):
            total = total + dot(a, both(g, b, wide), ((1,), (1,)))
        source += [total[:, :LANES], total[:, LANES:]]
    zero = jnp.zeros((2 * rows, LANES), BF16)
    hood = stencil()

    def sums(u):
        out = []
        for c in range(0, blocks + 2, 2):
            lo, hi = max(c - 1, 0), min(c + 3, blocks + 2)
            window = jnp.concatenate(u[lo:hi], axis=1)
            total = dot(window, hood[(lo - c + 1) * LANES : (hi - c + 1) * LANES])
            out += [total[:, :LANES], total[:, LANES:]]
        return out

    def solved(n):
        out = []
        for b in range(blocks + 2):
            inner = 0 < b <= blocks
            value = source[b - 1] + n[b] if inner else n[b]
            out.append((value * inv[b]).astype(BF16))
        return out

    first = [zero] + [(source[b] * inv[b + 1]).astype(BF16) for b in range(blocks)] + [zero]
    slip = solved(sums(solved(sums(first))))
    data = dot(jnp.concatenate(slip[1:-1], axis=1), both(greens[0], 0, cells))
    pad = jnp.zeros((LANES - REACH, 2 * LANES), BF16)
    data = data + dot(slip[0], jnp.concatenate([pad, both(low, 0, REACH)], axis=0))
    data = data + dot(slip[-1], jnp.concatenate([both(high, 0, REACH), pad], axis=0))
    real = weights[0] * (data[:rows, :LANES] - data[rows:, LANES:])
    imag = weights[0] * (data[rows:, :LANES] + data[:rows, LANES:])
    half = rows // 2
    keep[0], keep[1] = real[:half], imag[:half]
    send[0], send[1] = real[half:].astype(BF16), imag[half:].astype(BF16)


def shards(probes, green_blocks, noise_table, station_class, kappa_table, coeff_index):
    nfreq, ngroup = noise_table.shape
    nsens = lax.axis_size("sens")
    rows_dev = probes.shape[2]
    vector = jnp.transpose(probes, (0, 2, 1))
    station = station_class.reshape(1, -1)

    greens = [green_blocks] + [turned(green_blocks, "sens", k) for k in range(1, nsens)]
    mine = vector[None]
    for mask in (2 * nfreq, nfreq):
        mine = jnp.concatenate([mine, swapped(mine, "par", mask)], axis=0)
    low = shifted(green_blocks[:, -REACH:], "par", nfreq)
    high = shifted(green_blocks[:, :REACH], "par", -nfreq)
    vectors = [mine] + [turned(mine, "sens", k) for k in range(1, nsens)]
    stations = [station] + [turned(station, "sens", k) for k in range(1, nsens)]

    smem = pl.BlockSpec(memory_space=pltpu.SMEM)
    vmem = pl.BlockSpec(memory_space=pltpu.VMEM)
    half = SPLIT // 2 * rows_dev
    sensors = probes.shape[1]
    kernel = functools.partial(local_kernel, nsens, nfreq, kappa_table.shape[0], ngroup)
    keep, send = pl.pallas_call(
        kernel,
        out_shape=[
            jax.ShapeDtypeStruct((2, half, sensors), F32),
            jax.ShapeDtypeStruct((2, half, sensors), BF16),
        ],
        in_specs=[smem, smem] + [vmem] * (3 + 3 * nsens),
        out_specs=[vmem, vmem],
        compiler_params=pltpu.CompilerParams(vmem_limit_bytes=32 * 2**20),
    )(
        noise_table,
        kappa_table,
        coeff_index.reshape(-1, LANES),
        *stations,
        *vectors,
        *greens,
        low,
        high,
    )
    near = keep + swapped(send, "par", nfreq).astype(F32)
    far = swapped(near[:, rows_dev:].astype(BF16), "par", 2 * nfreq)
    return jnp.transpose(near[:, :rows_dev] + far.astype(F32), (0, 2, 1))


def solution(mesh):
    in_specs = (P(None, "sens", "par"), P(None, "par", "sens"), P(), P("sens"), P(), P())
    out_specs = P(None, "sens", "par")
    return jax.shard_map(shards, mesh=mesh, in_specs=in_specs, out_specs=out_specs, check_vma=False)
```

time: 79.6 us -> 35.8 us (0.45)
  waiting for transfers between devices: 31 us -> 10.5 us
  between operations: 13.7 us -> 0.13 us
  blocking collectives: 6.18 us -> 0 us
  matrix products: 5.54 us -> 0 us
  starting transfers between devices: 17 us -> 19.5 us
  Pallas kernels: 0 us -> 2.1 us
  other arithmetic: 3.1 us -> 1.36 us
  local copies, waits for them, and re-layouts: 2.7 us -> 1.86 us
    ppermute x8 -> x9, waiting for transfers between devices: 21.7 us -> 10.5 us  [the longest x4 7.1 us: swapped(): lax.ppermute(value, axis, [(i, i ^ mask) for i in range(lax.axis_size(axi...]
    all_gather x1 -> x0, waiting for transfers between devices: 8.56 us -> none  [shards(): lax.all_gather(green_blocks, 'sens', axis=2, tiled=True)]
    all_gather x1 -> x0, blocking collectives: 6.18 us -> none  [shards(): lax.all_gather(joined, 'sens', axis=1, tiled=True)]
    dot_general x11 -> x0, matrix products: 5.54 us -> none  [the longest x1 1.43 us: adjoint(): jnp.dot(green_part[0], probe_part[1], preferred_element_type=jnp.float32)]
    ppermute x8 -> x9, starting transfers between devices: 17 us -> 19.5 us  [the longest x4 10 us: swapped(): lax.ppermute(value, axis, [(i, i ^ mask) for i in range(lax.axis_size(axi...]
    pallas_call x0 -> x1, Pallas kernels: none -> 2.1 us  [shards(): pl.pallas_call(kernel, out_shape=[jax.ShapeDtypeStruct((2, half, sensors)...]
    convert_element_type x6 -> x0, other arithmetic: 1.48 us -> none  [the longest x1 0.79 us: shards(): (weight_col[None, :, None] * probes.astype(jnp.float32)).astype(jnp.bfloa...]
    another operation x3 -> x0, other arithmetic: 0.95 us -> none
  transfers between devices with their start and end apart: 9 -> 9, of which waited for: 6 -> 5; matrix products, arithmetic and copies ran while one was open for 5% -> 4% of each run, Pallas kernels for 0% -> 0%
where the time goes in v1:
time: 35.8 us; the launch traced here: 35.4 us
  starting transfers between devices  19.5 us (54%)
  waiting for transfers between devices  10.5 us (29%)
  Pallas kernels  2.1 us (6%)
  local copies, waits for them, and re-layouts  1.86 us (5%)
  other arithmetic  1.36 us (4%)
    ppermute x4, starting transfers between devices, swapped(): lax.ppermute(value, axis, [(i, i ^ mask) for i in range(lax.axis_size(axi...  10 us
    ppermute x4, waiting for transfers between devices, swapped(): lax.ppermute(value, axis, [(i, i ^ mask) for i in range(lax.axis_size(axi...  7.1 us
    ppermute x2, starting transfers between devices, shifted(): lax.ppermute(value, axis, [(i, i + step) for i in range(size) if 0 <= i +...  5.83 us
    ppermute x3, starting transfers between devices, turned(): lax.ppermute(value, axis, [(i, (i + step) % size) for i in range(size)])  3.68 us
    ppermute x3, waiting for transfers between devices, turned(): lax.ppermute(value, axis, [(i, (i + step) % size) for i in range(size)])  3.36 us
    pallas_call x1, Pallas kernels, shards(): pl.pallas_call(kernel, out_shape=[jax.ShapeDtypeStruct((2, half, sensors)...  2.1 us
    unnamed x12, local copies, waits for them, and re-layouts  1.06 us
    slice x1, local copies, waits for them, and re-layouts, shards(): high = shifted(green_blocks[:, :REACH], 'par', -nfreq)  0.79 us
  transfers between devices with their start and end apart: 9, of which 5 were waited for; matrix products, arithmetic and copies ran while one was open for 4% of the time, Pallas kernels for 0%

profile of v1, /device:TPU:0, one launch (start us, length us, event | category | flops | bytes accessed | tf_op | source)
XLA Modules:
  0.0 35.4 jit_solution(12962490847010432010)
XLA Ops:
  0.0 4.0 %collective-permute-start.1 = (bf16[1,2,32,128]{3,2,1,0:T(8,128)(2,1)}, bf16[1,2,32,128]{3,2,1,0:T(8,128)(2,1)S(1)}, u32[]{:S(2)}, u32[]{:S(2)}) collective-permute-start(bf16[1,2,32,128]{3,2,1,0:T(8,128)(2,1)} %bitcast.10), channel_id=1, source_target_pairs={{0,8},{1,9},{2,10},{3,11},{4,12},{5,13},{6,14},{7,15},{8,0},{9,1},... | collective-permute-start | bytes 49160 | tf_op jit(solution)/shard_map/ppermute | solution.py:19
  4.0 1.5 %collective-permute-start.4 = (bf16[2,1024,128]{2,1,0:T(8,128)(2,1)}, bf16[2,1024,128]{2,1,0:T(8,128)(2,1)S(1)}, u32[]{:S(2)}, u32[]{:S(2)}) collective-permute-start(bf16[2,1024,128]{2,1,0:T(8,128)(2,1)} %refs_4_.1), channel_id=1, source_target_pairs={{0,16},{16,0},{1,17},{17,1},{2,18},{18,2},{3,19},{19,3},{4,20},{20... | collective-permute-start | bytes 1572872 | tf_op jit(solution)/shard_map/ppermute | solution.py:24
  5.6 0.5 %collective-permute-done.1 = bf16[1,2,32,128]{3,2,1,0:T(8,128)(2,1)S(1)} collective-permute-done((bf16[1,2,32,128]{3,2,1,0:T(8,128)(2,1)}, bf16[1,2,32,128]{3,2,1,0:T(8,128)(2,1)S(1)}, u32[]{:S(2)}, u32[]{:S(2)}) %collective-permute-start.1) | collective-permute-done | bytes 16416 | tf_op jit(solution)/shard_map/ppermute | solution.py:19
  6.0 0.7 %pad_maximum_fusion.1 = bf16[2,2,32,128]{3,2,1,0:T(8,128)(2,1)S(1)} fusion(bf16[1,2,32,128]{3,2,1,0:T(8,128)(2,1)S(1)} %collective-permute-done.1, bf16[1,2,32,128]{3,2,1,0:T(8,128)(2,1)} %bitcast.11), kind=kLoop, calls=%fused_computation.5 | loop fusion | flops 16384 | bytes 65536 | tf_op jit(solution)/shard_map/concatenate | solution.py:142
  6.8 1.8 %collective-permute-start.2 = (bf16[2,2,32,128]{3,2,1,0:T(8,128)(2,1)S(1)}, bf16[2,2,32,128]{3,2,1,0:T(8,128)(2,1)S(1)}, u32[]{:S(2)}, u32[]{:S(2)}) collective-permute-start(bf16[2,2,32,128]{3,2,1,0:T(8,128)(2,1)S(1)} %pad_maximum_fusion.1), channel_id=1, source_target_pairs={{0,4},{1,5},{2,6},{3,7},{4,0},{5,1},{6,2},{7,3},{8,12},{9,13},{10,... | collective-permute-start | bytes 98312 | tf_op jit(solution)/shard_map/ppermute | solution.py:19
  8.6 2.1 %collective-permute-done.2 = bf16[2,2,32,128]{3,2,1,0:T(8,128)(2,1)S(1)} collective-permute-done((bf16[2,2,32,128]{3,2,1,0:T(8,128)(2,1)S(1)}, bf16[2,2,32,128]{3,2,1,0:T(8,128)(2,1)S(1)}, u32[]{:S(2)}, u32[]{:S(2)}) %collective-permute-start.2) | collective-permute-done | bytes 32800 | tf_op jit(solution)/shard_map/ppermute | solution.py:19
  10.7 0.0 copy-done.5
  10.7 1.9 %collective-permute-start.3 = (bf16[4,2,32,128]{3,2,1,0:T(8,128)(2,1)S(1)}, bf16[4,2,32,128]{3,2,1,0:T(8,128)(2,1)S(1)}, u32[]{:S(2)}, u32[]{:S(2)}) collective-permute-start(bf16[4,2,32,128]{3,2,1,0:T(8,128)(2,1)S(1)} %pad_maximum_fusion.refs_2_), channel_id=1, source_target_pairs={{0,16},{16,0},{1,17},{17,1},{2,18},{18,2},{3,19},{19,3},{4,20},{20... | collective-permute-start | bytes 196616 | tf_op jit(solution)/shard_map/ppermute | solution.py:24
  12.6 0.8 %fusion.1 = (bf16[2,64,128]{2,1,0:T(8,128)(2,1)S(1)}, bf16[2,64,128]{2,1,0:T(8,128)(2,1)S(1)}) fusion(bf16[2,1024,128]{2,1,0:T(8,128)(2,1)} %refs_4_.1), kind=kLoop, calls=%fused_computation.6 | loop fusion | bytes 131072 | tf_op jit(solution)/shard_map/slice | solution.py:144
  13.4 1.3 %collective-permute-start.6 = (bf16[2,64,128]{2,1,0:T(8,128)(2,1)S(1)}, bf16[2,64,128]{2,1,0:T(8,128)(2,1)S(1)}, u32[]{:S(2)}, u32[]{:S(2)}) collective-permute-start(bf16[2,64,128]{2,1,0:T(8,128)(2,1)S(1)} %get-tuple-element.9), channel_id=1, source_target_pairs={{4,0},{5,1},{6,2},{7,3},{8,4},{9,5},{10,6},{11,7},{12,8},{13,9},{1... | collective-permute-start | bytes 98312 | tf_op jit(solution)/shard_map/ppermute | solution.py:29
  14.7 0.0 copy-start.4
  14.7 0.0 copy-start.2
  14.7 4.5 %collective-permute-start.5 = (bf16[2,64,128]{2,1,0:T(8,128)(2,1)S(1)}, bf16[2,64,128]{2,1,0:T(8,128)(2,1)S(1)}, u32[]{:S(2)}, u32[]{:S(2)}) collective-permute-start(bf16[2,64,128]{2,1,0:T(8,128)(2,1)S(1)} %get-tuple-element.10), channel_id=1, source_target_pairs={{0,4},{1,5},{2,6},{3,7},{4,8},{5,9},{6,10},{7,11},{8,12},{9,13},{1... | collective-permute-start | bytes 98312 | tf_op jit(solution)/shard_map/ppermute | solution.py:29
  19.3 0.0 copy-done.4
  19.3 0.0 copy-start.3
  19.3 0.2 collective-permute-start
  19.5 3.4 %collective-permute-done.refs_1_ = s32[1,128]{1,0:T(1,128)S(1)} collective-permute-done((s32[1,128]{1,0:T(1,128)S(1)}, s32[1,128]{1,0:T(1,128)S(1)}, u32[]{:S(2)}, u32[]{:S(2)}) %collective-permute-start) | collective-permute-done | bytes 544 | tf_op jit(solution)/shard_map/ppermute | solution.py:24
  22.9 0.0 collective-permute-done.6.refs_7_
  22.9 0.0 collective-permute-done.5.refs_6_
  22.9 0.0 collective-permute-done.3.refs_3_
  22.9 0.0 collective-permute-done.4.refs_5_
  22.9 0.0 copy-done.1
  22.9 0.0 copy-done.2
  22.9 0.0 copy-done.3
  23.0 0.0 copy-start
  23.0 1.0 %copy-done = bf16[2,1024,128]{2,1,0:T(8,128)(2,1)S(1)} copy-done((bf16[2,1024,128]{2,1,0:T(8,128)(2,1)S(1)}, bf16[2,1024,128]{2,1,0:T(8,128)(2,1)}, u32[]{:S(2)}) %copy-start) | copy-done | bytes 524312
  24.0 2.1 %shard_map.64 = (f32[2,64,128]{2,1,0:T(8,128)S(1)}, bf16[2,64,128]{2,1,0:T(8,128)(2,1)S(1)}) custom-call(f32[4,8]{1,0:T(4,128)S(1)} %copy-done.2, f32[16]{0:T(128)S(1)} %copy-done.3, s32[32,128]{1,0:T(8,128)S(1)} %bitcast.7, s32[1,128]{1,0:T(1,128)S(1)} %bitcast.9, s32[1,128]{1,0:T(1,128)S(1)} %collective-permute-done.refs_1_, ...), custom_call_target="tpu_custom_call" | custom-call | tf_op jit(solution)/shard_map/pallas_call | solution.py:153
  26.1 1.6 %collective-permute-start.7 = (bf16[2,64,128]{2,1,0:T(8,128)(2,1)S(1)}, bf16[2,64,128]{2,1,0:T(8,128)(2,1)S(1)}, u32[]{:S(2)}, u32[]{:S(2)}) collective-permute-start(bf16[2,64,128]{2,1,0:T(8,128)(2,1)S(1)} %get-tuple-element.8), channel_id=1, source_target_pairs={{0,4},{1,5},{2,6},{3,7},{4,0},{5,1},{6,2},{7,3},{8,12},{9,13},{10,... | collective-permute-start | bytes 98312 | tf_op jit(solution)/shard_map/ppermute | solution.py:19
  27.7 2.4 %collective-permute-done.7 = bf16[2,64,128]{2,1,0:T(8,128)(2,1)S(1)} collective-permute-done((bf16[2,64,128]{2,1,0:T(8,128)(2,1)S(1)}, bf16[2,64,128]{2,1,0:T(8,128)(2,1)S(1)}, u32[]{:S(2)}, u32[]{:S(2)}) %collective-permute-start.7) | collective-permute-done | bytes 32800 | tf_op jit(solution)/shard_map/ppermute | solution.py:19
  30.1 2.6 %collective-permute-start.8 = (bf16[2,32,128]{2,1,0:T(8,128)(2,1)S(1)}, bf16[2,32,128]{2,1,0:T(8,128)(2,1)S(1)}, u32[]{:S(2)}, u32[]{:S(2)}) collective-permute-start(bf16[2,32,128]{2,1,0:T(8,128)(2,1)S(1)} %slice.23), channel_id=1, source_target_pairs={{0,8},{1,9},{2,10},{3,11},{4,12},{5,13},{6,14},{7,15},{8,0},{9,1},... | collective-permute-start | bytes 49160 | tf_op jit(solution)/shard_map/ppermute | solution.py:19
  32.7 2.1 %collective-permute-done.8 = bf16[2,32,128]{2,1,0:T(8,128)(2,1)S(1)} collective-permute-done((bf16[2,32,128]{2,1,0:T(8,128)(2,1)S(1)}, bf16[2,32,128]{2,1,0:T(8,128)(2,1)S(1)}, u32[]{:S(2)}, u32[]{:S(2)}) %collective-permute-start.8) | collective-permute-done | bytes 16416 | tf_op jit(solution)/shard_map/ppermute | solution.py:19
  34.8 0.6 %fusion = f32[2,128,32]{1,2,0:T(8,128)} fusion(f32[2,64,128]{2,1,0:T(8,128)S(1)} %convert_add_fusion, bf16[2,32,128]{2,1,0:T(8,128)(2,1)S(1)} %collective-permute-done.8), kind=kLoop, calls=%fused_computation.4 | loop fusion | flops 16384 | bytes 81920 | tf_op jit(solution)/shard_map/transpose | solution.py:174
  (5 shorter events, 0.0 us)
Async XLA Ops:
  0.0 10.7 %copy-start.5 = (bf16[2,128,32]{1,2,0:T(8,128)(2,1)S(1)}, bf16[2,128,32]{1,2,0:T(8,128)(2,1)}, u32[]{:S(2)}) copy-start(bf16[2,128,32]{1,2,0:T(8,128)(2,1)} %param.6) | copy-start | bytes 49156
  0.0 6.0 %collective-permute-start.1 = (bf16[1,2,32,128]{3,2,1,0:T(8,128)(2,1)}, bf16[1,2,32,128]{3,2,1,0:T(8,128)(2,1)S(1)}, u32[]{:S(2)}, u32[]{:S(2)}) collective-permute-start(bf16[1,2,32,128]{3,2,1,0:T(8,128)(2,1)} %bitcast.10), channel_id=1, source_target_pairs={{0,8},{1,9},{2,10},{3,11},{4,12},{5,13},{6,14},{7,15},{8,0},{9,1},... | collective-permute-start | bytes 49160 | tf_op jit(solution)/shard_map/ppermute | solution.py:19
  4.0 18.9 %collective-permute-start.4 = (bf16[2,1024,128]{2,1,0:T(8,128)(2,1)}, bf16[2,1024,128]{2,1,0:T(8,128)(2,1)S(1)}, u32[]{:S(2)}, u32[]{:S(2)}) collective-permute-start(bf16[2,1024,128]{2,1,0:T(8,128)(2,1)} %refs_4_.1), channel_id=1, source_target_pairs={{0,16},{16,0},{1,17},{17,1},{2,18},{18,2},{3,19},{19,3},{4,20},{20... | collective-permute-start | bytes 1572872 | tf_op jit(solution)/shard_map/ppermute | solution.py:24
  6.8 3.9 %collective-permute-start.2 = (bf16[2,2,32,128]{3,2,1,0:T(8,128)(2,1)S(1)}, bf16[2,2,32,128]{3,2,1,0:T(8,128)(2,1)S(1)}, u32[]{:S(2)}, u32[]{:S(2)}) collective-permute-start(bf16[2,2,32,128]{3,2,1,0:T(8,128)(2,1)S(1)} %pad_maximum_fusion.1), channel_id=1, source_target_pairs={{0,4},{1,5},{2,6},{3,7},{4,0},{5,1},{6,2},{7,3},{8,12},{9,13},{10,... | collective-permute-start | bytes 98312 | tf_op jit(solution)/shard_map/ppermute | solution.py:19
  10.7 12.2 %collective-permute-start.3 = (bf16[4,2,32,128]{3,2,1,0:T(8,128)(2,1)S(1)}, bf16[4,2,32,128]{3,2,1,0:T(8,128)(2,1)S(1)}, u32[]{:S(2)}, u32[]{:S(2)}) collective-permute-start(bf16[4,2,32,128]{3,2,1,0:T(8,128)(2,1)S(1)} %pad_maximum_fusion.refs_2_), channel_id=1, source_target_pairs={{0,16},{16,0},{1,17},{17,1},{2,18},{18,2},{3,19},{19,3},{4,20},{20... | collective-permute-start | bytes 196616 | tf_op jit(solution)/shard_map/ppermute | solution.py:24
  12.6 10.3 %copy-start.1 = (s32[4096]{0:T(1024)S(1)}, s32[4096]{0:T(1024)}, u32[]{:S(2)}) copy-start(s32[4096]{0:T(1024)} %param.11) | copy-start | bytes 49156
  13.4 9.5 %collective-permute-start.6 = (bf16[2,64,128]{2,1,0:T(8,128)(2,1)S(1)}, bf16[2,64,128]{2,1,0:T(8,128)(2,1)S(1)}, u32[]{:S(2)}, u32[]{:S(2)}) collective-permute-start(bf16[2,64,128]{2,1,0:T(8,128)(2,1)S(1)} %get-tuple-element.9), channel_id=1, source_target_pairs={{4,0},{5,1},{6,2},{7,3},{8,4},{9,5},{10,6},{11,7},{12,8},{13,9},{1... | collective-permute-start | bytes 98312 | tf_op jit(solution)/shard_map/ppermute | solution.py:29
  14.7 4.6 %copy-start.4 = (s32[128]{0:T(128)S(1)}, s32[128]{0:T(128)}, u32[]{:S(2)}) copy-start(s32[128]{0:T(128)} %param.9) | copy-start | bytes 1540
  14.7 8.2 %copy-start.2 = (f32[4,8]{1,0:T(4,128)S(1)}, f32[4,8]{1,0:T(4,128)}, u32[]{:S(2)}) copy-start(f32[4,8]{1,0:T(4,128)} %noise.1) | copy-start | bytes 388
  14.7 8.2 %collective-permute-start.5 = (bf16[2,64,128]{2,1,0:T(8,128)(2,1)S(1)}, bf16[2,64,128]{2,1,0:T(8,128)(2,1)S(1)}, u32[]{:S(2)}, u32[]{:S(2)}) collective-permute-start(bf16[2,64,128]{2,1,0:T(8,128)(2,1)S(1)} %get-tuple-element.10), channel_id=1, source_target_pairs={{0,4},{1,5},{2,6},{3,7},{4,8},{5,9},{6,10},{7,11},{8,12},{9,13},{1... | collective-permute-start | bytes 98312 | tf_op jit(solution)/shard_map/ppermute | solution.py:29
  19.3 3.7 %copy-start.3 = (f32[16]{0:T(128)S(1)}, f32[16]{0:T(128)}, u32[]{:S(2)}) copy-start(f32[16]{0:T(128)} %kappa.1) | copy-start | bytes 196
  19.3 3.6 %collective-permute-start = (s32[1,128]{1,0:T(1,128)S(1)}, s32[1,128]{1,0:T(1,128)S(1)}, u32[]{:S(2)}, u32[]{:S(2)}) collective-permute-start(s32[1,128]{1,0:T(1,128)S(1)} %bitcast.8), channel_id=1, source_target_pairs={{0,16},{16,0},{1,17},{17,1},{2,18},{18,2},{3,19},{19,3},{4,20},{20... | collective-permute-start | bytes 1544 | tf_op jit(solution)/shard_map/ppermute | solution.py:24
  23.0 1.0 %copy-start = (bf16[2,1024,128]{2,1,0:T(8,128)(2,1)S(1)}, bf16[2,1024,128]{2,1,0:T(8,128)(2,1)}, u32[]{:S(2)}) copy-start(bf16[2,1024,128]{2,1,0:T(8,128)(2,1)} %refs_4_.1) | copy-start | bytes 1572868
  26.1 4.0 %collective-permute-start.7 = (bf16[2,64,128]{2,1,0:T(8,128)(2,1)S(1)}, bf16[2,64,128]{2,1,0:T(8,128)(2,1)S(1)}, u32[]{:S(2)}, u32[]{:S(2)}) collective-permute-start(bf16[2,64,128]{2,1,0:T(8,128)(2,1)S(1)} %get-tuple-element.8), channel_id=1, source_target_pairs={{0,4},{1,5},{2,6},{3,7},{4,0},{5,1},{6,2},{7,3},{8,12},{9,13},{10,... | collective-permute-start | bytes 98312 | tf_op jit(solution)/shard_map/ppermute | solution.py:19
  30.1 4.7 %collective-permute-start.8 = (bf16[2,32,128]{2,1,0:T(8,128)(2,1)S(1)}, bf16[2,32,128]{2,1,0:T(8,128)(2,1)S(1)}, u32[]{:S(2)}, u32[]{:S(2)}) collective-permute-start(bf16[2,32,128]{2,1,0:T(8,128)(2,1)S(1)} %slice.23), channel_id=1, source_target_pairs={{0,8},{1,9},{2,10},{3,11},{4,12},{5,13},{6,14},{7,15},{8,0},{9,1},... | collective-permute-start | bytes 49160 | tf_op jit(solution)/shard_map/ppermute | solution.py:19

commit v2 on v1

v2 whole, which is shorter than its diff:
```python
import functools

import jax
import jax.numpy as jnp
from jax import lax
from jax.experimental import pallas as pl
from jax.experimental.pallas import tpu as pltpu
from jax.sharding import PartitionSpec as P

SPLIT = 4
DIP = 32
LANES = 128
REACH = 2 * DIP
F32 = jnp.float32
BF16 = jnp.bfloat16
PARAMS = pltpu.CompilerParams(vmem_limit_bytes=32 * 2**20)


def swapped(value, axis, mask):
    return lax.ppermute(value, axis, [(i, i ^ mask) for i in range(lax.axis_size(axis))])


def turned(value, axis, step):
    size = lax.axis_size(axis)
    return lax.ppermute(value, axis, [(i, (i + step) % size) for i in range(size)])


def crossed(value, axis, nfreq):
    pairs = [(p * nfreq + f, (p + 1) * nfreq + f) for p in range(1, SPLIT - 1, 2) for f in range(nfreq)]
    return lax.ppermute(value, axis, pairs + [(b, a) for a, b in pairs])


def dot(a, b, form=((1,), (0,))):
    return lax.dot_general(a, b, (form, ((), ())), preferred_element_type=F32)


def chosen(table, index, count, place):
    value = jnp.zeros(index.shape, F32)
    for k in range(count):
        value = jnp.where(index == k, place(table, k), value)
    return value


def stencil():
    row = lax.broadcasted_iota(jnp.int32, (4 * LANES, 2 * LANES), 0)
    col = lax.broadcasted_iota(jnp.int32, (4 * LANES, 2 * LANES), 1)
    away = row - LANES - col
    dip = lax.rem(col, DIP)
    hit = (away == DIP) | (away == -DIP)
    hit = hit | ((away == 1) & (dip != DIP - 1)) | ((away == -1) & (dip != 0))
    return hit.astype(F32).astype(BF16)


def planes(ref, b, n):
    return jnp.concatenate([ref[0, b : b + n], ref[1, b : b + n]], axis=1)


def lhs(z):
    rows = z.shape[0] * z.shape[2]
    zr, zi = z[:, 0].reshape(rows, LANES), z[:, 1].reshape(rows, LANES)
    top = jnp.concatenate([zr, zi], axis=1)
    return jnp.concatenate([top, jnp.concatenate([zi, -zr], axis=1)], axis=0)


def own_kernel(nfreq, nclass, kappa, coeff, vector, green, operator, source, inverse, hood):
    part = lax.div(lax.axis_index("par"), nfreq)
    cells = green.shape[1]
    blocks = cells // LANES
    parts = coeff.shape[0] // blocks

    def inv(index):
        return 1.0 / (4.0 + chosen(kappa, index, nclass, lambda t, k: t[k]))

    before = inv(coeff[pl.ds(jnp.maximum(part * blocks - 1, 0), 1), :])
    after = inv(coeff[pl.ds(jnp.minimum((part + 1) * blocks, parts * blocks - 1), 1), :])
    inverse[0:blocks, :] = inv(coeff[pl.ds(part * blocks, blocks), :])
    inverse[blocks : blocks + 1, :] = jnp.where(part < parts - 1, after, 0.0)
    inverse[blocks + 1 : blocks + 2, :] = jnp.where(part > 0, before, 0.0)
    hood[...] = stencil()
    both = planes(green, 0, cells)
    operator[...] = both
    source[...] = dot(lhs(vector[...]), both, ((1,), (1,)))


def slip_kernel(nfreq, nsens, weight, inverse, hood, source, operator, facing, other, *refs):
    vectors, refs = refs[: nsens - 1], refs[nsens - 1 :]
    greens, (keep, send) = refs[: nsens - 1], refs[nsens - 1 :]
    part = lax.div(lax.axis_index("par"), nfreq)
    cells = operator.shape[0]
    blocks = cells // LANES
    rows = source.shape[0] // 2
    inv = [inverse[(b - 1) % (blocks + 2) : (b - 1) % (blocks + 2) + 1] for b in range(blocks + 2)]
    left = [lhs(v[...]) for v in vectors]
    wide = 2 * LANES
    src = []
    for b in range(0, cells, wide):
        total = source[:, b : b + wide]
        for a, g in zip(left, greens):
            total = total + dot(a, planes(g, b, wide), ((1,), (1,)))
        src += [total[:, :LANES], total[:, LANES:]]
    zero = jnp.zeros((2 * rows, LANES), BF16)

    def sums(u):
        out = []
        for c in range(0, blocks + 2, 2):
            lo, hi = max(c - 1, 0), min(c + 3, blocks + 2)
            window = jnp.concatenate(u[lo:hi], axis=1)
            total = dot(window, hood[(lo - c + 1) * LANES : (hi - c + 1) * LANES])
            out += [total[:, :LANES], total[:, LANES:]]
        return out

    def solved(n):
        out = []
        for b in range(blocks + 2):
            value = src[b - 1] + n[b] if 0 < b <= blocks else n[b]
            out.append((value * inv[b]).astype(BF16))
        return out

    first = [zero] + [(src[b] * inv[b + 1]).astype(BF16) for b in range(blocks)] + [zero]
    slip = solved(sums(solved(sums(first))))
    data = dot(jnp.concatenate(slip[1:-1], axis=1), operator[...])
    odd = lax.rem(part, 2) == 1
    near, far = planes(facing.at[1], 0, REACH), planes(other, 0, REACH)
    low, high = jnp.where(odd, near, far), jnp.where(odd, far, near)
    pad = jnp.zeros((LANES - REACH, wide), BF16)
    data = data + dot(slip[0], jnp.concatenate([pad, low], axis=0))
    data = data + dot(slip[-1], jnp.concatenate([high, pad], axis=0))
    real = weight[...] * (data[:rows, :LANES] - data[rows:, LANES:])
    imag = weight[...] * (data[rows:, :LANES] + data[:rows, LANES:])
    half = rows // 2
    keep[0], keep[1] = real[:half], imag[:half]
    send[0], send[1] = real[half:].astype(BF16), imag[half:].astype(BF16)


def shards(probes, green_blocks, noise_table, station_class, kappa_table, coeff_index):
    nfreq, ngroup = noise_table.shape
    nsens = lax.axis_size("sens")
    sensors, rows_dev = probes.shape[1:]
    cells = green_blocks.shape[1]
    par = lax.axis_index("par")
    odd = par // nfreq % 2 == 1
    vector = jnp.transpose(probes, (0, 2, 1))

    greens = [turned(green_blocks, "sens", k) for k in range(1, nsens)]
    partner = swapped(vector, "par", 2 * nfreq)

    variances = lax.dynamic_index_in_dim(noise_table, par % nfreq, 0)
    member = station_class[None, :] == jnp.arange(ngroup, dtype=jnp.int32)[:, None]
    variance = jnp.sum(jnp.where(member, variances.reshape(ngroup, 1), 0.0), axis=0, keepdims=True)
    weight = 1.0 / jnp.sqrt(variance)

    first, last = green_blocks[:, :REACH], green_blocks[:, -REACH:]
    facing, other = jnp.where(odd, first, last), jnp.where(odd, last, first)

    mine = jnp.stack([vector, partner])
    sent = jnp.stack([mine.reshape(2, -1, sensors), facing])
    got = swapped(sent, "par", nfreq)
    other = crossed(other, "par", nfreq)
    raw = jnp.concatenate([mine, got[0].reshape(mine.shape)], axis=0)
    vectors = (weight[None, None] * raw.astype(F32)).astype(BF16)
    rest = [turned(vectors, "sens", k) for k in range(1, nsens)]

    smem = pl.BlockSpec(memory_space=pltpu.SMEM)
    vmem = pl.BlockSpec(memory_space=pltpu.VMEM)
    rows = SPLIT * rows_dev
    operator, source, inverse, hood = pl.pallas_call(
        functools.partial(own_kernel, nfreq, kappa_table.shape[0]),
        out_shape=[
            jax.ShapeDtypeStruct((cells, 2 * sensors), BF16),
            jax.ShapeDtypeStruct((2 * rows, cells), F32),
            jax.ShapeDtypeStruct((cells // LANES + 2, LANES), F32),
            jax.ShapeDtypeStruct((4 * LANES, 2 * LANES), BF16),
        ],
        in_specs=[smem] + [vmem] * 3,
        out_specs=[vmem] * 4,
        compiler_params=PARAMS,
        name="own",
    )(kappa_table, coeff_index.reshape(-1, LANES), vectors, green_blocks)
    keep, send = pl.pallas_call(
        functools.partial(slip_kernel, nfreq, nsens),
        out_shape=[
            jax.ShapeDtypeStruct((2, rows // 2, sensors), F32),
            jax.ShapeDtypeStruct((2, rows // 2, sensors), BF16),
        ],
        in_specs=[vmem] * (5 + 2 * nsens),
        out_specs=[vmem] * 2,
        compiler_params=PARAMS,
        name="slip",
    )(weight, inverse, hood, source, operator, got, other, *rest, *greens)
    near = keep + swapped(send, "par", nfreq).astype(F32)
    far = swapped(near[:, rows_dev:].astype(BF16), "par", 2 * nfreq)
    return jnp.transpose(near[:, :rows_dev] + far.astype(F32), (0, 2, 1))


def solution(mesh):
    in_specs = (P(None, "sens", "par"), P(None, "par", "sens"), P(), P("sens"), P(), P())
    out_specs = P(None, "sens", "par")
    return jax.shard_map(shards, mesh=mesh, in_specs=in_specs, out_specs=out_specs, check_vma=False)
```

time: 35.8 us -> 30.4 us (0.85)
  starting transfers between devices: 19.5 us -> 14 us
  other arithmetic: 1.36 us -> 3.64 us
  local copies, waits for them, and re-layouts: 1.86 us -> 0.03 us
  waiting for transfers between devices: 10.5 us -> 9.79 us
  Pallas kernels: 2.1 us -> 2.47 us
    ppermute x2 -> x1, starting transfers between devices: 5.83 us -> 0.78 us  [crossed(): return lax.ppermute(value, axis, pairs + [(b, a) for a, b in pairs])]
    ppermute x3 -> x2, starting transfers between devices: 3.68 us -> 2.32 us  [turned(): lax.ppermute(value, axis, [(i, (i + step) % size) for i in range(size)])]
    unnamed x12 -> x8, local copies, waits for them, and re-layouts: 1.06 us -> 0.02 us
    ppermute x4, starting transfers between devices: 10 us -> 10.9 us  [swapped(): lax.ppermute(value, axis, [(i, i ^ mask) for i in range(lax.axis_size(axi...]
    select_n x0 -> x1, other arithmetic: none -> 0.8 us  [shards(): facing, other = (jnp.where(odd, first, last), jnp.where(odd, last, first))]
    ppermute x4, waiting for transfers between devices: 7.1 us -> 6.3 us  [swapped(): lax.ppermute(value, axis, [(i, i ^ mask) for i in range(lax.axis_size(axi...]
    slice x1, local copies, waits for them, and re-layouts: 0.79 us -> 0.01 us  [shards(): raw = jnp.concatenate([mine, got[0].reshape(mine.shape)], axis=0)]
    convert_element_type x0 -> x1, other arithmetic: none -> 0.75 us  [shards(): vectors = (weight[None, None] * raw.astype(F32)).astype(BF16)]
  transfers between devices with their start and end apart: 9 -> 7, of which waited for: 5 -> 4; matrix products, arithmetic and copies ran while one was open for 4% -> 10% of each run, Pallas kernels for 0% -> 3%
where the time goes in v2:
time: 30.4 us; the launch traced here: 30.1 us
  starting transfers between devices  14 us (46%)
  waiting for transfers between devices  9.79 us (32%)
  other arithmetic  3.64 us (12%)
  Pallas kernels  2.47 us (8%)
    ppermute x4, starting transfers between devices, swapped(): lax.ppermute(value, axis, [(i, i ^ mask) for i in range(lax.axis_size(axi...  10.9 us
    ppermute x4, waiting for transfers between devices, swapped(): lax.ppermute(value, axis, [(i, i ^ mask) for i in range(lax.axis_size(axi...  6.3 us
    ppermute x2, waiting for transfers between devices, turned(): lax.ppermute(value, axis, [(i, (i + step) % size) for i in range(size)])  3.48 us
    ppermute x2, starting transfers between devices, turned(): lax.ppermute(value, axis, [(i, (i + step) % size) for i in range(size)])  2.32 us
    pallas_call x1, Pallas kernels, shards(): pl.pallas_call(functools.partial(slip_kernel, nfreq, nsens), out_shape=[j...  1.44 us
    pallas_call x1, Pallas kernels, shards(): pl.pallas_call(functools.partial(own_kernel, nfreq, kappa_table.shape[0])...  1.03 us
    select_n x1, other arithmetic, shards(): facing, other = (jnp.where(odd, first, last), jnp.where(odd, last, first))  0.8 us
    ppermute x1, starting transfers between devices, crossed(): return lax.ppermute(value, axis, pairs + [(b, a) for a, b in pairs])  0.78 us
  transfers between devices with their start and end apart: 7, of which 4 were waited for; matrix products, arithmetic and copies ran while one was open for 10% of the time, Pallas kernels for 3%

profile of v2, /device:TPU:0, one launch (start us, length us, event | category | flops | bytes accessed | tf_op | source)
XLA Modules:
  0.0 30.1 jit_solution(3594245642377804830)
XLA Ops:
  0.0 0.0 copy-start
  0.0 0.0 copy-start.1
  0.0 4.0 %collective-permute-start = (bf16[2,32,128]{2,1,0:T(8,128)(2,1)}, bf16[2,32,128]{2,1,0:T(8,128)(2,1)S(1)}, u32[]{:S(2)}, u32[]{:S(2)}) collective-permute-start(bf16[2,32,128]{2,1,0:T(8,128)(2,1)} %bitcast.19), channel_id=1, source_target_pairs={{0,8},{1,9},{2,10},{3,11},{4,12},{5,13},{6,14},{7,15},{8,0},{9,1},... | collective-permute-start | bytes 49160 | tf_op jit(solution)/shard_map/ppermute | solution.py:20
  4.0 1.5 %collective-permute-start.4 = (bf16[2,1024,128]{2,1,0:T(8,128)(2,1)}, bf16[2,1024,128]{2,1,0:T(8,128)(2,1)S(1)}, u32[]{:S(2)}, u32[]{:S(2)}) collective-permute-start(bf16[2,1024,128]{2,1,0:T(8,128)(2,1)} %green.1), channel_id=1, source_target_pairs={{0,16},{16,0},{1,17},{17,1},{2,18},{18,2},{3,19},{19,3},{4,20},{20... | collective-permute-start | bytes 1572872 | tf_op jit(solution)/shard_map/ppermute | solution.py:25
  5.6 0.8 %broadcast_select_fusion = (bf16[2,64,128]{2,1,0:T(8,128)(2,1)S(1)}, bf16[1,2,64,128]{3,2,1,0:T(8,128)(2,1)S(1)}) fusion(pred[]{:T(512)S(6)} %eq.22, bf16[2,1024,128]{2,1,0:T(8,128)(2,1)} %green.1), kind=kLoop, calls=%fused_computation.7 | loop fusion | flops 32768 | bytes 131073 | tf_op jit(solution)/shard_map/jit(_where)/select_n | solution.py:153
  6.4 0.0 copy-done
  6.4 0.7 %select_reduce_fusion = f32[128]{0:T(128)S(1)} fusion(f32[8]{0:T(128)S(1)} %dynamic-slice_bitcast_fusion, s32[128]{0:T(128)} %param.9), kind=kLoop, calls=%fused_computation.8 | loop fusion | flops 2944 | bytes 1056 | tf_op jit(solution)/shard_map/reduce_sum | solution.py:149
  7.1 0.0 collective-permute-done
  7.1 0.7 %pad_maximum_fusion = bf16[2,2,64,128]{3,2,1,0:T(8,128)(2,1)S(1)} fusion(bf16[1,2,64,128]{3,2,1,0:T(8,128)(2,1)S(1)} %get-tuple-element.18, bf16[1,1,64,128]{3,2,1,0:T(8,128)(2,1)S(1)} %bitcast.22, bf16[1,1,64,128]{3,2,1,0:T(8,128)(2,1)} %bitcast.20), kind=kLoop, calls=%fused_computation.1 | loop fusion | flops 65536 | bytes 131072 | tf_op jit(solution)/shard_map/stack | solution.py:156
  7.9 1.6 %collective-permute-start.1 = (bf16[2,2,64,128]{3,2,1,0:T(8,128)(2,1)S(1)}, bf16[2,2,64,128]{3,2,1,0:T(8,128)(2,1)S(1)}, u32[]{:S(2)}, u32[]{:S(2)}) collective-permute-start(bf16[2,2,64,128]{3,2,1,0:T(8,128)(2,1)S(1)} %pad_maximum_fusion), channel_id=1, source_target_pairs={{0,4},{1,5},{2,6},{3,7},{4,0},{5,1},{6,2},{7,3},{8,12},{9,13},{10,... | collective-permute-start | bytes 196616 | tf_op jit(solution)/shard_map/ppermute | solution.py:20
  9.4 2.7 %collective-permute-done.1.facing = bf16[2,2,64,128]{3,2,1,0:T(8,128)(2,1)S(1)} collective-permute-done((bf16[2,2,64,128]{3,2,1,0:T(8,128)(2,1)S(1)}, bf16[2,2,64,128]{3,2,1,0:T(8,128)(2,1)S(1)}, u32[]{:S(2)}, u32[]{:S(2)}) %collective-permute-start.1) | collective-permute-done | bytes 65568 | tf_op jit(solution)/shard_map/ppermute | solution.py:20
  12.1 0.0 copy-start.2
  12.1 0.7 %multiply_convert_fusion.vector = bf16[4,2,32,128]{3,2,1,0:T(8,128)(2,1)S(1)} fusion(bf16[2,2,32,128]{3,2,1,0:T(8,128)(2,1)S(1)} %bitcast.18, bf16[1,2,32,128]{3,2,1,0:T(8,128)(2,1)S(1)} %bitcast.23, bf16[1,2,32,128]{3,2,1,0:T(8,128)(2,1)} %bitcast.21, f32[128]{0:T(128)S(1)} %get-tuple-element.19), kind=kLoop, calls=%fused_computation | loop fusion | flops 163840 | bytes 131584 | tf_op jit(solution)/shard_map/convert_element_type | solution.py:160
  12.9 0.8 %collective-permute-start.3 = (bf16[4,2,32,128]{3,2,1,0:T(8,128)(2,1)S(1)}, bf16[4,2,32,128]{3,2,1,0:T(8,128)(2,1)S(1)}, u32[]{:S(2)}, u32[]{:S(2)}) collective-permute-start(bf16[4,2,32,128]{3,2,1,0:T(8,128)(2,1)S(1)} %multiply_convert_fusion.vector), channel_id=1, source_target_pairs={{0,16},{16,0},{1,17},{17,1},{2,18},{18,2},{3,19},{19,3},{4,20},{20... | collective-permute-start | bytes 196616 | tf_op jit(solution)/shard_map/ppermute | solution.py:25
  13.7 0.0 copy-start.3
  13.7 0.8 %collective-permute-start.2 = (bf16[2,64,128]{2,1,0:T(8,128)(2,1)S(1)}, bf16[2,64,128]{2,1,0:T(8,128)(2,1)S(1)}, u32[]{:S(2)}, u32[]{:S(2)}) collective-permute-start(bf16[2,64,128]{2,1,0:T(8,128)(2,1)S(1)} %get-tuple-element.17), channel_id=1, source_target_pairs={{4,8},{5,9},{6,10},{7,11},{8,4},{9,5},{10,6},{11,7},{20,24},{21,25... | collective-permute-start | bytes 98312 | tf_op jit(solution)/shard_map/ppermute | solution.py:30
  14.5 0.0 copy-done.1
  14.5 0.0 copy-done.2
  14.5 0.0 copy-done.3
  14.5 1.0 %own.1 = (bf16[1024,256]{1,0:T(8,128)(2,1)S(1)}, f32[256,1024]{1,0:T(8,128)S(1)}, f32[10,128]{1,0:T(8,128)S(1)}, bf16[512,256]{1,0:T(8,128)(2,1)S(1)}) custom-call(f32[16]{0:T(128)S(1)} %copy-done.3, s32[32,128]{1,0:T(8,128)S(1)} %bitcast.17, bf16[4,2,32,128]{3,2,1,0:T(8,128)(2,1)S(1)} %multiply_convert_fusion.vector, bf16[2,1024,128]{2,1,0:T(8,128)(2,1)S(1)} %copy-done.1), custom_call_target="tpu_custom_call" | custom-call | tf_op jit(solution)/shard_map/own/pallas_call | solution.py:166
  15.5 0.0 collective-permute-done.2.other
  15.6 3.5 %collective-permute-done.3.refs_0_ = bf16[4,2,32,128]{3,2,1,0:T(8,128)(2,1)S(1)} collective-permute-done((bf16[4,2,32,128]{3,2,1,0:T(8,128)(2,1)S(1)}, bf16[4,2,32,128]{3,2,1,0:T(8,128)(2,1)S(1)}, u32[]{:S(2)}, u32[]{:S(2)}) %collective-permute-start.3) | collective-permute-done | bytes 65568 | tf_op jit(solution)/shard_map/ppermute | solution.py:25
  19.0 0.0 collective-permute-done.4.refs_1_
  19.0 1.4 %slip.1 = (f32[2,64,128]{2,1,0:T(8,128)S(1)}, bf16[2,64,128]{2,1,0:T(8,128)(2,1)S(1)}) custom-call(f32[1,128]{1,0:T(1,128)S(1)} %get-tuple-element.20.weight, f32[10,128]{1,0:T(8,128)S(1)} %get-tuple-element.11.inverse, bf16[512,256]{1,0:T(8,128)(2,1)S(1)} %get-tuple-element.12.hood, f32[256,1024]{1,0:T(8,128)S(1)} %get-tuple-element.13.source, ...), custom_call_target="tpu_custom_call" | custom-call | tf_op jit(solution)/shard_map/slip/pallas_call | solution.py:179
  20.5 2.2 %collective-permute-start.5 = (bf16[2,64,128]{2,1,0:T(8,128)(2,1)S(1)}, bf16[2,64,128]{2,1,0:T(8,128)(2,1)S(1)}, u32[]{:S(2)}, u32[]{:S(2)}) collective-permute-start(bf16[2,64,128]{2,1,0:T(8,128)(2,1)S(1)} %get-tuple-element.16), channel_id=1, source_target_pairs={{0,4},{1,5},{2,6},{3,7},{4,0},{5,1},{6,2},{7,3},{8,12},{9,13},{10,... | collective-permute-start | bytes 98312 | tf_op jit(solution)/shard_map/ppermute | solution.py:20
  22.7 1.9 %collective-permute-done.5 = bf16[2,64,128]{2,1,0:T(8,128)(2,1)S(1)} collective-permute-done((bf16[2,64,128]{2,1,0:T(8,128)(2,1)S(1)}, bf16[2,64,128]{2,1,0:T(8,128)(2,1)S(1)}, u32[]{:S(2)}, u32[]{:S(2)}) %collective-permute-start.5) | collective-permute-done | bytes 32800 | tf_op jit(solution)/shard_map/ppermute | solution.py:20
  24.6 3.2 %collective-permute-start.6 = (bf16[2,32,128]{2,1,0:T(8,128)(2,1)S(1)}, bf16[2,32,128]{2,1,0:T(8,128)(2,1)S(1)}, u32[]{:S(2)}, u32[]{:S(2)}) collective-permute-start(bf16[2,32,128]{2,1,0:T(8,128)(2,1)S(1)} %slice.32), channel_id=1, source_target_pairs={{0,8},{1,9},{2,10},{3,11},{4,12},{5,13},{6,14},{7,15},{8,0},{9,1},... | collective-permute-start | bytes 49160 | tf_op jit(solution)/shard_map/ppermute | solution.py:20
  27.7 1.7 %collective-permute-done.6 = bf16[2,32,128]{2,1,0:T(8,128)(2,1)S(1)} collective-permute-done((bf16[2,32,128]{2,1,0:T(8,128)(2,1)S(1)}, bf16[2,32,128]{2,1,0:T(8,128)(2,1)S(1)}, u32[]{:S(2)}, u32[]{:S(2)}) %collective-permute-start.6) | collective-permute-done | bytes 16416 | tf_op jit(solution)/shard_map/ppermute | solution.py:20
  29.5 0.6 %fusion = f32[2,128,32]{1,2,0:T(8,128)} fusion(f32[2,64,128]{2,1,0:T(8,128)S(1)} %convert_add_fusion, bf16[2,32,128]{2,1,0:T(8,128)(2,1)S(1)} %collective-permute-done.6), kind=kLoop, calls=%fused_computation.5 | loop fusion | flops 16384 | bytes 81920 | tf_op jit(solution)/shard_map/transpose | solution.py:192
  (5 shorter events, 0.0 us)
Async XLA Ops:
  0.0 6.4 %copy-start = (f32[4,8]{1,0:T(4,128)S(1)}, f32[4,8]{1,0:T(4,128)}, u32[]{:S(2)}) copy-start(f32[4,8]{1,0:T(4,128)} %param.8) | copy-start | bytes 388
  0.0 14.5 %copy-start.1 = (bf16[2,1024,128]{2,1,0:T(8,128)(2,1)S(1)}, bf16[2,1024,128]{2,1,0:T(8,128)(2,1)}, u32[]{:S(2)}) copy-start(bf16[2,1024,128]{2,1,0:T(8,128)(2,1)} %green.1) | copy-start | bytes 1572868
  0.0 7.1 %collective-permute-start = (bf16[2,32,128]{2,1,0:T(8,128)(2,1)}, bf16[2,32,128]{2,1,0:T(8,128)(2,1)S(1)}, u32[]{:S(2)}, u32[]{:S(2)}) collective-permute-start(bf16[2,32,128]{2,1,0:T(8,128)(2,1)} %bitcast.19), channel_id=1, source_target_pairs={{0,8},{1,9},{2,10},{3,11},{4,12},{5,13},{6,14},{7,15},{8,0},{9,1},... | collective-permute-start | bytes 49160 | tf_op jit(solution)/shard_map/ppermute | solution.py:20
  4.0 15.0 %collective-permute-start.4 = (bf16[2,1024,128]{2,1,0:T(8,128)(2,1)}, bf16[2,1024,128]{2,1,0:T(8,128)(2,1)S(1)}, u32[]{:S(2)}, u32[]{:S(2)}) collective-permute-start(bf16[2,1024,128]{2,1,0:T(8,128)(2,1)} %green.1), channel_id=1, source_target_pairs={{0,16},{16,0},{1,17},{17,1},{2,18},{18,2},{3,19},{19,3},{4,20},{20... | collective-permute-start | bytes 1572872 | tf_op jit(solution)/shard_map/ppermute | solution.py:25
  7.9 4.3 %collective-permute-start.1 = (bf16[2,2,64,128]{3,2,1,0:T(8,128)(2,1)S(1)}, bf16[2,2,64,128]{3,2,1,0:T(8,128)(2,1)S(1)}, u32[]{:S(2)}, u32[]{:S(2)}) collective-permute-start(bf16[2,2,64,128]{3,2,1,0:T(8,128)(2,1)S(1)} %pad_maximum_fusion), channel_id=1, source_target_pairs={{0,4},{1,5},{2,6},{3,7},{4,0},{5,1},{6,2},{7,3},{8,12},{9,13},{10,... | collective-permute-start | bytes 196616 | tf_op jit(solution)/shard_map/ppermute | solution.py:20
  12.1 2.4 %copy-start.2 = (s32[4096]{0:T(1024)S(1)}, s32[4096]{0:T(1024)}, u32[]{:S(2)}) copy-start(s32[4096]{0:T(1024)} %param.11) | copy-start | bytes 49156
  12.9 6.2 %collective-permute-start.3 = (bf16[4,2,32,128]{3,2,1,0:T(8,128)(2,1)S(1)}, bf16[4,2,32,128]{3,2,1,0:T(8,128)(2,1)S(1)}, u32[]{:S(2)}, u32[]{:S(2)}) collective-permute-start(bf16[4,2,32,128]{3,2,1,0:T(8,128)(2,1)S(1)} %multiply_convert_fusion.vector), channel_id=1, source_target_pairs={{0,16},{16,0},{1,17},{17,1},{2,18},{18,2},{3,19},{19,3},{4,20},{20... | collective-permute-start | bytes 196616 | tf_op jit(solution)/shard_map/ppermute | solution.py:25
  13.7 0.8 %copy-start.3 = (f32[16]{0:T(128)S(1)}, f32[16]{0:T(128)}, u32[]{:S(2)}) copy-start(f32[16]{0:T(128)} %kappa.1) | copy-start | bytes 196
  13.7 1.9 %collective-permute-start.2 = (bf16[2,64,128]{2,1,0:T(8,128)(2,1)S(1)}, bf16[2,64,128]{2,1,0:T(8,128)(2,1)S(1)}, u32[]{:S(2)}, u32[]{:S(2)}) collective-permute-start(bf16[2,64,128]{2,1,0:T(8,128)(2,1)S(1)} %get-tuple-element.17), channel_id=1, source_target_pairs={{4,8},{5,9},{6,10},{7,11},{8,4},{9,5},{10,6},{11,7},{20,24},{21,25... | collective-permute-start | bytes 98312 | tf_op jit(solution)/shard_map/ppermute | solution.py:30
  20.5 4.1 %collective-permute-start.5 = (bf16[2,64,128]{2,1,0:T(8,128)(2,1)S(1)}, bf16[2,64,128]{2,1,0:T(8,128)(2,1)S(1)}, u32[]{:S(2)}, u32[]{:S(2)}) collective-permute-start(bf16[2,64,128]{2,1,0:T(8,128)(2,1)S(1)} %get-tuple-element.16), channel_id=1, source_target_pairs={{0,4},{1,5},{2,6},{3,7},{4,0},{5,1},{6,2},{7,3},{8,12},{9,13},{10,... | collective-permute-start | bytes 98312 | tf_op jit(solution)/shard_map/ppermute | solution.py:20
  24.6 4.9 %collective-permute-start.6 = (bf16[2,32,128]{2,1,0:T(8,128)(2,1)S(1)}, bf16[2,32,128]{2,1,0:T(8,128)(2,1)S(1)}, u32[]{:S(2)}, u32[]{:S(2)}) collective-permute-start(bf16[2,32,128]{2,1,0:T(8,128)(2,1)S(1)} %slice.32), channel_id=1, source_target_pairs={{0,8},{1,9},{2,10},{3,11},{4,12},{5,13},{6,14},{7,15},{8,0},{9,1},... | collective-permute-start | bytes 49160 | tf_op jit(solution)/shard_map/ppermute | solution.py:20

commit v3 on v2

--- a/solution.py
+++ b/solution.py
@@ -13,6 +13,8 @@
 REACH = 2 * DIP
 F32 = jnp.float32
 BF16 = jnp.bfloat16
+PRIOR = pl.CostEstimate(flops=1, bytes_accessed=1, transcendentals=0)
+BESIDE = pl.CostEstimate(flops=575_000_000, bytes_accessed=1, transcendentals=0)
 PARAMS = pltpu.CompilerParams(vmem_limit_bytes=32 * 2**20)
 
 
@@ -62,7 +64,21 @@
     return jnp.concatenate([top, jnp.concatenate([zi, -zr], axis=1)], axis=0)
 
 
-def own_kernel(nfreq, nclass, kappa, coeff, vector, green, operator, source, inverse, hood):
+def prep_kernel(nfreq, noise, station, vector, green, weight, held, facing, other):
+    par = lax.axis_index("par")
+    freq, part = lax.rem(par, nfreq), lax.div(par, nfreq)
+    odd = lax.rem(part, 2)
+    cells = green.shape[1]
+    first = pl.multiple_of(odd * (cells - REACH), REACH)
+    last = pl.multiple_of((1 - odd) * (cells - REACH), REACH)
+    held[...] = vector[...]
+    facing[...] = green[:, pl.ds(last, REACH)]
+    other[...] = green[:, pl.ds(first, REACH)]
+    variance = chosen(noise, station[...], noise.shape[1], lambda t, k: t[freq, k])
+    weight[...] = 1.0 / jnp.sqrt(variance)
+
+
+def own_kernel(nfreq, nclass, kappa, coeff, vector, green, facing, other, operator, rims, source, inverse, hood):
     part = lax.div(lax.axis_index("par"), nfreq)
     cells = green.shape[1]
     blocks = cells // LANES
@@ -77,15 +93,17 @@
     inverse[blocks : blocks + 1, :] = jnp.where(part < parts - 1, after, 0.0)
     inverse[blocks + 1 : blocks + 2, :] = jnp.where(part > 0, before, 0.0)
     hood[...] = stencil()
+    odd = lax.rem(part, 2) == 1
+    near, far = planes(facing.at[1], 0, REACH), planes(other, 0, REACH)
+    rims[0], rims[1] = jnp.where(odd, far, near), jnp.where(odd, near, far)
     both = planes(green, 0, cells)
     operator[...] = both
     source[...] = dot(lhs(vector[...]), both, ((1,), (1,)))
 
 
-def slip_kernel(nfreq, nsens, weight, inverse, hood, source, operator, facing, other, *refs):
+def slip_kernel(nsens, weight, inverse, hood, source, operator, rims, *refs):
     vectors, refs = refs[: nsens - 1], refs[nsens - 1 :]
     greens, (keep, send) = refs[: nsens - 1], refs[nsens - 1 :]
-    part = lax.div(lax.axis_index("par"), nfreq)
     cells = operator.shape[0]
     blocks = cells // LANES
     rows = source.shape[0] // 2
@@ -119,12 +137,9 @@
     first = [zero] + [(src[b] * inv[b + 1]).astype(BF16) for b in range(blocks)] + [zero]
     slip = solved(sums(solved(sums(first))))
     data = dot(jnp.concatenate(slip[1:-1], axis=1), operator[...])
-    odd = lax.rem(part, 2) == 1
-    near, far = planes(facing.at[1], 0, REACH), planes(other, 0, REACH)
-    low, high = jnp.where(odd, near, far), jnp.where(odd, far, near)
     pad = jnp.zeros((LANES - REACH, wide), BF16)
-    data = data + dot(slip[0], jnp.concatenate([pad, low], axis=0))
-    data = data + dot(slip[-1], jnp.concatenate([high, pad], axis=0))
+    data = data + dot(slip[0], jnp.concatenate([pad, rims[1]], axis=0))
+    data = data + dot(slip[-1], jnp.concatenate([rims[0], pad], axis=0))
     real = weight[...] * (data[:rows, :LANES] - data[rows:, LANES:])
     imag = weight[...] * (data[rows:, :LANES] + data[:rows, LANES:])
     half = rows // 2
@@ -133,60 +148,66 @@
 
 
 def shards(probes, green_blocks, noise_table, station_class, kappa_table, coeff_index):
-    nfreq, ngroup = noise_table.shape
+    nfreq = noise_table.shape[0]
     nsens = lax.axis_size("sens")
     sensors, rows_dev = probes.shape[1:]
     cells = green_blocks.shape[1]
-    par = lax.axis_index("par")
-    odd = par // nfreq % 2 == 1
+    smem = pl.BlockSpec(memory_space=pltpu.SMEM)
+    vmem = pl.BlockSpec(memory_space=pltpu.VMEM)
+    greens = [turned(green_blocks, "sens", k) for k in range(1, nsens)]
     vector = jnp.transpose(probes, (0, 2, 1))
-
-    greens = [turned(green_blocks, "sens", k) for k in range(1, nsens)]
     partner = swapped(vector, "par", 2 * nfreq)
 
-    variances = lax.dynamic_index_in_dim(noise_table, par % nfreq, 0)
-    member = station_class[None, :] == jnp.arange(ngroup, dtype=jnp.int32)[:, None]
-    variance = jnp.sum(jnp.where(member, variances.reshape(ngroup, 1), 0.0), axis=0, keepdims=True)
-    weight = 1.0 / jnp.sqrt(variance)
-
-    first, last = green_blocks[:, :REACH], green_blocks[:, -REACH:]
-    facing, other = jnp.where(odd, first, last), jnp.where(odd, last, first)
-
-    mine = jnp.stack([vector, partner])
+    rim = jax.ShapeDtypeStruct((2, REACH, sensors), BF16)
+    weight, held, facing, other = pl.pallas_call(
+        functools.partial(prep_kernel, nfreq),
+        out_shape=[
+            jax.ShapeDtypeStruct((1, sensors), F32),
+            jax.ShapeDtypeStruct((2, rows_dev, sensors), BF16),
+            rim,
+            rim,
+        ],
+        in_specs=[smem] + [vmem] * 3,
+        out_specs=[vmem] * 4,
+        compiler_params=PARAMS,
+        cost_estimate=PRIOR,
+        name="prep",
+    )(noise_table, station_class.reshape(1, -1), vector, green_blocks)
+
+    mine = jnp.stack([held, partner])
     sent = jnp.stack([mine.reshape(2, -1, sensors), facing])
     got = swapped(sent, "par", nfreq)
     other = crossed(other, "par", nfreq)
-    raw = jnp.concatenate([mine, got[0].reshape(mine.shape)], axis=0)
-    vectors = (weight[None, None] * raw.astype(F32)).astype(BF16)
+    vectors = jnp.concatenate([mine, got[0].reshape(mine.shape)], axis=0)
+    vectors = (weight * vectors.astype(F32)).astype(BF16)
     rest = [turned(vectors, "sens", k) for k in range(1, nsens)]
-
-    smem = pl.BlockSpec(memory_space=pltpu.SMEM)
-    vmem = pl.BlockSpec(memory_space=pltpu.VMEM)
     rows = SPLIT * rows_dev
-    operator, source, inverse, hood = pl.pallas_call(
+    operator, rims, source, inverse, hood = pl.pallas_call(
         functools.partial(own_kernel, nfreq, kappa_table.shape[0]),
         out_shape=[
             jax.ShapeDtypeStruct((cells, 2 * sensors), BF16),
+            jax.ShapeDtypeStruct((2, REACH, 2 * sensors), BF16),
             jax.ShapeDtypeStruct((2 * rows, cells), F32),
             jax.ShapeDtypeStruct((cells // LANES + 2, LANES), F32),
             jax.ShapeDtypeStruct((4 * LANES, 2 * LANES), BF16),
         ],
-        in_specs=[smem] + [vmem] * 3,
-        out_specs=[vmem] * 4,
+        in_specs=[smem] + [vmem] * 5,
+        out_specs=[vmem] * 5,
         compiler_params=PARAMS,
+        cost_estimate=BESIDE,
         name="own",
-    )(kappa_table, coeff_index.reshape(-1, LANES), vectors, green_blocks)
+    )(kappa_table, coeff_index.reshape(-1, LANES), vectors, green_blocks, got, other)
     keep, send = pl.pallas_call(
-        functools.partial(slip_kernel, nfreq, nsens),
+        functools.partial(slip_kernel, nsens),
         out_shape=[
             jax.ShapeDtypeStruct((2, rows // 2, sensors), F32),
             jax.ShapeDtypeStruct((2, rows // 2, sensors), BF16),
         ],
-        in_specs=[vmem] * (5 + 2 * nsens),
+        in_specs=[vmem] * (4 + 2 * nsens),
         out_specs=[vmem] * 2,
         compiler_params=PARAMS,
         name="slip",
-    )(weight, inverse, hood, source, operator, got, other, *rest, *greens)
+    )(weight, inverse, hood, source, operator, rims, *rest, *greens)
     near = keep + swapped(send, "par", nfreq).astype(F32)
     far = swapped(near[:, rows_dev:].astype(BF16), "par", 2 * nfreq)
     return jnp.transpose(near[:, :rows_dev] + far.astype(F32), (0, 2, 1))

time: 30.4 us -> 28.1 us (0.924)
  other arithmetic: 3.64 us -> 0.66 us
  local copies, waits for them, and re-layouts: 0.03 us -> 1.89 us
  waiting for transfers between devices: 9.79 us -> 8.84 us
  starting transfers between devices: 14 us -> 13.2 us
  Pallas kernels: 2.47 us -> 3.04 us
    ppermute x4, starting transfers between devices: 10.9 us -> 9.04 us  [swapped(): lax.ppermute(value, axis, [(i, i ^ mask) for i in range(lax.axis_size(axi...]
    unnamed x8 -> x14, local copies, waits for them, and re-layouts: 0.02 us -> 1.88 us
    ppermute x2, starting transfers between devices: 2.32 us -> 3.54 us  [turned(): lax.ppermute(value, axis, [(i, (i + step) % size) for i in range(size)])]
    ppermute x2, waiting for transfers between devices: 3.48 us -> 2.61 us  [turned(): lax.ppermute(value, axis, [(i, (i + step) % size) for i in range(size)])]
    select_n x1 -> x0, other arithmetic: 0.8 us -> none  [shards(): facing, other = (jnp.where(odd, first, last), jnp.where(odd, last, first))]
    reduce_sum x1 -> x0, other arithmetic: 0.74 us -> none  [shards(): jnp.sum(jnp.where(member, variances.reshape(ngroup, 1), 0.0), axis=0, kee...]
    convert_element_type x1, other arithmetic: 0.75 us -> 0.02 us  [shards(): vectors = (weight * vectors.astype(F32)).astype(BF16)]
    another operation x1, other arithmetic: 0.73 us -> 0.01 us  [shards(): sent = jnp.stack([mine.reshape(2, -1, sensors), facing])]
  transfers between devices with their start and end apart: 7 -> 7, of which waited for: 4 -> 4; matrix products, arithmetic and copies ran while one was open for 10% -> 0% of each run, Pallas kernels for 3% -> 6%
where the time goes in v3:
time: 28.1 us; the launch traced here: 27.7 us
  starting transfers between devices  13.2 us (47%)
  waiting for transfers between devices  8.84 us (31%)
  Pallas kernels  3.04 us (11%)
  local copies, waits for them, and re-layouts  1.89 us (7%)
  other arithmetic  0.66 us (2%)
    ppermute x4, starting transfers between devices, swapped(): lax.ppermute(value, axis, [(i, i ^ mask) for i in range(lax.axis_size(axi...  9.04 us
    ppermute x4, waiting for transfers between devices, swapped(): lax.ppermute(value, axis, [(i, i ^ mask) for i in range(lax.axis_size(axi...  6.23 us
    ppermute x2, starting transfers between devices, turned(): lax.ppermute(value, axis, [(i, (i + step) % size) for i in range(size)])  3.54 us
    ppermute x2, waiting for transfers between devices, turned(): lax.ppermute(value, axis, [(i, (i + step) % size) for i in range(size)])  2.61 us
    unnamed x14, local copies, waits for them, and re-layouts  1.88 us
    pallas_call x1, Pallas kernels, shards(): pl.pallas_call(functools.partial(slip_kernel, nsens), out_shape=[jax.Shap...  1.42 us
    pallas_call x1, Pallas kernels, shards(): pl.pallas_call(functools.partial(own_kernel, nfreq, kappa_table.shape[0])...  1.03 us
    ppermute x1, starting transfers between devices, crossed(): return lax.ppermute(value, axis, pairs + [(b, a) for a, b in pairs])  0.65 us
  transfers between devices with their start and end apart: 7, of which 4 were waited for; matrix products, arithmetic and copies ran while one was open for 0% of the time, Pallas kernels for 6%

profile of v3, /device:TPU:0, one launch (start us, length us, event | category | flops | bytes accessed | tf_op | source)
XLA Modules:
  0.0 27.7 jit_solution(15127095093574498894)
XLA Ops:
  0.0 0.0 copy-start.3
  0.0 3.0 %collective-permute-start.4 = (bf16[2,1024,128]{2,1,0:T(8,128)(2,1)}, bf16[2,1024,128]{2,1,0:T(8,128)(2,1)S(1)}, u32[]{:S(2)}, u32[]{:S(2)}) collective-permute-start(bf16[2,1024,128]{2,1,0:T(8,128)(2,1)} %green.3), channel_id=1, source_target_pairs={{0,16},{16,0},{1,17},{17,1},{2,18},{18,2},{3,19},{19,3},{4,20},{20... | collective-permute-start | bytes 1572872 | tf_op jit(solution)/shard_map/ppermute | solution.py:27
  3.0 0.0 copy-start.4
  3.0 2.6 %collective-permute-start = (bf16[2,32,128]{2,1,0:T(8,128)(2,1)}, bf16[2,32,128]{2,1,0:T(8,128)(2,1)S(1)}, u32[]{:S(2)}, u32[]{:S(2)}) collective-permute-start(bf16[2,32,128]{2,1,0:T(8,128)(2,1)} %bitcast.15), channel_id=1, source_target_pairs={{0,8},{1,9},{2,10},{3,11},{4,12},{5,13},{6,14},{7,15},{8,0},{9,1},... | collective-permute-start | bytes 49160 | tf_op jit(solution)/shard_map/ppermute | solution.py:22
  5.6 0.0 copy-done.3
  5.6 0.0 copy-done.4
  5.6 0.0 copy-start
  5.6 1.0 %copy-done = bf16[2,1024,128]{2,1,0:T(8,128)(2,1)S(1)} copy-done((bf16[2,1024,128]{2,1,0:T(8,128)(2,1)S(1)}, bf16[2,1024,128]{2,1,0:T(8,128)(2,1)}, u32[]{:S(2)}) %copy-start) | copy-done | bytes 524312
  6.6 0.0 copy-start.2
  6.6 0.7 %copy-done.2 = bf16[2,128,32]{1,2,0:T(8,128)(2,1)S(1)} copy-done((bf16[2,128,32]{1,2,0:T(8,128)(2,1)S(1)}, bf16[2,128,32]{1,2,0:T(8,128)(2,1)}, u32[]{:S(2)}) %copy-start.2) | copy-done | bytes 16408
  7.3 0.0 copy-start.1
  7.3 0.6 %prep.1 = (f32[1,128]{1,0:T(1,128)S(1)}, bf16[2,32,128]{2,1,0:T(8,128)(2,1)S(1)}, bf16[2,64,128]{2,1,0:T(8,128)(2,1)S(1)}, bf16[2,64,128]{2,1,0:T(8,128)(2,1)S(1)}) custom-call(f32[4,8]{1,0:T(4,128)S(1)} %copy-done.3, s32[1,128]{1,0:T(1,128)S(1)} %bitcast.18, bf16[2,32,128]{2,1,0:T(8,128)(2,1)S(1)} %bitcast.16, bf16[2,1024,128]{2,1,0:T(8,128)(2,1)S(1)} %copy-done), custom_call_target="tpu_custom_call" | custom-call | flops 1 | bytes 1 | tf_op jit(solution)/shard_map/prep/pallas_call | solution.py:162
  7.9 0.0 collective-permute-done
  8.0 1.6 %collective-permute-start.1 = (bf16[2,2,64,128]{3,2,1,0:T(8,128)(2,1)S(1)}, bf16[2,2,64,128]{3,2,1,0:T(8,128)(2,1)S(1)}, u32[]{:S(2)}, u32[]{:S(2)}) collective-permute-start(bf16[2,2,64,128]{3,2,1,0:T(8,128)(2,1)S(1)} %pad_maximum_fusion), channel_id=1, source_target_pairs={{0,4},{1,5},{2,6},{3,7},{4,0},{5,1},{6,2},{7,3},{8,12},{9,13},{10,... | collective-permute-start | bytes 196616 | tf_op jit(solution)/shard_map/ppermute | solution.py:22
  9.6 0.7 %collective-permute-start.2 = (bf16[2,64,128]{2,1,0:T(8,128)(2,1)S(1)}, bf16[2,64,128]{2,1,0:T(8,128)(2,1)S(1)}, u32[]{:S(2)}, u32[]{:S(2)}) collective-permute-start(bf16[2,64,128]{2,1,0:T(8,128)(2,1)S(1)} %get-tuple-element.19), channel_id=1, source_target_pairs={{4,8},{5,9},{6,10},{7,11},{8,4},{9,5},{10,6},{11,7},{20,24},{21,25... | collective-permute-start | bytes 98312 | tf_op jit(solution)/shard_map/ppermute | solution.py:32
  10.3 2.0 %collective-permute-done.1.facing = bf16[2,2,64,128]{3,2,1,0:T(8,128)(2,1)S(1)} collective-permute-done((bf16[2,2,64,128]{3,2,1,0:T(8,128)(2,1)S(1)}, bf16[2,2,64,128]{3,2,1,0:T(8,128)(2,1)S(1)}, u32[]{:S(2)}, u32[]{:S(2)}) %collective-permute-start.1) | collective-permute-done | bytes 65568 | tf_op jit(solution)/shard_map/ppermute | solution.py:22
  12.3 0.0 copy-start.5
  12.3 0.0 copy-start.6
  12.3 0.6 %collective-permute-start.3 = (bf16[4,2,32,128]{3,2,1,0:T(8,128)(2,1)S(1)}, bf16[4,2,32,128]{3,2,1,0:T(8,128)(2,1)S(1)}, u32[]{:S(2)}, u32[]{:S(2)}) collective-permute-start(bf16[4,2,32,128]{3,2,1,0:T(8,128)(2,1)S(1)} %multiply_convert_fusion.vector), channel_id=1, source_target_pairs={{0,16},{16,0},{1,17},{17,1},{2,18},{18,2},{3,19},{19,3},{4,20},{20... | collective-permute-start | bytes 196616 | tf_op jit(solution)/shard_map/ppermute | solution.py:27
  12.9 0.0 collective-permute-done.2.other
  12.9 0.0 copy-done.1
  12.9 0.1 copy-done.5
  13.0 0.0 copy-done.6
  13.0 1.0 %own.1 = (bf16[1024,256]{1,0:T(8,128)(2,1)S(1)}, bf16[2,64,256]{2,1,0:T(8,128)(2,1)S(1)}, f32[256,1024]{1,0:T(8,128)S(1)}, f32[10,128]{1,0:T(8,128)S(1)}, bf16[512,256]{1,0:T(8,128)(2,1)S(1)}) custom-call(f32[16]{0:T(128)S(1)} %copy-done.6, s32[32,128]{1,0:T(8,128)S(1)} %bitcast.19, bf16[4,2,32,128]{3,2,1,0:T(8,128)(2,1)S(1)} %multiply_convert_fusion.vector, ...), custom_call_target="tpu_custom_call" | custom-call | flops 575000000 | bytes 1 | tf_op jit(solution)/shard_map/own/pallas_call | solution.py:185
  14.1 2.6 %collective-permute-done.3.refs_0_ = bf16[4,2,32,128]{3,2,1,0:T(8,128)(2,1)S(1)} collective-permute-done((bf16[4,2,32,128]{3,2,1,0:T(8,128)(2,1)S(1)}, bf16[4,2,32,128]{3,2,1,0:T(8,128)(2,1)S(1)}, u32[]{:S(2)}, u32[]{:S(2)}) %collective-permute-start.3) | collective-permute-done | bytes 65568 | tf_op jit(solution)/shard_map/ppermute | solution.py:27
  16.7 0.0 collective-permute-done.4.refs_1_
  16.7 1.4 %slip.1 = (f32[2,64,128]{2,1,0:T(8,128)S(1)}, bf16[2,64,128]{2,1,0:T(8,128)(2,1)S(1)}) custom-call(f32[1,128]{1,0:T(1,128)S(1)} %get-tuple-element.16.weight, f32[10,128]{1,0:T(8,128)S(1)} %get-tuple-element.20.inverse, bf16[512,256]{1,0:T(8,128)(2,1)S(1)} %get-tuple-element.21.hood, f32[256,1024]{1,0:T(8,128)S(1)} %get-tuple-element.22.source, ...), custom_call_target="tpu_custom_call" | custom-call | tf_op jit(solution)/shard_map/slip/pallas_call | solution.py:200
  18.1 2.4 %collective-permute-start.5 = (bf16[2,64,128]{2,1,0:T(8,128)(2,1)S(1)}, bf16[2,64,128]{2,1,0:T(8,128)(2,1)S(1)}, u32[]{:S(2)}, u32[]{:S(2)}) collective-permute-start(bf16[2,64,128]{2,1,0:T(8,128)(2,1)S(1)} %get-tuple-element.26), channel_id=1, source_target_pairs={{0,4},{1,5},{2,6},{3,7},{4,0},{5,1},{6,2},{7,3},{8,12},{9,13},{10,... | collective-permute-start | bytes 98312 | tf_op jit(solution)/shard_map/ppermute | solution.py:22
  20.5 1.9 %collective-permute-done.5 = bf16[2,64,128]{2,1,0:T(8,128)(2,1)S(1)} collective-permute-done((bf16[2,64,128]{2,1,0:T(8,128)(2,1)S(1)}, bf16[2,64,128]{2,1,0:T(8,128)(2,1)S(1)}, u32[]{:S(2)}, u32[]{:S(2)}) %collective-permute-start.5) | collective-permute-done | bytes 32800 | tf_op jit(solution)/shard_map/ppermute | solution.py:22
  22.4 2.4 %collective-permute-start.6 = (bf16[2,32,128]{2,1,0:T(8,128)(2,1)S(1)}, bf16[2,32,128]{2,1,0:T(8,128)(2,1)S(1)}, u32[]{:S(2)}, u32[]{:S(2)}) collective-permute-start(bf16[2,32,128]{2,1,0:T(8,128)(2,1)S(1)} %slice.20), channel_id=1, source_target_pairs={{0,8},{1,9},{2,10},{3,11},{4,12},{5,13},{6,14},{7,15},{8,0},{9,1},... | collective-permute-start | bytes 49160 | tf_op jit(solution)/shard_map/ppermute | solution.py:22
  24.8 2.3 %collective-permute-done.6 = bf16[2,32,128]{2,1,0:T(8,128)(2,1)S(1)} collective-permute-done((bf16[2,32,128]{2,1,0:T(8,128)(2,1)S(1)}, bf16[2,32,128]{2,1,0:T(8,128)(2,1)S(1)}, u32[]{:S(2)}, u32[]{:S(2)}) %collective-permute-start.6) | collective-permute-done | bytes 16416 | tf_op jit(solution)/shard_map/ppermute | solution.py:22
  27.1 0.6 %fusion = f32[2,128,32]{1,2,0:T(8,128)} fusion(f32[2,64,128]{2,1,0:T(8,128)S(1)} %convert_add_fusion, bf16[2,32,128]{2,1,0:T(8,128)(2,1)S(1)} %collective-permute-done.6), kind=kLoop, calls=%fused_computation.5 | loop fusion | flops 16384 | bytes 81920 | tf_op jit(solution)/shard_map/transpose | solution.py:213
  (5 shorter events, 0.0 us)
Async XLA Ops:
  0.0 5.6 %copy-start.3 = (f32[4,8]{1,0:T(4,128)S(1)}, f32[4,8]{1,0:T(4,128)}, u32[]{:S(2)}) copy-start(f32[4,8]{1,0:T(4,128)} %noise.1) | copy-start | bytes 388
  0.0 16.7 %collective-permute-start.4 = (bf16[2,1024,128]{2,1,0:T(8,128)(2,1)}, bf16[2,1024,128]{2,1,0:T(8,128)(2,1)S(1)}, u32[]{:S(2)}, u32[]{:S(2)}) collective-permute-start(bf16[2,1024,128]{2,1,0:T(8,128)(2,1)} %green.3), channel_id=1, source_target_pairs={{0,16},{16,0},{1,17},{17,1},{2,18},{18,2},{3,19},{19,3},{4,20},{20... | collective-permute-start | bytes 1572872 | tf_op jit(solution)/shard_map/ppermute | solution.py:27
  3.0 2.6 %copy-start.4 = (s32[128]{0:T(128)S(1)}, s32[128]{0:T(128)}, u32[]{:S(2)}) copy-start(s32[128]{0:T(128)} %param.9) | copy-start | bytes 1540
  3.0 5.0 %collective-permute-start = (bf16[2,32,128]{2,1,0:T(8,128)(2,1)}, bf16[2,32,128]{2,1,0:T(8,128)(2,1)S(1)}, u32[]{:S(2)}, u32[]{:S(2)}) collective-permute-start(bf16[2,32,128]{2,1,0:T(8,128)(2,1)} %bitcast.15), channel_id=1, source_target_pairs={{0,8},{1,9},{2,10},{3,11},{4,12},{5,13},{6,14},{7,15},{8,0},{9,1},... | collective-permute-start | bytes 49160 | tf_op jit(solution)/shard_map/ppermute | solution.py:22
  5.6 1.0 %copy-start = (bf16[2,1024,128]{2,1,0:T(8,128)(2,1)S(1)}, bf16[2,1024,128]{2,1,0:T(8,128)(2,1)}, u32[]{:S(2)}) copy-start(bf16[2,1024,128]{2,1,0:T(8,128)(2,1)} %green.3) | copy-start | bytes 1572868
  6.6 0.7 %copy-start.2 = (bf16[2,128,32]{1,2,0:T(8,128)(2,1)S(1)}, bf16[2,128,32]{1,2,0:T(8,128)(2,1)}, u32[]{:S(2)}) copy-start(bf16[2,128,32]{1,2,0:T(8,128)(2,1)} %param.6) | copy-start | bytes 49156
  7.3 5.6 %copy-start.1 = (bf16[2,1024,128]{2,1,0:T(8,128)(2,1)S(1)}, bf16[2,1024,128]{2,1,0:T(8,128)(2,1)}, u32[]{:S(2)}) copy-start(bf16[2,1024,128]{2,1,0:T(8,128)(2,1)} %green.3) | copy-start | bytes 1572868
  8.0 4.3 %collective-permute-start.1 = (bf16[2,2,64,128]{3,2,1,0:T(8,128)(2,1)S(1)}, bf16[2,2,64,128]{3,2,1,0:T(8,128)(2,1)S(1)}, u32[]{:S(2)}, u32[]{:S(2)}) collective-permute-start(bf16[2,2,64,128]{3,2,1,0:T(8,128)(2,1)S(1)} %pad_maximum_fusion), channel_id=1, source_target_pairs={{0,4},{1,5},{2,6},{3,7},{4,0},{5,1},{6,2},{7,3},{8,12},{9,13},{10,... | collective-permute-start | bytes 196616 | tf_op jit(solution)/shard_map/ppermute | solution.py:22
  9.6 3.3 %collective-permute-start.2 = (bf16[2,64,128]{2,1,0:T(8,128)(2,1)S(1)}, bf16[2,64,128]{2,1,0:T(8,128)(2,1)S(1)}, u32[]{:S(2)}, u32[]{:S(2)}) collective-permute-start(bf16[2,64,128]{2,1,0:T(8,128)(2,1)S(1)} %get-tuple-element.19), channel_id=1, source_target_pairs={{4,8},{5,9},{6,10},{7,11},{8,4},{9,5},{10,6},{11,7},{20,24},{21,25... | collective-permute-start | bytes 98312 | tf_op jit(solution)/shard_map/ppermute | solution.py:32
  12.3 0.7 %copy-start.5 = (s32[4096]{0:T(1024)S(1)}, s32[4096]{0:T(1024)}, u32[]{:S(2)}) copy-start(s32[4096]{0:T(1024)} %param.11) | copy-start | bytes 49156
  12.3 0.7 %copy-start.6 = (f32[16]{0:T(128)S(1)}, f32[16]{0:T(128)}, u32[]{:S(2)}) copy-start(f32[16]{0:T(128)} %kappa.1) | copy-start | bytes 196
  12.3 4.3 %collective-permute-start.3 = (bf16[4,2,32,128]{3,2,1,0:T(8,128)(2,1)S(1)}, bf16[4,2,32,128]{3,2,1,0:T(8,128)(2,1)S(1)}, u32[]{:S(2)}, u32[]{:S(2)}) collective-permute-start(bf16[4,2,32,128]{3,2,1,0:T(8,128)(2,1)S(1)} %multiply_convert_fusion.vector), channel_id=1, source_target_pairs={{0,16},{16,0},{1,17},{17,1},{2,18},{18,2},{3,19},{19,3},{4,20},{20... | collective-permute-start | bytes 196616 | tf_op jit(solution)/shard_map/ppermute | solution.py:27
  18.1 4.3 %collective-permute-start.5 = (bf16[2,64,128]{2,1,0:T(8,128)(2,1)S(1)}, bf16[2,64,128]{2,1,0:T(8,128)(2,1)S(1)}, u32[]{:S(2)}, u32[]{:S(2)}) collective-permute-start(bf16[2,64,128]{2,1,0:T(8,128)(2,1)S(1)} %get-tuple-element.26), channel_id=1, source_target_pairs={{0,4},{1,5},{2,6},{3,7},{4,0},{5,1},{6,2},{7,3},{8,12},{9,13},{10,... | collective-permute-start | bytes 98312 | tf_op jit(solution)/shard_map/ppermute | solution.py:22
  22.4 4.7 %collective-permute-start.6 = (bf16[2,32,128]{2,1,0:T(8,128)(2,1)S(1)}, bf16[2,32,128]{2,1,0:T(8,128)(2,1)S(1)}, u32[]{:S(2)}, u32[]{:S(2)}) collective-permute-start(bf16[2,32,128]{2,1,0:T(8,128)(2,1)S(1)} %slice.20), channel_id=1, source_target_pairs={{0,8},{1,9},{2,10},{3,11},{4,12},{5,13},{6,14},{7,15},{8,0},{9,1},... | collective-permute-start | bytes 49160 | tf_op jit(solution)/shard_map/ppermute | solution.py:22

commit v4 on v3

v4 whole, which is shorter than its diff:
```python
import functools

import jax
import jax.numpy as jnp
from jax import lax
from jax.experimental import pallas as pl
from jax.experimental.pallas import tpu as pltpu
from jax.sharding import PartitionSpec as P

SPLIT = 4
DIP = 32
LANES = 128
REACH = 2 * DIP
F32 = jnp.float32
BF16 = jnp.bfloat16
PRIOR = pl.CostEstimate(flops=1, bytes_accessed=1, transcendentals=0)
BESIDE = pl.CostEstimate(flops=575_000_000, bytes_accessed=1, transcendentals=0)
PARAMS = pltpu.CompilerParams(vmem_limit_bytes=32 * 2**20)


def swapped(value, axis, mask):
    return lax.ppermute(value, axis, [(i, i ^ mask) for i in range(lax.axis_size(axis))])


def turned(value, axis, step):
    size = lax.axis_size(axis)
    return lax.ppermute(value, axis, [(i, (i + step) % size) for i in range(size)])


def crossed(value, axis, nfreq):
    pairs = [(p * nfreq + f, (p + 1) * nfreq + f) for p in range(1, SPLIT - 1, 2) for f in range(nfreq)]
    return lax.ppermute(value, axis, pairs + [(b, a) for a, b in pairs])


def dot(a, b, form=((1,), (0,))):
    return lax.dot_general(a, b, (form, ((), ())), preferred_element_type=F32)


def chosen(table, index, count, place):
    value = jnp.zeros(index.shape, F32)
    for k in range(count):
        value = jnp.where(index == k, place(table, k), value)
    return value


def stencil():
    row = lax.broadcasted_iota(jnp.int32, (LANES, LANES + 2 * DIP), 0)
    col = lax.broadcasted_iota(jnp.int32, (LANES, LANES + 2 * DIP), 1)
    away = col - DIP - row
    dip = lax.rem(row, DIP)
    hit = (away == DIP) | (away == -DIP)
    hit = hit | ((away == 1) & (dip != DIP - 1)) | ((away == -1) & (dip != 0))
    return hit.astype(F32).astype(BF16)


def planes(ref, b, n):
    return jnp.concatenate([ref[0, b : b + n], ref[1, b : b + n]], axis=1)


def lhs(z):
    rows = z.shape[0] * z.shape[2]
    zr, zi = z[:, 0].reshape(rows, LANES), z[:, 1].reshape(rows, LANES)
    top = jnp.concatenate([zr, zi], axis=1)
    return jnp.concatenate([top, jnp.concatenate([zi, -zr], axis=1)], axis=0)


def prep_kernel(nfreq, noise, station, vector, green, weight, held, facing, other):
    par = lax.axis_index("par")
    freq, part = lax.rem(par, nfreq), lax.div(par, nfreq)
    odd = lax.rem(part, 2)
    cells = green.shape[1]
    first = pl.multiple_of(odd * (cells - REACH), REACH)
    last = pl.multiple_of((1 - odd) * (cells - REACH), REACH)
    held[...] = vector[...]
    facing[...] = green[:, pl.ds(last, REACH)]
    other[...] = green[:, pl.ds(first, REACH)]
    variance = chosen(noise, station[...], noise.shape[1], lambda t, k: t[freq, k])
    weight[...] = 1.0 / jnp.sqrt(variance)


def gram(swept, operator):
    full = dot(swept, operator)
    real = full[:LANES, :LANES] + full[LANES:, LANES:]
    imag = full[:LANES, LANES:] - full[LANES:, :LANES]
    both = jnp.concatenate([real, imag], axis=1)
    high = both.astype(BF16)
    return high, (both - high.astype(F32)).astype(BF16)


def applied(z, high, low):
    side = lhs(z)
    return dot(side, high, ((1,), (1,))) + dot(side, low, ((1,), (1,)))


def own_kernel(nfreq, nclass, kappa, coeff, vector, green, facing, other, swept, base, operator, inverse, first, second):
    part = lax.div(lax.axis_index("par"), nfreq)
    cells = green.shape[1]
    blocks = cells // LANES
    parts = coeff.shape[0] // blocks
    extent = cells + 2 * REACH

    def column(index, inside):
        value = 1.0 / (4.0 + chosen(kappa, index, nclass, lambda t, k: t[k]))
        value = jnp.where(inside, value, 0.0)
        return jnp.transpose(jnp.broadcast_to(value, (LANES, LANES)))

    before = coeff[pl.ds(jnp.maximum(part * blocks - 1, 0), 1), :]
    after = coeff[pl.ds(jnp.minimum((part + 1) * blocks, parts * blocks - 1), 1), :]
    inverse[0:REACH] = column(before, part > 0)[LANES - REACH :]
    inverse[extent - REACH : extent] = column(after, part < parts - 1)[:REACH]
    for b in range(blocks):
        inverse[REACH + b * LANES : REACH + (b + 1) * LANES] = column(
            coeff[pl.ds(part * blocks + b, 1), :], True
        )

    odd = lax.rem(part, 2) == 1
    near, far = planes(facing.at[1], 0, REACH), planes(other, 0, REACH)
    operator[0:REACH] = jnp.where(odd, near, far)
    operator[REACH : REACH + cells] = planes(green, 0, cells)
    operator[extent - REACH : extent] = jnp.where(odd, far, near)

    hood = stencil()
    none = jnp.zeros((DIP, 2 * LANES), BF16)
    for ref in (first, second):
        ref[0:DIP] = none
        ref[DIP + extent : 2 * DIP + extent] = none

    def solved(at, value):
        scale = inverse[at : at + LANES]
        return jnp.concatenate([scale, scale], axis=1) * value

    for at in range(0, extent, LANES):
        value = solved(at, operator[at : at + LANES].astype(F32))
        first[DIP + at : DIP + at + LANES] = value.astype(BF16)
    for at in range(0, extent, LANES):
        total = operator[at : at + LANES].astype(F32) + dot(hood, first[at : at + LANES + 2 * DIP])
        second[DIP + at : DIP + at + LANES] = solved(at, total).astype(BF16)
    for at in range(REACH, REACH + cells, LANES):
        total = operator[at : at + LANES].astype(F32) + dot(hood, second[at : at + LANES + 2 * DIP])
        swept[:, at - REACH : at - REACH + LANES] = jnp.transpose(solved(at, total)).astype(BF16)
    high, low = gram(swept[...], operator[REACH : REACH + cells])
    base[...] = applied(vector[...], high, low)


def cross_kernel(swept, green, pair):
    pair[0], pair[1] = gram(swept[...], planes(green, 0, green.shape[1]))


def data_kernel(nsens, weight, base, *refs):
    vectors, pairs, (keep, send) = refs[: nsens - 1], refs[nsens - 1 : 2 * nsens - 2], refs[2 * nsens - 2 :]
    data = base[...]
    for v, p in zip(vectors, pairs):
        data = data + applied(v[...], p[0], p[1])
    data = weight[...] * data
    half = data.shape[0] // 4
    for k in range(2):
        keep[k] = data[2 * k * half : (2 * k + 1) * half]
        send[k] = data[(2 * k + 1) * half : (2 * k + 2) * half].astype(BF16)


def shards(probes, green_blocks, noise_table, station_class, kappa_table, coeff_index):
    nfreq = noise_table.shape[0]
    nsens = lax.axis_size("sens")
    sensors, rows_dev = probes.shape[1:]
    cells = green_blocks.shape[1]
    smem = pl.BlockSpec(memory_space=pltpu.SMEM)
    vmem = pl.BlockSpec(memory_space=pltpu.VMEM)
    greens = [turned(green_blocks, "sens", k) for k in range(1, nsens)]
    vector = jnp.transpose(probes, (0, 2, 1))
    partner = swapped(vector, "par", 2 * nfreq)

    rim = jax.ShapeDtypeStruct((2, REACH, sensors), BF16)
    weight, held, facing, other = pl.pallas_call(
        functools.partial(prep_kernel, nfreq),
        out_shape=[
            jax.ShapeDtypeStruct((1, sensors), F32),
            jax.ShapeDtypeStruct((2, rows_dev, sensors), BF16),
            rim,
            rim,
        ],
        in_specs=[smem] + [vmem] * 3,
        out_specs=[vmem] * 4,
        compiler_params=PARAMS,
        cost_estimate=PRIOR,
        name="prep",
    )(noise_table, station_class.reshape(1, -1), vector, green_blocks)

    mine = jnp.stack([held, partner])
    sent = jnp.stack([mine.reshape(2, -1, sensors), facing])
    got = swapped(sent, "par", nfreq)
    other = crossed(other, "par", nfreq)
    vectors = jnp.concatenate([mine, got[0].reshape(mine.shape)], axis=0)
    vectors = (weight * vectors.astype(F32)).astype(BF16)
    rest = [turned(vectors, "sens", k) for k in range(1, nsens)]
    rows = SPLIT * rows_dev
    extent = cells + 2 * REACH
    swept, base = pl.pallas_call(
        functools.partial(own_kernel, nfreq, kappa_table.shape[0]),
        out_shape=[
            jax.ShapeDtypeStruct((2 * sensors, cells), BF16),
            jax.ShapeDtypeStruct((2 * rows, sensors), F32),
        ],
        in_specs=[smem] + [vmem] * 5,
        out_specs=[vmem] * 2,
        scratch_shapes=[
            pltpu.VMEM((extent, 2 * sensors), BF16),
            pltpu.VMEM((extent, LANES), F32),
            pltpu.VMEM((extent + 2 * DIP, 2 * sensors), BF16),
            pltpu.VMEM((extent + 2 * DIP, 2 * sensors), BF16),
        ],
        compiler_params=PARAMS,
        cost_estimate=BESIDE,
        name="own",
    )(kappa_table, coeff_index.reshape(-1, LANES), vectors, green_blocks, got, other)
    pairs = [
        pl.pallas_call(
            cross_kernel,
            out_shape=jax.ShapeDtypeStruct((2, sensors, 2 * sensors), BF16),
            in_specs=[vmem] * 2,
            out_specs=vmem,
            compiler_params=PARAMS,
            cost_estimate=PRIOR,
            name="cross",
        )(swept, g)
        for g in greens
    ]
    keep, send = pl.pallas_call(
        functools.partial(data_kernel, nsens),
        out_shape=[
            jax.ShapeDtypeStruct((2, rows // 2, sensors), F32),
            jax.ShapeDtypeStruct((2, rows // 2, sensors), BF16),
        ],
        in_specs=[vmem] * (2 * nsens),
        out_specs=[vmem] * 2,
        compiler_params=PARAMS,
        name="data",
    )(weight, base, *rest, *pairs)
    near = keep + swapped(send, "par", nfreq).astype(F32)
    far = swapped(near[:, rows_dev:].astype(BF16), "par", 2 * nfreq)
    return jnp.transpose(near[:, :rows_dev] + far.astype(F32), (0, 2, 1))


def solution(mesh):
    in_specs = (P(None, "sens", "par"), P(None, "par", "sens"), P(), P("sens"), P(), P())
    out_specs = P(None, "sens", "par")
    return jax.shard_map(shards, mesh=mesh, in_specs=in_specs, out_specs=out_specs, check_vma=False)
```

time: 28.1 us -> 27.2 us (0.968)
  waiting for transfers between devices: 8.84 us -> 7.23 us
  starting transfers between devices: 13.2 us -> 14.1 us
    ppermute x2, waiting for transfers between devices: 2.61 us -> 1.58 us  [turned(): lax.ppermute(value, axis, [(i, (i + step) % size) for i in range(size)])]
    pallas_call x1 -> x2, Pallas kernels: 1.42 us -> 0.54 us  [the longest x1 0.32 us: shards(): pl.pallas_call(cross_kernel, out_shape=jax.ShapeDtypeStruct((2, sensors,...]
    ppermute x4, starting transfers between devices: 9.04 us -> 9.91 us  [swapped(): lax.ppermute(value, axis, [(i, i ^ mask) for i in range(lax.axis_size(axi...]
    pallas_call x1, Pallas kernels: 1.03 us -> 1.73 us  [shards(): pl.pallas_call(functools.partial(own_kernel, nfreq, kappa_table.shape[0])...]
    ppermute x4, waiting for transfers between devices: 6.23 us -> 5.65 us  [swapped(): lax.ppermute(value, axis, [(i, i ^ mask) for i in range(lax.axis_size(axi...]
  transfers between devices with their start and end apart: 7 -> 7, of which waited for: 4 -> 5; matrix products, arithmetic and copies ran while one was open for 0% -> 0% of each run, Pallas kernels for 6% -> 10%
where the time goes in v4:
time: 27.2 us; the launch traced here: 26.8 us
  starting transfers between devices  14.1 us (52%)
  waiting for transfers between devices  7.23 us (27%)
  Pallas kernels  2.86 us (11%)
  local copies, waits for them, and re-layouts  1.89 us (7%)
  other arithmetic  0.66 us (2%)
    ppermute x4, starting transfers between devices, swapped(): lax.ppermute(value, axis, [(i, i ^ mask) for i in range(lax.axis_size(axi...  9.91 us
    ppermute x4, waiting for transfers between devices, swapped(): lax.ppermute(value, axis, [(i, i ^ mask) for i in range(lax.axis_size(axi...  5.65 us
    ppermute x2, starting transfers between devices, turned(): lax.ppermute(value, axis, [(i, (i + step) % size) for i in range(size)])  3.54 us
    unnamed x14, local copies, waits for them, and re-layouts  1.88 us
    pallas_call x1, Pallas kernels, shards(): pl.pallas_call(functools.partial(own_kernel, nfreq, kappa_table.shape[0])...  1.73 us
    ppermute x2, waiting for transfers between devices, turned(): lax.ppermute(value, axis, [(i, (i + step) % size) for i in range(size)])  1.58 us
    ppermute x1, starting transfers between devices, crossed(): return lax.ppermute(value, axis, pairs + [(b, a) for a, b in pairs])  0.65 us
    transpose x1, other arithmetic, shards(): return jnp.transpose(near[:, :rows_dev] + far.astype(F32), (0, 2, 1))  0.62 us
  transfers between devices with their start and end apart: 7, of which 5 were waited for; matrix products, arithmetic and copies ran while one was open for 0% of the time, Pallas kernels for 10%

profile of v4, /device:TPU:0, one launch (start us, length us, event | category | flops | bytes accessed | tf_op | source)
XLA Modules:
  0.0 26.8 jit_solution(2254034093941282851)
XLA Ops:
  0.0 0.0 copy-start.3
  0.0 3.0 %collective-permute-start.4 = (bf16[2,1024,128]{2,1,0:T(8,128)(2,1)}, bf16[2,1024,128]{2,1,0:T(8,128)(2,1)S(1)}, u32[]{:S(2)}, u32[]{:S(2)}) collective-permute-start(bf16[2,1024,128]{2,1,0:T(8,128)(2,1)} %green.3), channel_id=1, source_target_pairs={{0,16},{16,0},{1,17},{17,1},{2,18},{18,2},{3,19},{19,3},{4,20},{20... | collective-permute-start | bytes 1572872 | tf_op jit(solution)/shard_map/ppermute | solution.py:27
  3.0 0.0 copy-start.4
  3.0 2.6 %collective-permute-start = (bf16[2,32,128]{2,1,0:T(8,128)(2,1)}, bf16[2,32,128]{2,1,0:T(8,128)(2,1)S(1)}, u32[]{:S(2)}, u32[]{:S(2)}) collective-permute-start(bf16[2,32,128]{2,1,0:T(8,128)(2,1)} %bitcast.15), channel_id=1, source_target_pairs={{0,8},{1,9},{2,10},{3,11},{4,12},{5,13},{6,14},{7,15},{8,0},{9,1},... | collective-permute-start | bytes 49160 | tf_op jit(solution)/shard_map/ppermute | solution.py:22
  5.6 0.0 copy-done.3
  5.6 0.0 copy-done.4
  5.6 1.0 %copy-done = bf16[2,1024,128]{2,1,0:T(8,128)(2,1)S(1)} copy-done((bf16[2,1024,128]{2,1,0:T(8,128)(2,1)S(1)}, bf16[2,1024,128]{2,1,0:T(8,128)(2,1)}, u32[]{:S(2)}) %copy-start) | copy-done | bytes 524312
  6.6 0.0 copy-start.2
  6.6 0.7 %copy-done.2 = bf16[2,128,32]{1,2,0:T(8,128)(2,1)S(1)} copy-done((bf16[2,128,32]{1,2,0:T(8,128)(2,1)S(1)}, bf16[2,128,32]{1,2,0:T(8,128)(2,1)}, u32[]{:S(2)}) %copy-start.2) | copy-done | bytes 16408
  7.3 0.0 copy-start.1
  7.3 0.6 %prep.1 = (f32[1,128]{1,0:T(1,128)S(1)}, bf16[2,32,128]{2,1,0:T(8,128)(2,1)S(1)}, bf16[2,64,128]{2,1,0:T(8,128)(2,1)S(1)}, bf16[2,64,128]{2,1,0:T(8,128)(2,1)S(1)}) custom-call(f32[4,8]{1,0:T(4,128)S(1)} %copy-done.3, s32[1,128]{1,0:T(1,128)S(1)} %bitcast.18, bf16[2,32,128]{2,1,0:T(8,128)(2,1)S(1)} %bitcast.16, bf16[2,1024,128]{2,1,0:T(8,128)(2,1)S(1)} %copy-done), custom_call_target="tpu_custom_call" | custom-call | flops 1 | bytes 1 | tf_op jit(solution)/shard_map/prep/pallas_call | solution.py:173
  7.9 0.0 collective-permute-done
  8.0 1.6 %collective-permute-start.1 = (bf16[2,2,64,128]{3,2,1,0:T(8,128)(2,1)S(1)}, bf16[2,2,64,128]{3,2,1,0:T(8,128)(2,1)S(1)}, u32[]{:S(2)}, u32[]{:S(2)}) collective-permute-start(bf16[2,2,64,128]{3,2,1,0:T(8,128)(2,1)S(1)} %pad_maximum_fusion), channel_id=1, source_target_pairs={{0,4},{1,5},{2,6},{3,7},{4,0},{5,1},{6,2},{7,3},{8,12},{9,13},{10,... | collective-permute-start | bytes 196616 | tf_op jit(solution)/shard_map/ppermute | solution.py:22
  9.6 0.7 %collective-permute-start.2 = (bf16[2,64,128]{2,1,0:T(8,128)(2,1)S(1)}, bf16[2,64,128]{2,1,0:T(8,128)(2,1)S(1)}, u32[]{:S(2)}, u32[]{:S(2)}) collective-permute-start(bf16[2,64,128]{2,1,0:T(8,128)(2,1)S(1)} %get-tuple-element.16), channel_id=1, source_target_pairs={{4,8},{5,9},{6,10},{7,11},{8,4},{9,5},{10,6},{11,7},{20,24},{21,25... | collective-permute-start | bytes 98312 | tf_op jit(solution)/shard_map/ppermute | solution.py:32
  10.3 2.0 %collective-permute-done.1.facing = bf16[2,2,64,128]{3,2,1,0:T(8,128)(2,1)S(1)} collective-permute-done((bf16[2,2,64,128]{3,2,1,0:T(8,128)(2,1)S(1)}, bf16[2,2,64,128]{3,2,1,0:T(8,128)(2,1)S(1)}, u32[]{:S(2)}, u32[]{:S(2)}) %collective-permute-start.1) | collective-permute-done | bytes 65568 | tf_op jit(solution)/shard_map/ppermute | solution.py:22
  12.3 0.0 copy-start.5
  12.3 0.0 copy-start.6
  12.3 0.6 %collective-permute-start.3 = (bf16[4,2,32,128]{3,2,1,0:T(8,128)(2,1)S(1)}, bf16[4,2,32,128]{3,2,1,0:T(8,128)(2,1)S(1)}, u32[]{:S(2)}, u32[]{:S(2)}) collective-permute-start(bf16[4,2,32,128]{3,2,1,0:T(8,128)(2,1)S(1)} %multiply_convert_fusion.vector), channel_id=1, source_target_pairs={{0,16},{16,0},{1,17},{17,1},{2,18},{18,2},{3,19},{19,3},{4,20},{20... | collective-permute-start | bytes 196616 | tf_op jit(solution)/shard_map/ppermute | solution.py:27
  12.9 0.0 collective-permute-done.2.other
  12.9 0.0 copy-done.1
  12.9 0.1 copy-done.5
  13.0 0.0 copy-done.6
  13.0 1.7 %own.1 = (bf16[256,1024]{1,0:T(8,128)(2,1)S(1)}, f32[256,128]{1,0:T(8,128)S(1)}) custom-call(f32[16]{0:T(128)S(1)} %copy-done.6, s32[32,128]{1,0:T(8,128)S(1)} %bitcast.19, bf16[4,2,32,128]{3,2,1,0:T(8,128)(2,1)S(1)} %multiply_convert_fusion.vector, bf16[2,1024,128]{2,1,0:T(8,128)(2,1)S(1)} %copy-done.1, ...), custom_call_target="tpu_custom_call" | custom-call | flops 575000000 | bytes 1 | tf_op jit(solution)/shard_map/own/pallas_call | solution.py:197
  14.8 1.1 %collective-permute-done.4.green = bf16[2,1024,128]{2,1,0:T(8,128)(2,1)S(1)} collective-permute-done((bf16[2,1024,128]{2,1,0:T(8,128)(2,1)}, bf16[2,1024,128]{2,1,0:T(8,128)(2,1)S(1)}, u32[]{:S(2)}, u32[]{:S(2)}) %collective-permute-start.4) | collective-permute-done | bytes 524320 | tf_op jit(solution)/shard_map/ppermute | solution.py:27
  15.8 0.3 %cross.1.refs_1_ = bf16[2,128,256]{2,1,0:T(8,128)(2,1)S(1)} custom-call(bf16[256,1024]{1,0:T(8,128)(2,1)S(1)} %get-tuple-element.18.swept, bf16[2,1024,128]{2,1,0:T(8,128)(2,1)S(1)} %collective-permute-done.4.green), custom_call_target="tpu_custom_call" | custom-call | flops 1 | bytes 1 | tf_op jit(solution)/shard_map/cross/pallas_call | solution.py:216
  16.1 0.5 %collective-permute-done.3.refs_0_ = bf16[4,2,32,128]{3,2,1,0:T(8,128)(2,1)S(1)} collective-permute-done((bf16[4,2,32,128]{3,2,1,0:T(8,128)(2,1)S(1)}, bf16[4,2,32,128]{3,2,1,0:T(8,128)(2,1)S(1)}, u32[]{:S(2)}, u32[]{:S(2)}) %collective-permute-start.3) | collective-permute-done | bytes 65568 | tf_op jit(solution)/shard_map/ppermute | solution.py:27
  16.7 0.2 data.1
  16.9 2.4 %collective-permute-start.5 = (bf16[2,64,128]{2,1,0:T(8,128)(2,1)S(1)}, bf16[2,64,128]{2,1,0:T(8,128)(2,1)S(1)}, u32[]{:S(2)}, u32[]{:S(2)}) collective-permute-start(bf16[2,64,128]{2,1,0:T(8,128)(2,1)S(1)} %get-tuple-element.20), channel_id=1, source_target_pairs={{0,4},{1,5},{2,6},{3,7},{4,0},{5,1},{6,2},{7,3},{8,12},{9,13},{10,... | collective-permute-start | bytes 98312 | tf_op jit(solution)/shard_map/ppermute | solution.py:22
  19.3 1.9 %collective-permute-done.5 = bf16[2,64,128]{2,1,0:T(8,128)(2,1)S(1)} collective-permute-done((bf16[2,64,128]{2,1,0:T(8,128)(2,1)S(1)}, bf16[2,64,128]{2,1,0:T(8,128)(2,1)S(1)}, u32[]{:S(2)}, u32[]{:S(2)}) %collective-permute-start.5) | collective-permute-done | bytes 32800 | tf_op jit(solution)/shard_map/ppermute | solution.py:22
  21.2 3.3 %collective-permute-start.6 = (bf16[2,32,128]{2,1,0:T(8,128)(2,1)S(1)}, bf16[2,32,128]{2,1,0:T(8,128)(2,1)S(1)}, u32[]{:S(2)}, u32[]{:S(2)}) collective-permute-start(bf16[2,32,128]{2,1,0:T(8,128)(2,1)S(1)} %slice.20), channel_id=1, source_target_pairs={{0,8},{1,9},{2,10},{3,11},{4,12},{5,13},{6,14},{7,15},{8,0},{9,1},... | collective-permute-start | bytes 49160 | tf_op jit(solution)/shard_map/ppermute | solution.py:22
  24.5 1.7 %collective-permute-done.6 = bf16[2,32,128]{2,1,0:T(8,128)(2,1)S(1)} collective-permute-done((bf16[2,32,128]{2,1,0:T(8,128)(2,1)S(1)}, bf16[2,32,128]{2,1,0:T(8,128)(2,1)S(1)}, u32[]{:S(2)}, u32[]{:S(2)}) %collective-permute-start.6) | collective-permute-done | bytes 16416 | tf_op jit(solution)/shard_map/ppermute | solution.py:22
  26.2 0.6 %fusion = f32[2,128,32]{1,2,0:T(8,128)} fusion(f32[2,64,128]{2,1,0:T(8,128)S(1)} %convert_add_fusion, bf16[2,32,128]{2,1,0:T(8,128)(2,1)S(1)} %collective-permute-done.6), kind=kLoop, calls=%fused_computation.5 | loop fusion | flops 16384 | bytes 81920 | tf_op jit(solution)/shard_map/transpose | solution.py:240
  (6 shorter events, 0.0 us)
Async XLA Ops:
  0.0 5.6 %copy-start.3 = (f32[4,8]{1,0:T(4,128)S(1)}, f32[4,8]{1,0:T(4,128)}, u32[]{:S(2)}) copy-start(f32[4,8]{1,0:T(4,128)} %noise.1) | copy-start | bytes 388
  0.0 15.8 %collective-permute-start.4 = (bf16[2,1024,128]{2,1,0:T(8,128)(2,1)}, bf16[2,1024,128]{2,1,0:T(8,128)(2,1)S(1)}, u32[]{:S(2)}, u32[]{:S(2)}) collective-permute-start(bf16[2,1024,128]{2,1,0:T(8,128)(2,1)} %green.3), channel_id=1, source_target_pairs={{0,16},{16,0},{1,17},{17,1},{2,18},{18,2},{3,19},{19,3},{4,20},{20... | collective-permute-start | bytes 1572872 | tf_op jit(solution)/shard_map/ppermute | solution.py:27
  3.0 2.6 %copy-start.4 = (s32[128]{0:T(128)S(1)}, s32[128]{0:T(128)}, u32[]{:S(2)}) copy-start(s32[128]{0:T(128)} %param.9) | copy-start | bytes 1540
  3.0 5.0 %collective-permute-start = (bf16[2,32,128]{2,1,0:T(8,128)(2,1)}, bf16[2,32,128]{2,1,0:T(8,128)(2,1)S(1)}, u32[]{:S(2)}, u32[]{:S(2)}) collective-permute-start(bf16[2,32,128]{2,1,0:T(8,128)(2,1)} %bitcast.15), channel_id=1, source_target_pairs={{0,8},{1,9},{2,10},{3,11},{4,12},{5,13},{6,14},{7,15},{8,0},{9,1},... | collective-permute-start | bytes 49160 | tf_op jit(solution)/shard_map/ppermute | solution.py:22
  5.6 1.0 %copy-start = (bf16[2,1024,128]{2,1,0:T(8,128)(2,1)S(1)}, bf16[2,1024,128]{2,1,0:T(8,128)(2,1)}, u32[]{:S(2)}) copy-start(bf16[2,1024,128]{2,1,0:T(8,128)(2,1)} %green.3) | copy-start | bytes 1572868
  6.6 0.7 %copy-start.2 = (bf16[2,128,32]{1,2,0:T(8,128)(2,1)S(1)}, bf16[2,128,32]{1,2,0:T(8,128)(2,1)}, u32[]{:S(2)}) copy-start(bf16[2,128,32]{1,2,0:T(8,128)(2,1)} %param.6) | copy-start | bytes 49156
  7.3 5.6 %copy-start.1 = (bf16[2,1024,128]{2,1,0:T(8,128)(2,1)S(1)}, bf16[2,1024,128]{2,1,0:T(8,128)(2,1)}, u32[]{:S(2)}) copy-start(bf16[2,1024,128]{2,1,0:T(8,128)(2,1)} %green.3) | copy-start | bytes 1572868
  8.0 4.3 %collective-permute-start.1 = (bf16[2,2,64,128]{3,2,1,0:T(8,128)(2,1)S(1)}, bf16[2,2,64,128]{3,2,1,0:T(8,128)(2,1)S(1)}, u32[]{:S(2)}, u32[]{:S(2)}) collective-permute-start(bf16[2,2,64,128]{3,2,1,0:T(8,128)(2,1)S(1)} %pad_maximum_fusion), channel_id=1, source_target_pairs={{0,4},{1,5},{2,6},{3,7},{4,0},{5,1},{6,2},{7,3},{8,12},{9,13},{10,... | collective-permute-start | bytes 196616 | tf_op jit(solution)/shard_map/ppermute | solution.py:22
  9.6 3.3 %collective-permute-start.2 = (bf16[2,64,128]{2,1,0:T(8,128)(2,1)S(1)}, bf16[2,64,128]{2,1,0:T(8,128)(2,1)S(1)}, u32[]{:S(2)}, u32[]{:S(2)}) collective-permute-start(bf16[2,64,128]{2,1,0:T(8,128)(2,1)S(1)} %get-tuple-element.16), channel_id=1, source_target_pairs={{4,8},{5,9},{6,10},{7,11},{8,4},{9,5},{10,6},{11,7},{20,24},{21,25... | collective-permute-start | bytes 98312 | tf_op jit(solution)/shard_map/ppermute | solution.py:32
  12.3 0.7 %copy-start.5 = (s32[4096]{0:T(1024)S(1)}, s32[4096]{0:T(1024)}, u32[]{:S(2)}) copy-start(s32[4096]{0:T(1024)} %param.11) | copy-start | bytes 49156
  12.3 0.7 %copy-start.6 = (f32[16]{0:T(128)S(1)}, f32[16]{0:T(128)}, u32[]{:S(2)}) copy-start(f32[16]{0:T(128)} %kappa.1) | copy-start | bytes 196
  12.3 4.3 %collective-permute-start.3 = (bf16[4,2,32,128]{3,2,1,0:T(8,128)(2,1)S(1)}, bf16[4,2,32,128]{3,2,1,0:T(8,128)(2,1)S(1)}, u32[]{:S(2)}, u32[]{:S(2)}) collective-permute-start(bf16[4,2,32,128]{3,2,1,0:T(8,128)(2,1)S(1)} %multiply_convert_fusion.vector), channel_id=1, source_target_pairs={{0,16},{16,0},{1,17},{17,1},{2,18},{18,2},{3,19},{19,3},{4,20},{20... | collective-permute-start | bytes 196616 | tf_op jit(solution)/shard_map/ppermute | solution.py:27
  16.9 4.3 %collective-permute-start.5 = (bf16[2,64,128]{2,1,0:T(8,128)(2,1)S(1)}, bf16[2,64,128]{2,1,0:T(8,128)(2,1)S(1)}, u32[]{:S(2)}, u32[]{:S(2)}) collective-permute-start(bf16[2,64,128]{2,1,0:T(8,128)(2,1)S(1)} %get-tuple-element.20), channel_id=1, source_target_pairs={{0,4},{1,5},{2,6},{3,7},{4,0},{5,1},{6,2},{7,3},{8,12},{9,13},{10,... | collective-permute-start | bytes 98312 | tf_op jit(solution)/shard_map/ppermute | solution.py:22
  21.2 5.0 %collective-permute-start.6 = (bf16[2,32,128]{2,1,0:T(8,128)(2,1)S(1)}, bf16[2,32,128]{2,1,0:T(8,128)(2,1)S(1)}, u32[]{:S(2)}, u32[]{:S(2)}) collective-permute-start(bf16[2,32,128]{2,1,0:T(8,128)(2,1)S(1)} %slice.20), channel_id=1, source_target_pairs={{0,8},{1,9},{2,10},{3,11},{4,12},{5,13},{6,14},{7,15},{8,0},{9,1},... | collective-permute-start | bytes 49160 | tf_op jit(solution)/shard_map/ppermute | solution.py:22

commit v5 on v4

--- a/solution.py
+++ b/solution.py
@@ -28,8 +28,12 @@
 
 
 def crossed(value, axis, nfreq):
-    pairs = [(p * nfreq + f, (p + 1) * nfreq + f) for p in range(1, SPLIT - 1, 2) for f in range(nfreq)]
-    return lax.ppermute(value, axis, pairs + [(b, a) for a, b in pairs])
+    pairs = []
+    for i in range(lax.axis_size(axis)):
+        part = i // nfreq
+        outer = part in (0, SPLIT - 1)
+        pairs.append((i, i ^ 1 if outer else i + nfreq if part % 2 else i - nfreq))
+    return lax.ppermute(value, axis, pairs)
 
 
 def dot(a, b, form=((1,), (0,))):
@@ -99,19 +103,19 @@
     parts = coeff.shape[0] // blocks
     extent = cells + 2 * REACH
 
-    def column(index, inside):
-        value = 1.0 / (4.0 + chosen(kappa, index, nclass, lambda t, k: t[k]))
-        value = jnp.where(inside, value, 0.0)
+    def inv(index):
+        return 1.0 / (4.0 + chosen(kappa, index, nclass, lambda t, k: t[k]))
+
+    def column(value):
         return jnp.transpose(jnp.broadcast_to(value, (LANES, LANES)))
 
-    before = coeff[pl.ds(jnp.maximum(part * blocks - 1, 0), 1), :]
-    after = coeff[pl.ds(jnp.minimum((part + 1) * blocks, parts * blocks - 1), 1), :]
-    inverse[0:REACH] = column(before, part > 0)[LANES - REACH :]
-    inverse[extent - REACH : extent] = column(after, part < parts - 1)[:REACH]
+    before = inv(coeff[pl.ds(jnp.maximum(part * blocks - 1, 0), 1), :])
+    after = inv(coeff[pl.ds(jnp.minimum((part + 1) * blocks, parts * blocks - 1), 1), :])
+    inside = inv(coeff[pl.ds(pl.multiple_of(part * blocks, blocks), blocks), :])
+    inverse[0:REACH] = column(jnp.where(part > 0, before, 0.0))[LANES - REACH :]
+    inverse[extent - REACH : extent] = column(jnp.where(part < parts - 1, after, 0.0))[:REACH]
     for b in range(blocks):
-        inverse[REACH + b * LANES : REACH + (b + 1) * LANES] = column(
-            coeff[pl.ds(part * blocks + b, 1), :], True
-        )
+        inverse[REACH + b * LANES : REACH + (b + 1) * LANES] = column(inside[b : b + 1])
 
     odd = lax.rem(part, 2) == 1
     near, far = planes(facing.at[1], 0, REACH), planes(other, 0, REACH)

time: 27.2 us -> 26.5 us (0.974)
  starting transfers between devices: 14.1 us -> 12.2 us
  waiting for transfers between devices: 7.23 us -> 8.52 us
    ppermute x4, waiting for transfers between devices: 5.65 us -> 6.94 us  [swapped(): lax.ppermute(value, axis, [(i, i ^ mask) for i in range(lax.axis_size(axi...]
    ppermute x4, starting transfers between devices: 9.91 us -> 8.66 us  [swapped(): lax.ppermute(value, axis, [(i, i ^ mask) for i in range(lax.axis_size(axi...]
    ppermute x1, starting transfers between devices: 0.65 us -> 0.01 us  [crossed(): return lax.ppermute(value, axis, pairs)]
where the time goes in v5:
time: 26.5 us; the launch traced here: 26.2 us
  starting transfers between devices  12.2 us (46%)
  waiting for transfers between devices  8.52 us (32%)
  Pallas kernels  2.87 us (11%)
  local copies, waits for them, and re-layouts  1.89 us (7%)
  other arithmetic  0.66 us (2%)
    ppermute x4, starting transfers between devices, swapped(): lax.ppermute(value, axis, [(i, i ^ mask) for i in range(lax.axis_size(axi...  8.66 us
    ppermute x4, waiting for transfers between devices, swapped(): lax.ppermute(value, axis, [(i, i ^ mask) for i in range(lax.axis_size(axi...  6.94 us
    ppermute x2, starting transfers between devices, turned(): lax.ppermute(value, axis, [(i, (i + step) % size) for i in range(size)])  3.54 us
    unnamed x14, local copies, waits for them, and re-layouts  1.88 us
    pallas_call x1, Pallas kernels, shards(): pl.pallas_call(functools.partial(own_kernel, nfreq, kappa_table.shape[0])...  1.73 us
    ppermute x2, waiting for transfers between devices, turned(): lax.ppermute(value, axis, [(i, (i + step) % size) for i in range(size)])  1.58 us
    transpose x1, other arithmetic, shards(): return jnp.transpose(near[:, :rows_dev] + far.astype(F32), (0, 2, 1))  0.62 us
    pallas_call x1, Pallas kernels, shards(): pl.pallas_call(functools.partial(prep_kernel, nfreq), out_shape=[jax.Shap...  0.59 us
  transfers between devices with their start and end apart: 7, of which 5 were waited for; matrix products, arithmetic and copies ran while one was open for 0% of the time, Pallas kernels for 10%

profile of v5, /device:TPU:0, one launch (start us, length us, event | category | flops | bytes accessed | tf_op | source)
XLA Modules:
  0.0 26.2 jit_solution(10053282937582322880)
XLA Ops:
  0.0 0.0 copy-start.3
  0.0 3.0 %collective-permute-start.4 = (bf16[2,1024,128]{2,1,0:T(8,128)(2,1)}, bf16[2,1024,128]{2,1,0:T(8,128)(2,1)S(1)}, u32[]{:S(2)}, u32[]{:S(2)}) collective-permute-start(bf16[2,1024,128]{2,1,0:T(8,128)(2,1)} %green.3), channel_id=1, source_target_pairs={{0,16},{16,0},{1,17},{17,1},{2,18},{18,2},{3,19},{19,3},{4,20},{20... | collective-permute-start | bytes 1572872 | tf_op jit(solution)/shard_map/ppermute | solution.py:27
  3.0 0.0 copy-start.4
  3.0 2.6 %collective-permute-start = (bf16[2,32,128]{2,1,0:T(8,128)(2,1)}, bf16[2,32,128]{2,1,0:T(8,128)(2,1)S(1)}, u32[]{:S(2)}, u32[]{:S(2)}) collective-permute-start(bf16[2,32,128]{2,1,0:T(8,128)(2,1)} %bitcast.15), channel_id=1, source_target_pairs={{0,8},{1,9},{2,10},{3,11},{4,12},{5,13},{6,14},{7,15},{8,0},{9,1},... | collective-permute-start | bytes 49160 | tf_op jit(solution)/shard_map/ppermute | solution.py:22
  5.6 0.0 copy-done.3
  5.6 0.0 copy-done.4
  5.6 0.0 copy-start
  5.6 1.0 %copy-done = bf16[2,1024,128]{2,1,0:T(8,128)(2,1)S(1)} copy-done((bf16[2,1024,128]{2,1,0:T(8,128)(2,1)S(1)}, bf16[2,1024,128]{2,1,0:T(8,128)(2,1)}, u32[]{:S(2)}) %copy-start) | copy-done | bytes 524312
  6.6 0.0 copy-start.2
  6.6 0.7 %copy-done.2 = bf16[2,128,32]{1,2,0:T(8,128)(2,1)S(1)} copy-done((bf16[2,128,32]{1,2,0:T(8,128)(2,1)S(1)}, bf16[2,128,32]{1,2,0:T(8,128)(2,1)}, u32[]{:S(2)}) %copy-start.2) | copy-done | bytes 16408
  7.3 0.0 copy-start.1
  7.3 0.6 %prep.1 = (f32[1,128]{1,0:T(1,128)S(1)}, bf16[2,32,128]{2,1,0:T(8,128)(2,1)S(1)}, bf16[2,64,128]{2,1,0:T(8,128)(2,1)S(1)}, bf16[2,64,128]{2,1,0:T(8,128)(2,1)S(1)}) custom-call(f32[4,8]{1,0:T(4,128)S(1)} %copy-done.3, s32[1,128]{1,0:T(1,128)S(1)} %bitcast.18, bf16[2,32,128]{2,1,0:T(8,128)(2,1)S(1)} %bitcast.16, bf16[2,1024,128]{2,1,0:T(8,128)(2,1)S(1)} %copy-done), custom_call_target="tpu_custom_call" | custom-call | flops 1 | bytes 1 | tf_op jit(solution)/shard_map/prep/pallas_call | solution.py:177
  7.9 0.0 collective-permute-done
  8.0 1.6 %collective-permute-start.1 = (bf16[2,2,64,128]{3,2,1,0:T(8,128)(2,1)S(1)}, bf16[2,2,64,128]{3,2,1,0:T(8,128)(2,1)S(1)}, u32[]{:S(2)}, u32[]{:S(2)}) collective-permute-start(bf16[2,2,64,128]{3,2,1,0:T(8,128)(2,1)S(1)} %pad_maximum_fusion), channel_id=1, source_target_pairs={{0,4},{1,5},{2,6},{3,7},{4,0},{5,1},{6,2},{7,3},{8,12},{9,13},{10,... | collective-permute-start | bytes 196616 | tf_op jit(solution)/shard_map/ppermute | solution.py:22
  9.6 0.0 collective-permute-start.2
  9.6 2.7 %collective-permute-done.1.facing = bf16[2,2,64,128]{3,2,1,0:T(8,128)(2,1)S(1)} collective-permute-done((bf16[2,2,64,128]{3,2,1,0:T(8,128)(2,1)S(1)}, bf16[2,2,64,128]{3,2,1,0:T(8,128)(2,1)S(1)}, u32[]{:S(2)}, u32[]{:S(2)}) %collective-permute-start.1) | collective-permute-done | bytes 65568 | tf_op jit(solution)/shard_map/ppermute | solution.py:22
  12.3 0.0 copy-start.6
  12.3 0.6 %collective-permute-start.3 = (bf16[4,2,32,128]{3,2,1,0:T(8,128)(2,1)S(1)}, bf16[4,2,32,128]{3,2,1,0:T(8,128)(2,1)S(1)}, u32[]{:S(2)}, u32[]{:S(2)}) collective-permute-start(bf16[4,2,32,128]{3,2,1,0:T(8,128)(2,1)S(1)} %multiply_convert_fusion.vector), channel_id=1, source_target_pairs={{0,16},{16,0},{1,17},{17,1},{2,18},{18,2},{3,19},{19,3},{4,20},{20... | collective-permute-start | bytes 196616 | tf_op jit(solution)/shard_map/ppermute | solution.py:27
  12.9 0.0 collective-permute-done.2.other
  12.9 0.0 copy-done.1
  12.9 0.1 copy-done.5
  13.0 0.0 copy-done.6
  13.0 1.7 %own.1 = (bf16[256,1024]{1,0:T(8,128)(2,1)S(1)}, f32[256,128]{1,0:T(8,128)S(1)}) custom-call(f32[16]{0:T(128)S(1)} %copy-done.6, s32[32,128]{1,0:T(8,128)S(1)} %bitcast.19, bf16[4,2,32,128]{3,2,1,0:T(8,128)(2,1)S(1)} %multiply_convert_fusion.vector, bf16[2,1024,128]{2,1,0:T(8,128)(2,1)S(1)} %copy-done.1, ...), custom_call_target="tpu_custom_call" | custom-call | flops 575000000 | bytes 1 | tf_op jit(solution)/shard_map/own/pallas_call | solution.py:201
  14.8 1.0 %collective-permute-done.4.green = bf16[2,1024,128]{2,1,0:T(8,128)(2,1)S(1)} collective-permute-done((bf16[2,1024,128]{2,1,0:T(8,128)(2,1)}, bf16[2,1024,128]{2,1,0:T(8,128)(2,1)S(1)}, u32[]{:S(2)}, u32[]{:S(2)}) %collective-permute-start.4) | collective-permute-done | bytes 524320 | tf_op jit(solution)/shard_map/ppermute | solution.py:27
  15.8 0.3 %cross.1.refs_1_ = bf16[2,128,256]{2,1,0:T(8,128)(2,1)S(1)} custom-call(bf16[256,1024]{1,0:T(8,128)(2,1)S(1)} %get-tuple-element.18.swept, bf16[2,1024,128]{2,1,0:T(8,128)(2,1)S(1)} %collective-permute-done.4.green), custom_call_target="tpu_custom_call" | custom-call | flops 1 | bytes 1 | tf_op jit(solution)/shard_map/cross/pallas_call | solution.py:220
  16.1 0.5 %collective-permute-done.3.refs_0_ = bf16[4,2,32,128]{3,2,1,0:T(8,128)(2,1)S(1)} collective-permute-done((bf16[4,2,32,128]{3,2,1,0:T(8,128)(2,1)S(1)}, bf16[4,2,32,128]{3,2,1,0:T(8,128)(2,1)S(1)}, u32[]{:S(2)}, u32[]{:S(2)}) %collective-permute-start.3) | collective-permute-done | bytes 65568 | tf_op jit(solution)/shard_map/ppermute | solution.py:27
  16.7 0.2 data.1
  16.9 1.7 %collective-permute-start.5 = (bf16[2,64,128]{2,1,0:T(8,128)(2,1)S(1)}, bf16[2,64,128]{2,1,0:T(8,128)(2,1)S(1)}, u32[]{:S(2)}, u32[]{:S(2)}) collective-permute-start(bf16[2,64,128]{2,1,0:T(8,128)(2,1)S(1)} %get-tuple-element.20), channel_id=1, source_target_pairs={{0,4},{1,5},{2,6},{3,7},{4,0},{5,1},{6,2},{7,3},{8,12},{9,13},{10,... | collective-permute-start | bytes 98312 | tf_op jit(solution)/shard_map/ppermute | solution.py:22
  18.6 2.3 %collective-permute-done.5 = bf16[2,64,128]{2,1,0:T(8,128)(2,1)S(1)} collective-permute-done((bf16[2,64,128]{2,1,0:T(8,128)(2,1)S(1)}, bf16[2,64,128]{2,1,0:T(8,128)(2,1)S(1)}, u32[]{:S(2)}, u32[]{:S(2)}) %collective-permute-start.5) | collective-permute-done | bytes 32800 | tf_op jit(solution)/shard_map/ppermute | solution.py:22
  20.9 2.7 %collective-permute-start.6 = (bf16[2,32,128]{2,1,0:T(8,128)(2,1)S(1)}, bf16[2,32,128]{2,1,0:T(8,128)(2,1)S(1)}, u32[]{:S(2)}, u32[]{:S(2)}) collective-permute-start(bf16[2,32,128]{2,1,0:T(8,128)(2,1)S(1)} %slice.20), channel_id=1, source_target_pairs={{0,8},{1,9},{2,10},{3,11},{4,12},{5,13},{6,14},{7,15},{8,0},{9,1},... | collective-permute-start | bytes 49160 | tf_op jit(solution)/shard_map/ppermute | solution.py:22
  23.6 2.0 %collective-permute-done.6 = bf16[2,32,128]{2,1,0:T(8,128)(2,1)S(1)} collective-permute-done((bf16[2,32,128]{2,1,0:T(8,128)(2,1)S(1)}, bf16[2,32,128]{2,1,0:T(8,128)(2,1)S(1)}, u32[]{:S(2)}, u32[]{:S(2)}) %collective-permute-start.6) | collective-permute-done | bytes 16416 | tf_op jit(solution)/shard_map/ppermute | solution.py:22
  25.6 0.6 %fusion = f32[2,128,32]{1,2,0:T(8,128)} fusion(f32[2,64,128]{2,1,0:T(8,128)S(1)} %convert_add_fusion, bf16[2,32,128]{2,1,0:T(8,128)(2,1)S(1)} %collective-permute-done.6), kind=kLoop, calls=%fused_computation.5 | loop fusion | flops 16384 | bytes 81920 | tf_op jit(solution)/shard_map/transpose | solution.py:244
  (6 shorter events, 0.1 us)
Async XLA Ops:
  0.0 5.6 %copy-start.3 = (f32[4,8]{1,0:T(4,128)S(1)}, f32[4,8]{1,0:T(4,128)}, u32[]{:S(2)}) copy-start(f32[4,8]{1,0:T(4,128)} %noise.1) | copy-start | bytes 388
  0.0 15.8 %collective-permute-start.4 = (bf16[2,1024,128]{2,1,0:T(8,128)(2,1)}, bf16[2,1024,128]{2,1,0:T(8,128)(2,1)S(1)}, u32[]{:S(2)}, u32[]{:S(2)}) collective-permute-start(bf16[2,1024,128]{2,1,0:T(8,128)(2,1)} %green.3), channel_id=1, source_target_pairs={{0,16},{16,0},{1,17},{17,1},{2,18},{18,2},{3,19},{19,3},{4,20},{20... | collective-permute-start | bytes 1572872 | tf_op jit(solution)/shard_map/ppermute | solution.py:27
  3.0 2.6 %copy-start.4 = (s32[128]{0:T(128)S(1)}, s32[128]{0:T(128)}, u32[]{:S(2)}) copy-start(s32[128]{0:T(128)} %param.9) | copy-start | bytes 1540
  3.0 5.0 %collective-permute-start = (bf16[2,32,128]{2,1,0:T(8,128)(2,1)}, bf16[2,32,128]{2,1,0:T(8,128)(2,1)S(1)}, u32[]{:S(2)}, u32[]{:S(2)}) collective-permute-start(bf16[2,32,128]{2,1,0:T(8,128)(2,1)} %bitcast.15), channel_id=1, source_target_pairs={{0,8},{1,9},{2,10},{3,11},{4,12},{5,13},{6,14},{7,15},{8,0},{9,1},... | collective-permute-start | bytes 49160 | tf_op jit(solution)/shard_map/ppermute | solution.py:22
  5.6 1.0 %copy-start = (bf16[2,1024,128]{2,1,0:T(8,128)(2,1)S(1)}, bf16[2,1024,128]{2,1,0:T(8,128)(2,1)}, u32[]{:S(2)}) copy-start(bf16[2,1024,128]{2,1,0:T(8,128)(2,1)} %green.3) | copy-start | bytes 1572868
  6.6 0.7 %copy-start.2 = (bf16[2,128,32]{1,2,0:T(8,128)(2,1)S(1)}, bf16[2,128,32]{1,2,0:T(8,128)(2,1)}, u32[]{:S(2)}) copy-start(bf16[2,128,32]{1,2,0:T(8,128)(2,1)} %param.6) | copy-start | bytes 49156
  7.3 5.6 %copy-start.1 = (bf16[2,1024,128]{2,1,0:T(8,128)(2,1)S(1)}, bf16[2,1024,128]{2,1,0:T(8,128)(2,1)}, u32[]{:S(2)}) copy-start(bf16[2,1024,128]{2,1,0:T(8,128)(2,1)} %green.3) | copy-start | bytes 1572868
  8.0 4.3 %collective-permute-start.1 = (bf16[2,2,64,128]{3,2,1,0:T(8,128)(2,1)S(1)}, bf16[2,2,64,128]{3,2,1,0:T(8,128)(2,1)S(1)}, u32[]{:S(2)}, u32[]{:S(2)}) collective-permute-start(bf16[2,2,64,128]{3,2,1,0:T(8,128)(2,1)S(1)} %pad_maximum_fusion), channel_id=1, source_target_pairs={{0,4},{1,5},{2,6},{3,7},{4,0},{5,1},{6,2},{7,3},{8,12},{9,13},{10,... | collective-permute-start | bytes 196616 | tf_op jit(solution)/shard_map/ppermute | solution.py:22
  9.6 3.3 %collective-permute-start.2 = (bf16[2,64,128]{2,1,0:T(8,128)(2,1)S(1)}, bf16[2,64,128]{2,1,0:T(8,128)(2,1)S(1)}, u32[]{:S(2)}, u32[]{:S(2)}) collective-permute-start(bf16[2,64,128]{2,1,0:T(8,128)(2,1)S(1)} %get-tuple-element.16), channel_id=1, source_target_pairs={{0,1},{1,0},{2,3},{3,2},{4,8},{5,9},{6,10},{7,11},{8,4},{9,5},{10,... | collective-permute-start | bytes 98312 | tf_op jit(solution)/shard_map/ppermute | solution.py:36
  12.3 0.7 %copy-start.5 = (s32[4096]{0:T(1024)S(1)}, s32[4096]{0:T(1024)}, u32[]{:S(2)}) copy-start(s32[4096]{0:T(1024)} %param.11) | copy-start | bytes 49156
  12.3 0.7 %copy-start.6 = (f32[16]{0:T(128)S(1)}, f32[16]{0:T(128)}, u32[]{:S(2)}) copy-start(f32[16]{0:T(128)} %kappa.1) | copy-start | bytes 196
  12.3 4.3 %collective-permute-start.3 = (bf16[4,2,32,128]{3,2,1,0:T(8,128)(2,1)S(1)}, bf16[4,2,32,128]{3,2,1,0:T(8,128)(2,1)S(1)}, u32[]{:S(2)}, u32[]{:S(2)}) collective-permute-start(bf16[4,2,32,128]{3,2,1,0:T(8,128)(2,1)S(1)} %multiply_convert_fusion.vector), channel_id=1, source_target_pairs={{0,16},{16,0},{1,17},{17,1},{2,18},{18,2},{3,19},{19,3},{4,20},{20... | collective-permute-start | bytes 196616 | tf_op jit(solution)/shard_map/ppermute | solution.py:27
  16.9 4.0 %collective-permute-start.5 = (bf16[2,64,128]{2,1,0:T(8,128)(2,1)S(1)}, bf16[2,64,128]{2,1,0:T(8,128)(2,1)S(1)}, u32[]{:S(2)}, u32[]{:S(2)}) collective-permute-start(bf16[2,64,128]{2,1,0:T(8,128)(2,1)S(1)} %get-tuple-element.20), channel_id=1, source_target_pairs={{0,4},{1,5},{2,6},{3,7},{4,0},{5,1},{6,2},{7,3},{8,12},{9,13},{10,... | collective-permute-start | bytes 98312 | tf_op jit(solution)/shard_map/ppermute | solution.py:22
  20.9 4.7 %collective-permute-start.6 = (bf16[2,32,128]{2,1,0:T(8,128)(2,1)S(1)}, bf16[2,32,128]{2,1,0:T(8,128)(2,1)S(1)}, u32[]{:S(2)}, u32[]{:S(2)}) collective-permute-start(bf16[2,32,128]{2,1,0:T(8,128)(2,1)S(1)} %slice.20), channel_id=1, source_target_pairs={{0,8},{1,9},{2,10},{3,11},{4,12},{5,13},{6,14},{7,15},{8,0},{9,1},... | collective-permute-start | bytes 49160 | tf_op jit(solution)/shard_map/ppermute | solution.py:22

commit v6 on v5

--- a/solution.py
+++ b/solution.py
@@ -10,6 +10,8 @@
 SPLIT = 4
 DIP = 32
 LANES = 128
+ROUTES = ((1, 3, 2, 0), (2, 1, 0, 3), (3, 0, 1, 2), (0, 2, 3, 1))
+PLACE = (0, 2, 1, 3)
 REACH = 2 * DIP
 F32 = jnp.float32
 BF16 = jnp.bfloat16
@@ -33,6 +35,14 @@
         part = i // nfreq
         outer = part in (0, SPLIT - 1)
         pairs.append((i, i ^ 1 if outer else i + nfreq if part % 2 else i - nfreq))
+    return lax.ppermute(value, axis, pairs)
+
+
+def routed(value, axis, nfreq, route):
+    pairs = []
+    for i in range(lax.axis_size(axis)):
+        part = i // nfreq
+        pairs.append((i, i + (route[part] - part) * nfreq if route[part] != part else i ^ 1))
     return lax.ppermute(value, axis, pairs)
 
 
@@ -150,16 +160,21 @@
     pair[0], pair[1] = gram(swept[...], planes(green, 0, green.shape[1]))
 
 
-def data_kernel(nsens, weight, base, *refs):
-    vectors, pairs, (keep, send) = refs[: nsens - 1], refs[nsens - 1 : 2 * nsens - 2], refs[2 * nsens - 2 :]
+def data_kernel(nfreq, nsens, weight, base, *refs):
+    vectors, pairs, (keep, *sends, total) = refs[: nsens - 1], refs[nsens - 1 : 2 * nsens - 2], refs[2 * nsens - 2 :]
+    part = lax.div(lax.axis_index("par"), nfreq)
     data = base[...]
     for v, p in zip(vectors, pairs):
         data = data + applied(v[...], p[0], p[1])
-    data = weight[...] * data
-    half = data.shape[0] // 4
+    total[...] = weight[...] * data
+    half = data.shape[0] // 2
+    rows = half // SPLIT
     for k in range(2):
-        keep[k] = data[2 * k * half : (2 * k + 1) * half]
-        send[k] = data[(2 * k + 1) * half : (2 * k + 2) * half].astype(BF16)
+        keep[k] = total[k * half : k * half + rows]
+    for send, route in zip(sends, ROUTES):
+        place = sum(jnp.where(part == p, PLACE[p ^ q], 0) for p, q in enumerate(route))
+        for k in range(2):
+            send[k] = total[pl.ds(pl.multiple_of(k * half + place * rows, rows), rows), :].astype(BF16)
 
 
 def shards(probes, green_blocks, noise_table, station_class, kappa_table, coeff_index):
@@ -228,20 +243,26 @@
         )(swept, g)
         for g in greens
     ]
-    keep, send = pl.pallas_call(
-        functools.partial(data_kernel, nsens),
+    keep, *sends = pl.pallas_call(
+        functools.partial(data_kernel, nfreq, nsens),
         out_shape=[
-            jax.ShapeDtypeStruct((2, rows // 2, sensors), F32),
-            jax.ShapeDtypeStruct((2, rows // 2, sensors), BF16),
+            jax.ShapeDtypeStruct((2, rows_dev, sensors), dtype) for dtype in [F32] + [BF16] * len(ROUTES)
         ],
         in_specs=[vmem] * (2 * nsens),
-        out_specs=[vmem] * 2,
+        out_specs=[vmem] * (1 + len(ROUTES)),
+        scratch_shapes=[pltpu.VMEM((2 * rows, sensors), F32)],
         compiler_params=PARAMS,
         name="data",
     )(weight, base, *rest, *pairs)
-    near = keep + swapped(send, "par", nfreq).astype(F32)
-    far = swapped(near[:, rows_dev:].astype(BF16), "par", 2 * nfreq)
-    return jnp.transpose(near[:, :rows_dev] + far.astype(F32), (0, 2, 1))
+    part = lax.axis_index("par") // nfreq
+    for route, send in zip(ROUTES, sends):
+        share = routed(send, "par", nfreq, route).astype(F32)
+        keep = lax.optimization_barrier(keep)
+        for p in range(SPLIT):
+            if route[p] == p:
+                share = jnp.where(part == p, 0.0, share)
+        keep = keep + share
+    return jnp.transpose(keep, (0, 2, 1))
 
 
 def solution(mesh):

time: 26.5 us -> 24.4 us (0.921)
  waiting for transfers between devices: 8.52 us -> 6.69 us
  starting transfers between devices: 12.2 us -> 11.9 us
    ppermute x4 -> x2, starting transfers between devices: 8.66 us -> 4.23 us  [swapped(): lax.ppermute(value, axis, [(i, i ^ mask) for i in range(lax.axis_size(axi...]
    ppermute x4 -> x2, waiting for transfers between devices: 6.94 us -> 2.69 us  [swapped(): lax.ppermute(value, axis, [(i, i ^ mask) for i in range(lax.axis_size(axi...]
    ppermute x0 -> x4, starting transfers between devices: none -> 4.11 us  [routed(): return lax.ppermute(value, axis, pairs)]
    ppermute x0 -> x4, waiting for transfers between devices: none -> 2.42 us  [routed(): return lax.ppermute(value, axis, pairs)]
  transfers between devices with their start and end apart: 7 -> 9, of which waited for: 5 -> 6; matrix products, arithmetic and copies ran while one was open for 0% -> 0% of each run, Pallas kernels for 10% -> 11%
where the time goes in v6:
time: 24.4 us; the launch traced here: 24.1 us
  starting transfers between devices  11.9 us (49%)
  waiting for transfers between devices  6.69 us (27%)
  Pallas kernels  2.88 us (12%)
  local copies, waits for them, and re-layouts  1.89 us (8%)
  other arithmetic  0.67 us (3%)
    ppermute x2, starting transfers between devices, swapped(): lax.ppermute(value, axis, [(i, i ^ mask) for i in range(lax.axis_size(axi...  4.23 us
    ppermute x4, starting transfers between devices, routed(): return lax.ppermute(value, axis, pairs)  4.11 us
    ppermute x2, starting transfers between devices, turned(): lax.ppermute(value, axis, [(i, (i + step) % size) for i in range(size)])  3.54 us
    ppermute x2, waiting for transfers between devices, swapped(): lax.ppermute(value, axis, [(i, i ^ mask) for i in range(lax.axis_size(axi...  2.69 us
    ppermute x4, waiting for transfers between devices, routed(): return lax.ppermute(value, axis, pairs)  2.42 us
    unnamed x14, local copies, waits for them, and re-layouts  1.88 us
    pallas_call x1, Pallas kernels, shards(): pl.pallas_call(functools.partial(own_kernel, nfreq, kappa_table.shape[0])...  1.73 us
    ppermute x2, waiting for transfers between devices, turned(): lax.ppermute(value, axis, [(i, (i + step) % size) for i in range(size)])  1.58 us
  transfers between devices with their start and end apart: 9, of which 6 were waited for; matrix products, arithmetic and copies ran while one was open for 0% of the time, Pallas kernels for 11%

profile of v6, /device:TPU:0, one launch (start us, length us, event | category | flops | bytes accessed | tf_op | source)
XLA Modules:
  0.0 24.1 jit_solution(11923579227807826190)
XLA Ops:
  0.0 0.0 copy-start.3
  0.0 3.0 %collective-permute-start.4 = (bf16[2,1024,128]{2,1,0:T(8,128)(2,1)}, bf16[2,1024,128]{2,1,0:T(8,128)(2,1)S(1)}, u32[]{:S(2)}, u32[]{:S(2)}) collective-permute-start(bf16[2,1024,128]{2,1,0:T(8,128)(2,1)} %green.3), channel_id=1, source_target_pairs={{0,16},{16,0},{1,17},{17,1},{2,18},{18,2},{3,19},{19,3},{4,20},{20... | collective-permute-start | bytes 1572872 | tf_op jit(solution)/shard_map/ppermute | solution.py:29
  3.0 2.6 %collective-permute-start = (bf16[2,32,128]{2,1,0:T(8,128)(2,1)}, bf16[2,32,128]{2,1,0:T(8,128)(2,1)S(1)}, u32[]{:S(2)}, u32[]{:S(2)}) collective-permute-start(bf16[2,32,128]{2,1,0:T(8,128)(2,1)} %bitcast.15), channel_id=1, source_target_pairs={{0,8},{1,9},{2,10},{3,11},{4,12},{5,13},{6,14},{7,15},{8,0},{9,1},... | collective-permute-start | bytes 49160 | tf_op jit(solution)/shard_map/ppermute | solution.py:24
  5.6 0.0 copy-done.3
  5.6 0.0 copy-done.4
  5.6 1.0 %copy-done = bf16[2,1024,128]{2,1,0:T(8,128)(2,1)S(1)} copy-done((bf16[2,1024,128]{2,1,0:T(8,128)(2,1)S(1)}, bf16[2,1024,128]{2,1,0:T(8,128)(2,1)}, u32[]{:S(2)}) %copy-start) | copy-done | bytes 524312
  6.6 0.7 %copy-done.2 = bf16[2,128,32]{1,2,0:T(8,128)(2,1)S(1)} copy-done((bf16[2,128,32]{1,2,0:T(8,128)(2,1)S(1)}, bf16[2,128,32]{1,2,0:T(8,128)(2,1)}, u32[]{:S(2)}) %copy-start.2) | copy-done | bytes 16408
  7.3 0.6 %prep.1 = (f32[1,128]{1,0:T(1,128)S(1)}, bf16[2,32,128]{2,1,0:T(8,128)(2,1)S(1)}, bf16[2,64,128]{2,1,0:T(8,128)(2,1)S(1)}, bf16[2,64,128]{2,1,0:T(8,128)(2,1)S(1)}) custom-call(f32[4,8]{1,0:T(4,128)S(1)} %copy-done.3, s32[1,128]{1,0:T(1,128)S(1)} %bitcast.18, bf16[2,32,128]{2,1,0:T(8,128)(2,1)S(1)} %bitcast.16, bf16[2,1024,128]{2,1,0:T(8,128)(2,1)S(1)} %copy-done), custom_call_target="tpu_custom_call" | custom-call | flops 1 | bytes 1 | tf_op jit(solution)/shard_map/prep/pallas_call | solution.py:192
  7.9 0.0 collective-permute-done
  8.0 1.6 %collective-permute-start.1 = (bf16[2,2,64,128]{3,2,1,0:T(8,128)(2,1)S(1)}, bf16[2,2,64,128]{3,2,1,0:T(8,128)(2,1)S(1)}, u32[]{:S(2)}, u32[]{:S(2)}) collective-permute-start(bf16[2,2,64,128]{3,2,1,0:T(8,128)(2,1)S(1)} %pad_maximum_fusion), channel_id=1, source_target_pairs={{0,4},{1,5},{2,6},{3,7},{4,0},{5,1},{6,2},{7,3},{8,12},{9,13},{10,... | collective-permute-start | bytes 196616 | tf_op jit(solution)/shard_map/ppermute | solution.py:24
  9.6 0.0 collective-permute-start.2
  9.6 2.7 %collective-permute-done.1.facing = bf16[2,2,64,128]{3,2,1,0:T(8,128)(2,1)S(1)} collective-permute-done((bf16[2,2,64,128]{3,2,1,0:T(8,128)(2,1)S(1)}, bf16[2,2,64,128]{3,2,1,0:T(8,128)(2,1)S(1)}, u32[]{:S(2)}, u32[]{:S(2)}) %collective-permute-start.1) | collective-permute-done | bytes 65568 | tf_op jit(solution)/shard_map/ppermute | solution.py:24
  12.3 0.0 copy-start.6
  12.3 0.6 %collective-permute-start.3 = (bf16[4,2,32,128]{3,2,1,0:T(8,128)(2,1)S(1)}, bf16[4,2,32,128]{3,2,1,0:T(8,128)(2,1)S(1)}, u32[]{:S(2)}, u32[]{:S(2)}) collective-permute-start(bf16[4,2,32,128]{3,2,1,0:T(8,128)(2,1)S(1)} %multiply_convert_fusion.vector), channel_id=1, source_target_pairs={{0,16},{16,0},{1,17},{17,1},{2,18},{18,2},{3,19},{19,3},{4,20},{20... | collective-permute-start | bytes 196616 | tf_op jit(solution)/shard_map/ppermute | solution.py:29
  12.9 0.0 collective-permute-done.2.other
  12.9 0.0 copy-done.1
  12.9 0.1 copy-done.5
  13.0 0.0 copy-done.6
  13.0 1.7 %own.1 = (bf16[256,1024]{1,0:T(8,128)(2,1)S(1)}, f32[256,128]{1,0:T(8,128)S(1)}) custom-call(f32[16]{0:T(128)S(1)} %copy-done.6, s32[32,128]{1,0:T(8,128)S(1)} %bitcast.19, bf16[4,2,32,128]{3,2,1,0:T(8,128)(2,1)S(1)} %multiply_convert_fusion.vector, bf16[2,1024,128]{2,1,0:T(8,128)(2,1)S(1)} %copy-done.1, ...), custom_call_target="tpu_custom_call" | custom-call | flops 575000000 | bytes 1 | tf_op jit(solution)/shard_map/own/pallas_call | solution.py:216
  14.8 1.0 %collective-permute-done.4.green = bf16[2,1024,128]{2,1,0:T(8,128)(2,1)S(1)} collective-permute-done((bf16[2,1024,128]{2,1,0:T(8,128)(2,1)}, bf16[2,1024,128]{2,1,0:T(8,128)(2,1)S(1)}, u32[]{:S(2)}, u32[]{:S(2)}) %collective-permute-start.4) | collective-permute-done | bytes 524320 | tf_op jit(solution)/shard_map/ppermute | solution.py:29
  15.8 0.3 %cross.1.refs_1_ = bf16[2,128,256]{2,1,0:T(8,128)(2,1)S(1)} custom-call(bf16[256,1024]{1,0:T(8,128)(2,1)S(1)} %get-tuple-element.21.swept, bf16[2,1024,128]{2,1,0:T(8,128)(2,1)S(1)} %collective-permute-done.4.green), custom_call_target="tpu_custom_call" | custom-call | flops 1 | bytes 1 | tf_op jit(solution)/shard_map/cross/pallas_call | solution.py:235
  16.1 0.5 %collective-permute-done.3.refs_0_ = bf16[4,2,32,128]{3,2,1,0:T(8,128)(2,1)S(1)} collective-permute-done((bf16[4,2,32,128]{3,2,1,0:T(8,128)(2,1)S(1)}, bf16[4,2,32,128]{3,2,1,0:T(8,128)(2,1)S(1)}, u32[]{:S(2)}, u32[]{:S(2)}) %collective-permute-start.3) | collective-permute-done | bytes 65568 | tf_op jit(solution)/shard_map/ppermute | solution.py:29
  16.7 0.2 %data.1 = (f32[2,32,128]{2,1,0:T(8,128)S(1)}, bf16[2,32,128]{2,1,0:T(8,128)(2,1)S(1)}, bf16[2,32,128]{2,1,0:T(8,128)(2,1)S(1)}, bf16[2,32,128]{2,1,0:T(8,128)(2,1)S(1)}, bf16[2,32,128]{2,1,0:T(8,128)(2,1)S(1)}) custom-call(f32[1,128]{1,0:T(1,128)S(1)} %get-tuple-element.16.weight, f32[256,128]{1,0:T(8,128)S(1)} %get-tuple-element.20.base, ...), custom_call_target="tpu_custom_call" | custom-call | tf_op jit(solution)/shard_map/data/pallas_call | solution.py:246
  16.9 1.7 %collective-permute-start.5 = (bf16[2,32,128]{2,1,0:T(8,128)(2,1)S(1)}, bf16[2,32,128]{2,1,0:T(8,128)(2,1)S(1)}, u32[]{:S(2)}, u32[]{:S(2)}) collective-permute-start(bf16[2,32,128]{2,1,0:T(8,128)(2,1)S(1)} %get-tuple-element.23), channel_id=1, source_target_pairs={{0,4},{1,5},{2,6},{3,7},{4,12},{5,13},{6,14},{7,15},{8,9},{9,8},{1... | collective-permute-start | bytes 49160 | tf_op jit(solution)/shard_map/ppermute | solution.py:46
  18.6 1.1 %collective-permute-start.6 = (bf16[2,32,128]{2,1,0:T(8,128)(2,1)S(1)}, bf16[2,32,128]{2,1,0:T(8,128)(2,1)S(1)}, u32[]{:S(2)}, u32[]{:S(2)}) collective-permute-start(bf16[2,32,128]{2,1,0:T(8,128)(2,1)S(1)} %get-tuple-element.24), channel_id=1, source_target_pairs={{0,8},{1,9},{2,10},{3,11},{4,5},{5,4},{6,7},{7,6},{8,0},{9,1},{10,... | collective-permute-start | bytes 49160 | tf_op jit(solution)/shard_map/ppermute | solution.py:46
  19.7 1.1 %collective-permute-start.7 = (bf16[2,32,128]{2,1,0:T(8,128)(2,1)S(1)}, bf16[2,32,128]{2,1,0:T(8,128)(2,1)S(1)}, u32[]{:S(2)}, u32[]{:S(2)}) collective-permute-start(bf16[2,32,128]{2,1,0:T(8,128)(2,1)S(1)} %get-tuple-element.25), channel_id=1, source_target_pairs={{0,12},{1,13},{2,14},{3,15},{4,0},{5,1},{6,2},{7,3},{8,4},{9,5},{1... | collective-permute-start | bytes 49160 | tf_op jit(solution)/shard_map/ppermute | solution.py:46
  20.8 0.2 collective-permute-start.8
  21.0 1.5 %collective-permute-done.5 = bf16[2,32,128]{2,1,0:T(8,128)(2,1)S(1)} collective-permute-done((bf16[2,32,128]{2,1,0:T(8,128)(2,1)S(1)}, bf16[2,32,128]{2,1,0:T(8,128)(2,1)S(1)}, u32[]{:S(2)}, u32[]{:S(2)}) %collective-permute-start.5) | collective-permute-done | bytes 16416 | tf_op jit(solution)/shard_map/ppermute | solution.py:46
  22.5 0.7 %collective-permute-done.6 = bf16[2,32,128]{2,1,0:T(8,128)(2,1)S(1)} collective-permute-done((bf16[2,32,128]{2,1,0:T(8,128)(2,1)S(1)}, bf16[2,32,128]{2,1,0:T(8,128)(2,1)S(1)}, u32[]{:S(2)}, u32[]{:S(2)}) %collective-permute-start.6) | collective-permute-done | bytes 16416 | tf_op jit(solution)/shard_map/ppermute | solution.py:46
  23.3 0.2 collective-permute-done.7
  23.5 0.0 collective-permute-done.8
  23.5 0.6 %add_bitcast_fusion = f32[2,128,32]{1,2,0:T(8,128)} fusion(f32[2,32,128]{2,1,0:T(8,128)S(1)} %convert_add_fusion, bf16[2,32,128]{2,1,0:T(8,128)(2,1)S(1)} %collective-permute-done.8, pred[]{:T(512)S(6)} %eq.15), kind=kLoop, calls=%fused_computation.2 | loop fusion | flops 24576 | bytes 81921 | tf_op jit(solution)/shard_map/transpose | solution.py:265
  (11 shorter events, 0.1 us)
Async XLA Ops:
  0.0 5.6 %copy-start.3 = (f32[4,8]{1,0:T(4,128)S(1)}, f32[4,8]{1,0:T(4,128)}, u32[]{:S(2)}) copy-start(f32[4,8]{1,0:T(4,128)} %noise.1) | copy-start | bytes 388
  0.0 15.8 %collective-permute-start.4 = (bf16[2,1024,128]{2,1,0:T(8,128)(2,1)}, bf16[2,1024,128]{2,1,0:T(8,128)(2,1)S(1)}, u32[]{:S(2)}, u32[]{:S(2)}) collective-permute-start(bf16[2,1024,128]{2,1,0:T(8,128)(2,1)} %green.3), channel_id=1, source_target_pairs={{0,16},{16,0},{1,17},{17,1},{2,18},{18,2},{3,19},{19,3},{4,20},{20... | collective-permute-start | bytes 1572872 | tf_op jit(solution)/shard_map/ppermute | solution.py:29
  3.0 2.6 %copy-start.4 = (s32[128]{0:T(128)S(1)}, s32[128]{0:T(128)}, u32[]{:S(2)}) copy-start(s32[128]{0:T(128)} %param.9) | copy-start | bytes 1540
  3.0 5.0 %collective-permute-start = (bf16[2,32,128]{2,1,0:T(8,128)(2,1)}, bf16[2,32,128]{2,1,0:T(8,128)(2,1)S(1)}, u32[]{:S(2)}, u32[]{:S(2)}) collective-permute-start(bf16[2,32,128]{2,1,0:T(8,128)(2,1)} %bitcast.15), channel_id=1, source_target_pairs={{0,8},{1,9},{2,10},{3,11},{4,12},{5,13},{6,14},{7,15},{8,0},{9,1},... | collective-permute-start | bytes 49160 | tf_op jit(solution)/shard_map/ppermute | solution.py:24
  5.6 1.0 %copy-start = (bf16[2,1024,128]{2,1,0:T(8,128)(2,1)S(1)}, bf16[2,1024,128]{2,1,0:T(8,128)(2,1)}, u32[]{:S(2)}) copy-start(bf16[2,1024,128]{2,1,0:T(8,128)(2,1)} %green.3) | copy-start | bytes 1572868
  6.6 0.7 %copy-start.2 = (bf16[2,128,32]{1,2,0:T(8,128)(2,1)S(1)}, bf16[2,128,32]{1,2,0:T(8,128)(2,1)}, u32[]{:S(2)}) copy-start(bf16[2,128,32]{1,2,0:T(8,128)(2,1)} %param.6) | copy-start | bytes 49156
  7.3 5.6 %copy-start.1 = (bf16[2,1024,128]{2,1,0:T(8,128)(2,1)S(1)}, bf16[2,1024,128]{2,1,0:T(8,128)(2,1)}, u32[]{:S(2)}) copy-start(bf16[2,1024,128]{2,1,0:T(8,128)(2,1)} %green.3) | copy-start | bytes 1572868
  8.0 4.3 %collective-permute-start.1 = (bf16[2,2,64,128]{3,2,1,0:T(8,128)(2,1)S(1)}, bf16[2,2,64,128]{3,2,1,0:T(8,128)(2,1)S(1)}, u32[]{:S(2)}, u32[]{:S(2)}) collective-permute-start(bf16[2,2,64,128]{3,2,1,0:T(8,128)(2,1)S(1)} %pad_maximum_fusion), channel_id=1, source_target_pairs={{0,4},{1,5},{2,6},{3,7},{4,0},{5,1},{6,2},{7,3},{8,12},{9,13},{10,... | collective-permute-start | bytes 196616 | tf_op jit(solution)/shard_map/ppermute | solution.py:24
  9.6 3.3 %collective-permute-start.2 = (bf16[2,64,128]{2,1,0:T(8,128)(2,1)S(1)}, bf16[2,64,128]{2,1,0:T(8,128)(2,1)S(1)}, u32[]{:S(2)}, u32[]{:S(2)}) collective-permute-start(bf16[2,64,128]{2,1,0:T(8,128)(2,1)S(1)} %get-tuple-element.19), channel_id=1, source_target_pairs={{0,1},{1,0},{2,3},{3,2},{4,8},{5,9},{6,10},{7,11},{8,4},{9,5},{10,... | collective-permute-start | bytes 98312 | tf_op jit(solution)/shard_map/ppermute | solution.py:38
  12.3 0.7 %copy-start.5 = (s32[4096]{0:T(1024)S(1)}, s32[4096]{0:T(1024)}, u32[]{:S(2)}) copy-start(s32[4096]{0:T(1024)} %param.11) | copy-start | bytes 49156
  12.3 0.7 %copy-start.6 = (f32[16]{0:T(128)S(1)}, f32[16]{0:T(128)}, u32[]{:S(2)}) copy-start(f32[16]{0:T(128)} %kappa.1) | copy-start | bytes 196
  12.3 4.3 %collective-permute-start.3 = (bf16[4,2,32,128]{3,2,1,0:T(8,128)(2,1)S(1)}, bf16[4,2,32,128]{3,2,1,0:T(8,128)(2,1)S(1)}, u32[]{:S(2)}, u32[]{:S(2)}) collective-permute-start(bf16[4,2,32,128]{3,2,1,0:T(8,128)(2,1)S(1)} %multiply_convert_fusion.vector), channel_id=1, source_target_pairs={{0,16},{16,0},{1,17},{17,1},{2,18},{18,2},{3,19},{19,3},{4,20},{20... | collective-permute-start | bytes 196616 | tf_op jit(solution)/shard_map/ppermute | solution.py:29
  16.9 5.6 %collective-permute-start.5 = (bf16[2,32,128]{2,1,0:T(8,128)(2,1)S(1)}, bf16[2,32,128]{2,1,0:T(8,128)(2,1)S(1)}, u32[]{:S(2)}, u32[]{:S(2)}) collective-permute-start(bf16[2,32,128]{2,1,0:T(8,128)(2,1)S(1)} %get-tuple-element.23), channel_id=1, source_target_pairs={{0,4},{1,5},{2,6},{3,7},{4,12},{5,13},{6,14},{7,15},{8,9},{9,8},{1... | collective-permute-start | bytes 49160 | tf_op jit(solution)/shard_map/ppermute | solution.py:46
  18.6 4.6 %collective-permute-start.6 = (bf16[2,32,128]{2,1,0:T(8,128)(2,1)S(1)}, bf16[2,32,128]{2,1,0:T(8,128)(2,1)S(1)}, u32[]{:S(2)}, u32[]{:S(2)}) collective-permute-start(bf16[2,32,128]{2,1,0:T(8,128)(2,1)S(1)} %get-tuple-element.24), channel_id=1, source_target_pairs={{0,8},{1,9},{2,10},{3,11},{4,5},{5,4},{6,7},{7,6},{8,0},{9,1},{10,... | collective-permute-start | bytes 49160 | tf_op jit(solution)/shard_map/ppermute | solution.py:46
  19.7 3.7 %collective-permute-start.7 = (bf16[2,32,128]{2,1,0:T(8,128)(2,1)S(1)}, bf16[2,32,128]{2,1,0:T(8,128)(2,1)S(1)}, u32[]{:S(2)}, u32[]{:S(2)}) collective-permute-start(bf16[2,32,128]{2,1,0:T(8,128)(2,1)S(1)} %get-tuple-element.25), channel_id=1, source_target_pairs={{0,12},{1,13},{2,14},{3,15},{4,0},{5,1},{6,2},{7,3},{8,4},{9,5},{1... | collective-permute-start | bytes 49160 | tf_op jit(solution)/shard_map/ppermute | solution.py:46
  20.8 2.7 %collective-permute-start.8 = (bf16[2,32,128]{2,1,0:T(8,128)(2,1)S(1)}, bf16[2,32,128]{2,1,0:T(8,128)(2,1)S(1)}, u32[]{:S(2)}, u32[]{:S(2)}) collective-permute-start(bf16[2,32,128]{2,1,0:T(8,128)(2,1)S(1)} %get-tuple-element.26), channel_id=1, source_target_pairs={{0,1},{1,0},{2,3},{3,2},{4,8},{5,9},{6,10},{7,11},{8,12},{9,13},{1... | collective-permute-start | bytes 49160 | tf_op jit(solution)/shard_map/ppermute | solution.py:46

commit v7 on v5

--- a/solution.py
+++ b/solution.py
@@ -10,6 +10,8 @@
 SPLIT = 4
 DIP = 32
 LANES = 128
+ROUTES = (((1, 2, 3, 0), (3, 2, 1, 0)), ((-1, -1, 0, -1), (2, -1, -1, -1)), ((3, 0, 1, 2), (1, 3, 0, 2)), ((2, 3, -1, 1), (-1, 0, 3, 1)))
+PLACE = (0, 1, 0, 2)
 REACH = 2 * DIP
 F32 = jnp.float32
 BF16 = jnp.bfloat16
@@ -33,6 +35,14 @@
         part = i // nfreq
         outer = part in (0, SPLIT - 1)
         pairs.append((i, i ^ 1 if outer else i + nfreq if part % 2 else i - nfreq))
+    return lax.ppermute(value, axis, pairs)
+
+
+def routed(value, axis, nfreq, step):
+    pairs = []
+    for i in range(lax.axis_size(axis)):
+        part, to = i // nfreq, step[i % 2][i // nfreq]
+        pairs.append((i, i ^ 1 if to < 0 else i + (to - part) * nfreq))
     return lax.ppermute(value, axis, pairs)
 
 
@@ -82,8 +92,7 @@
     weight[...] = 1.0 / jnp.sqrt(variance)
 
 
-def gram(swept, operator):
-    full = dot(swept, operator)
+def halves(full):
     real = full[:LANES, :LANES] + full[LANES:, LANES:]
     imag = full[:LANES, LANES:] - full[LANES:, :LANES]
     both = jnp.concatenate([real, imag], axis=1)
@@ -96,7 +105,7 @@
     return dot(side, high, ((1,), (1,))) + dot(side, low, ((1,), (1,)))
 
 
-def own_kernel(nfreq, nclass, kappa, coeff, vector, green, facing, other, swept, base, operator, inverse, first, second):
+def own_kernel(nfreq, nclass, kappa, coeff, green, facing, other, swept, operator, inverse, first, second):
     part = lax.div(lax.axis_index("par"), nfreq)
     cells = green.shape[1]
     blocks = cells // LANES
@@ -142,24 +151,40 @@
     for at in range(REACH, REACH + cells, LANES):
         total = operator[at : at + LANES].astype(F32) + dot(hood, second[at : at + LANES + 2 * DIP])
         swept[:, at - REACH : at - REACH + LANES] = jnp.transpose(solved(at, total)).astype(BF16)
-    high, low = gram(swept[...], operator[REACH : REACH + cells])
-    base[...] = applied(vector[...], high, low)
-
-
-def cross_kernel(swept, green, pair):
-    pair[0], pair[1] = gram(swept[...], planes(green, 0, green.shape[1]))
-
-
-def data_kernel(nsens, weight, base, *refs):
-    vectors, pairs, (keep, send) = refs[: nsens - 1], refs[nsens - 1 : 2 * nsens - 2], refs[2 * nsens - 2 :]
-    data = base[...]
-    for v, p in zip(vectors, pairs):
-        data = data + applied(v[...], p[0], p[1])
-    data = weight[...] * data
-    half = data.shape[0] // 4
+
+
+def cross_kernel(swept, *refs):
+    greens, pairs = refs[: len(refs) // 2], refs[len(refs) // 2 :]
+    for green, pair in zip(greens, pairs):
+        pair[0], pair[1] = halves(dot(swept[...], planes(green, 0, green.shape[1])))
+
+
+def data_of(nsens, weight, refs):
+    terms = [applied(v[...], p[0], p[1]) for v, p in zip(refs[:nsens], refs[nsens:])]
+    return weight[...] * sum(terms[1:], terms[0])
+
+
+def keep_kernel(nsens, weight, *refs):
+    data = data_of(nsens, weight, refs[:-1])
+    half = data.shape[0] // 2
     for k in range(2):
-        keep[k] = data[2 * k * half : (2 * k + 1) * half]
-        send[k] = data[(2 * k + 1) * half : (2 * k + 2) * half].astype(BF16)
+        refs[-1][k] = data[k * half : (k + 1) * half]
+
+
+def send_kernel(nfreq, nsens, weight, *refs):
+    refs, (*sends, total) = refs[: 2 * nsens], refs[2 * nsens :]
+    par = lax.axis_index("par")
+    part, odd = lax.div(par, nfreq), lax.rem(par, 2)
+    total[...] = data_of(nsens, weight, refs)
+    half = total.shape[0] // 2
+    rows = half // (SPLIT - 1)
+    for send, step in zip(sends, ROUTES):
+        place = 0
+        for core, route in enumerate(step):
+            for p, q in enumerate(route):
+                place = jnp.where((part == p) & (odd == core), PLACE[p ^ max(q, 0)], place)
+        for k in range(2):
+            send[k] = total[pl.ds(pl.multiple_of(k * half + place * rows, rows), rows), :].astype(BF16)
 
 
 def shards(probes, green_blocks, noise_table, station_class, kappa_table, coeff_index):
@@ -195,17 +220,16 @@
     other = crossed(other, "par", nfreq)
     vectors = jnp.concatenate([mine, got[0].reshape(mine.shape)], axis=0)
     vectors = (weight * vectors.astype(F32)).astype(BF16)
-    rest = [turned(vectors, "sens", k) for k in range(1, nsens)]
+    kept, given = vectors[:1], vectors[1:]
+    given, kept = lax.optimization_barrier((given, kept))
+    rests = [[turned(v, "sens", k) for k in range(1, nsens)] for v in (given, kept)]
     rows = SPLIT * rows_dev
     extent = cells + 2 * REACH
-    swept, base = pl.pallas_call(
+    swept = pl.pallas_call(
         functools.partial(own_kernel, nfreq, kappa_table.shape[0]),
-        out_shape=[
-            jax.ShapeDtypeStruct((2 * sensors, cells), BF16),
-            jax.ShapeDtypeStruct((2 * rows, sensors), F32),
-        ],
-        in_specs=[smem] + [vmem] * 5,
-        out_specs=[vmem] * 2,
+        out_shape=jax.ShapeDtypeStruct((2 * sensors, cells), BF16),
+        in_specs=[smem] + [vmem] * 4,
+        out_specs=vmem,
         scratch_shapes=[
             pltpu.VMEM((extent, 2 * sensors), BF16),
             pltpu.VMEM((extent, LANES), F32),
@@ -215,33 +239,47 @@
         compiler_params=PARAMS,
         cost_estimate=BESIDE,
         name="own",
-    )(kappa_table, coeff_index.reshape(-1, LANES), vectors, green_blocks, got, other)
-    pairs = [
-        pl.pallas_call(
-            cross_kernel,
-            out_shape=jax.ShapeDtypeStruct((2, sensors, 2 * sensors), BF16),
-            in_specs=[vmem] * 2,
-            out_specs=vmem,
-            compiler_params=PARAMS,
-            cost_estimate=PRIOR,
-            name="cross",
-        )(swept, g)
-        for g in greens
-    ]
-    keep, send = pl.pallas_call(
-        functools.partial(data_kernel, nsens),
-        out_shape=[
-            jax.ShapeDtypeStruct((2, rows // 2, sensors), F32),
-            jax.ShapeDtypeStruct((2, rows // 2, sensors), BF16),
-        ],
-        in_specs=[vmem] * (2 * nsens),
-        out_specs=[vmem] * 2,
-        compiler_params=PARAMS,
-        name="data",
-    )(weight, base, *rest, *pairs)
-    near = keep + swapped(send, "par", nfreq).astype(F32)
-    far = swapped(near[:, rows_dev:].astype(BF16), "par", 2 * nfreq)
-    return jnp.transpose(near[:, :rows_dev] + far.astype(F32), (0, 2, 1))
+    )(kappa_table, coeff_index.reshape(-1, LANES), green_blocks, got, other)
+    pairs = pl.pallas_call(
+        cross_kernel,
+        out_shape=[jax.ShapeDtypeStruct((2, sensors, 2 * sensors), BF16)] * nsens,
+        in_specs=[vmem] * (1 + nsens),
+        out_specs=[vmem] * nsens,
+        compiler_params=PARAMS,
+        cost_estimate=PRIOR,
+        name="cross",
+    )(swept, green_blocks, *greens)
+    sends = list(pl.pallas_call(
+        functools.partial(send_kernel, nfreq, nsens),
+        out_shape=[jax.ShapeDtypeStruct((2, rows_dev, sensors), BF16)] * len(ROUTES),
+        in_specs=[vmem] * (1 + 2 * nsens),
+        out_specs=[vmem] * len(ROUTES),
+        scratch_shapes=[pltpu.VMEM((2 * (rows - rows_dev), sensors), F32)],
+        compiler_params=PARAMS,
+        name="send",
+    )(weight, given, *rests[0], *pairs))
+    sends[2], rests[1] = lax.optimization_barrier((sends[2], rests[1]))
+    shares = [routed(send, "par", nfreq, step) for send, step in zip(sends, ROUTES)]
+    shares[0], kept = lax.optimization_barrier((shares[0], kept))
+    keep = pl.pallas_call(
+        functools.partial(keep_kernel, nsens),
+        out_shape=jax.ShapeDtypeStruct((2, rows_dev, sensors), F32),
+        in_specs=[vmem] * (1 + 2 * nsens),
+        out_specs=vmem,
+        compiler_params=PARAMS,
+        cost_estimate=PRIOR,
+        name="keep",
+    )(weight, kept, *rests[1], *pairs)
+    par = lax.axis_index("par")
+    for step, share in zip(ROUTES, shares):
+        share = share.astype(F32)
+        keep = lax.optimization_barrier(keep)
+        for core, route in enumerate(step):
+            for q in range(SPLIT):
+                if q not in route:
+                    share = jnp.where((par // nfreq == q) & (par % 2 == core), 0.0, share)
+        keep = keep + share
+    return jnp.transpose(keep, (0, 2, 1))
 
 
 def solution(mesh):

time: 26.5 us -> 24 us (0.906)
  waiting for transfers between devices: 8.52 us -> 4.46 us
  starting transfers between devices: 12.2 us -> 14 us
    ppermute x0 -> x4, starting transfers between devices: none -> 4.71 us  [routed(): return lax.ppermute(value, axis, pairs)]
    ppermute x4 -> x2, starting transfers between devices: 8.66 us -> 4.23 us  [swapped(): lax.ppermute(value, axis, [(i, i ^ mask) for i in range(lax.axis_size(axi...]
    ppermute x4 -> x2, waiting for transfers between devices: 6.94 us -> 2.69 us  [swapped(): lax.ppermute(value, axis, [(i, i ^ mask) for i in range(lax.axis_size(axi...]
    ppermute x2 -> x3, starting transfers between devices: 3.54 us -> 5.06 us  [turned(): lax.ppermute(value, axis, [(i, (i + step) % size) for i in range(size)])]
    ppermute x0 -> x4, waiting for transfers between devices: none -> 1.39 us  [routed(): return lax.ppermute(value, axis, pairs)]
    ppermute x2 -> x3, waiting for transfers between devices: 1.58 us -> 0.37 us  [turned(): lax.ppermute(value, axis, [(i, (i + step) % size) for i in range(size)])]
    pallas_call x1, Pallas kernels: 1.73 us -> 1.21 us  [shards(): pl.pallas_call(functools.partial(own_kernel, nfreq, kappa_table.shape[0])...]
    pallas_call x2 -> x3, Pallas kernels: 0.54 us -> 0.93 us  [the longest x1 0.45 us: shards(): pl.pallas_call(cross_kernel, out_shape=[jax.ShapeDtypeStruct((2, sensors,...]
  transfers between devices with their start and end apart: 7 -> 10, of which waited for: 5 -> 5; matrix products, arithmetic and copies ran while one was open for 0% -> 0% of each run, Pallas kernels for 10% -> 10%
where the time goes in v7:
time: 24 us; the launch traced here: 23.8 us
  starting transfers between devices  14 us (58%)
  waiting for transfers between devices  4.46 us (19%)
  Pallas kernels  2.73 us (11%)
  local copies, waits for them, and re-layouts  1.79 us (7%)
  other arithmetic  0.68 us (3%)
    ppermute x3, starting transfers between devices, turned(): lax.ppermute(value, axis, [(i, (i + step) % size) for i in range(size)])  5.06 us
    ppermute x4, starting transfers between devices, routed(): return lax.ppermute(value, axis, pairs)  4.71 us
    ppermute x2, starting transfers between devices, swapped(): lax.ppermute(value, axis, [(i, i ^ mask) for i in range(lax.axis_size(axi...  4.23 us
    ppermute x2, waiting for transfers between devices, swapped(): lax.ppermute(value, axis, [(i, i ^ mask) for i in range(lax.axis_size(axi...  2.69 us
    unnamed x14, local copies, waits for them, and re-layouts  1.78 us
    ppermute x4, waiting for transfers between devices, routed(): return lax.ppermute(value, axis, pairs)  1.39 us
    pallas_call x1, Pallas kernels, shards(): pl.pallas_call(functools.partial(own_kernel, nfreq, kappa_table.shape[0])...  1.21 us
    transpose x1, other arithmetic, shards(): return jnp.transpose(keep, (0, 2, 1))  0.63 us
  transfers between devices with their start and end apart: 10, of which 5 were waited for; matrix products, arithmetic and copies ran while one was open for 0% of the time, Pallas kernels for 10%

profile of v7, /device:TPU:0, one launch (start us, length us, event | category | flops | bytes accessed | tf_op | source)
XLA Modules:
  0.0 23.8 jit_solution(6419613892532049189)
XLA Ops:
  0.0 3.0 %collective-permute-start.4 = (bf16[2,1024,128]{2,1,0:T(8,128)(2,1)}, bf16[2,1024,128]{2,1,0:T(8,128)(2,1)S(1)}, u32[]{:S(2)}, u32[]{:S(2)}) collective-permute-start(bf16[2,1024,128]{2,1,0:T(8,128)(2,1)} %refs_0_.1), channel_id=1, source_target_pairs={{0,16},{16,0},{1,17},{17,1},{2,18},{18,2},{3,19},{19,3},{4,20},{20... | collective-permute-start | bytes 1572872 | tf_op jit(solution)/shard_map/ppermute | solution.py:29
  3.0 2.6 %collective-permute-start = (bf16[2,32,128]{2,1,0:T(8,128)(2,1)}, bf16[2,32,128]{2,1,0:T(8,128)(2,1)S(1)}, u32[]{:S(2)}, u32[]{:S(2)}) collective-permute-start(bf16[2,32,128]{2,1,0:T(8,128)(2,1)} %bitcast.15), channel_id=1, source_target_pairs={{0,8},{1,9},{2,10},{3,11},{4,12},{5,13},{6,14},{7,15},{8,0},{9,1},... | collective-permute-start | bytes 49160 | tf_op jit(solution)/shard_map/ppermute | solution.py:24
  5.6 0.0 copy-done.4
  5.6 1.0 %copy-done = bf16[2,1024,128]{2,1,0:T(8,128)(2,1)S(1)} copy-done((bf16[2,1024,128]{2,1,0:T(8,128)(2,1)S(1)}, bf16[2,1024,128]{2,1,0:T(8,128)(2,1)}, u32[]{:S(2)}) %copy-start) | copy-done | bytes 524312
  6.6 0.7 %copy-done.2 = bf16[2,128,32]{1,2,0:T(8,128)(2,1)S(1)} copy-done((bf16[2,128,32]{1,2,0:T(8,128)(2,1)S(1)}, bf16[2,128,32]{1,2,0:T(8,128)(2,1)}, u32[]{:S(2)}) %copy-start.2) | copy-done | bytes 16408
  7.3 0.6 %prep.1 = (f32[1,128]{1,0:T(1,128)S(1)}, bf16[2,32,128]{2,1,0:T(8,128)(2,1)S(1)}, bf16[2,64,128]{2,1,0:T(8,128)(2,1)S(1)}, bf16[2,64,128]{2,1,0:T(8,128)(2,1)S(1)}) custom-call(f32[4,8]{1,0:T(4,128)S(1)} %copy-done.3, s32[1,128]{1,0:T(1,128)S(1)} %bitcast.18, bf16[2,32,128]{2,1,0:T(8,128)(2,1)S(1)} %bitcast.16, bf16[2,1024,128]{2,1,0:T(8,128)(2,1)S(1)} %copy-done), custom_call_target="tpu_custom_call" | custom-call | flops 1 | bytes 1 | tf_op jit(solution)/shard_map/prep/pallas_call | solution.py:202
  7.9 0.0 collective-permute-done
  8.0 1.6 %collective-permute-start.1 = (bf16[2,2,64,128]{3,2,1,0:T(8,128)(2,1)S(1)}, bf16[2,2,64,128]{3,2,1,0:T(8,128)(2,1)S(1)}, u32[]{:S(2)}, u32[]{:S(2)}) collective-permute-start(bf16[2,2,64,128]{3,2,1,0:T(8,128)(2,1)S(1)} %pad_maximum_fusion), channel_id=1, source_target_pairs={{0,4},{1,5},{2,6},{3,7},{4,0},{5,1},{6,2},{7,3},{8,12},{9,13},{10,... | collective-permute-start | bytes 196616 | tf_op jit(solution)/shard_map/ppermute | solution.py:24
  9.6 0.0 collective-permute-start.3
  9.6 2.7 %collective-permute-done.1.facing = bf16[2,2,64,128]{3,2,1,0:T(8,128)(2,1)S(1)} collective-permute-done((bf16[2,2,64,128]{3,2,1,0:T(8,128)(2,1)S(1)}, bf16[2,2,64,128]{3,2,1,0:T(8,128)(2,1)S(1)}, u32[]{:S(2)}, u32[]{:S(2)}) %collective-permute-start.1) | collective-permute-done | bytes 65568 | tf_op jit(solution)/shard_map/ppermute | solution.py:24
  12.3 0.0 copy-start.5
  12.4 0.0 copy-start.6
  12.4 0.6 %collective-permute-start.2 = (bf16[3,2,32,128]{3,2,1,0:T(8,128)(2,1)S(1)}, bf16[3,2,32,128]{3,2,1,0:T(8,128)(2,1)S(1)}, u32[]{:S(2)}, u32[]{:S(2)}) collective-permute-start(bf16[3,2,32,128]{3,2,1,0:T(8,128)(2,1)S(1)} %slice.13.refs_0_), channel_id=1, source_target_pairs={{0,16},{16,0},{1,17},{17,1},{2,18},{18,2},{3,19},{19,3},{4,20},{20... | collective-permute-start | bytes 147464 | tf_op jit(solution)/shard_map/ppermute | solution.py:29
  12.9 1.5 %collective-permute-start.6 = (bf16[1,2,32,128]{3,2,1,0:T(8,128)(2,1)S(1)}, bf16[1,2,32,128]{3,2,1,0:T(8,128)(2,1)S(1)}, u32[]{:S(2)}, u32[]{:S(2)}) collective-permute-start(bf16[1,2,32,128]{3,2,1,0:T(8,128)(2,1)S(1)} %slice.14.refs_0_), channel_id=1, source_target_pairs={{0,16},{16,0},{1,17},{17,1},{2,18},{18,2},{3,19},{19,3},{4,20},{20... | collective-permute-start | bytes 49160 | tf_op jit(solution)/shard_map/ppermute | solution.py:29
  14.5 0.0 collective-permute-done.3.other
  14.5 0.0 copy-done.1
  14.5 1.2 %own.1.swept = bf16[256,1024]{1,0:T(8,128)(2,1)S(1)} custom-call(f32[16]{0:T(128)S(1)} %copy-done.6, s32[32,128]{1,0:T(8,128)S(1)} %bitcast.19, bf16[2,1024,128]{2,1,0:T(8,128)(2,1)S(1)} %copy-done.1, bf16[2,2,64,128]{3,2,1,0:T(8,128)(2,1)S(1)} %collective-permute-done.1.facing, bf16[2,64,128]{2,1,0:T(8,128)(2,1)S(1)} %collective-permute-done.3.other), custom_call_target="tpu_custom_call" | custom-call | flops 575000000 | bytes 1 | tf_op jit(solution)/shard_map/own/pallas_call | solution.py:228
  15.7 0.1 collective-permute-done.4.refs_1_
  15.8 0.4 %cross.1 = (bf16[2,128,256]{2,1,0:T(8,128)(2,1)S(1)}, bf16[2,128,256]{2,1,0:T(8,128)(2,1)S(1)}) custom-call(bf16[256,1024]{1,0:T(8,128)(2,1)S(1)} %own.1.swept, bf16[2,1024,128]{2,1,0:T(8,128)(2,1)S(1)} %copy-done.1, bf16[2,1024,128]{2,1,0:T(8,128)(2,1)S(1)} %collective-permute-done.4.refs_1_), custom_call_target="tpu_custom_call" | custom-call | flops 1 | bytes 1 | tf_op jit(solution)/shard_map/cross/pallas_call | solution.py:243
  16.3 0.3 %collective-permute-done.2.refs_1_ = bf16[3,2,32,128]{3,2,1,0:T(8,128)(2,1)S(1)} collective-permute-done((bf16[3,2,32,128]{3,2,1,0:T(8,128)(2,1)S(1)}, bf16[3,2,32,128]{3,2,1,0:T(8,128)(2,1)S(1)}, u32[]{:S(2)}, u32[]{:S(2)}) %collective-permute-start.2) | collective-permute-done | bytes 49184 | tf_op jit(solution)/shard_map/ppermute | solution.py:29
  16.5 0.3 %send.1 = (bf16[2,32,128]{2,1,0:T(8,128)(2,1)S(1)}, bf16[2,32,128]{2,1,0:T(8,128)(2,1)S(1)}, bf16[2,32,128]{2,1,0:T(8,128)(2,1)S(1)}, bf16[2,32,128]{2,1,0:T(8,128)(2,1)S(1)}) custom-call(f32[1,128]{1,0:T(1,128)S(1)} %get-tuple-element.21.weight, bf16[3,2,32,128]{3,2,1,0:T(8,128)(2,1)S(1)} %slice.13.refs_0_, ...), custom_call_target="tpu_custom_call" | custom-call | tf_op jit(solution)/shard_map/send/pallas_call | solution.py:252
  16.8 1.7 %collective-permute-start.5 = (bf16[2,32,128]{2,1,0:T(8,128)(2,1)S(1)}, bf16[2,32,128]{2,1,0:T(8,128)(2,1)S(1)}, u32[]{:S(2)}, u32[]{:S(2)}) collective-permute-start(bf16[2,32,128]{2,1,0:T(8,128)(2,1)S(1)} %get-tuple-element.28), channel_id=1, source_target_pairs={{0,4},{1,13},{2,6},{3,15},{4,8},{5,9},{6,10},{7,11},{8,12},{9,5},{... | collective-permute-start | bytes 49160 | tf_op jit(solution)/shard_map/ppermute | solution.py:46
  18.5 0.0 collective-permute-done.6.refs_1_
  18.5 0.5 %collective-permute-start.7 = (bf16[2,32,128]{2,1,0:T(8,128)(2,1)S(1)}, bf16[2,32,128]{2,1,0:T(8,128)(2,1)S(1)}, u32[]{:S(2)}, u32[]{:S(2)}) collective-permute-start(bf16[2,32,128]{2,1,0:T(8,128)(2,1)S(1)} %get-tuple-element.34), channel_id=1, source_target_pairs={{0,1},{1,9},{2,3},{3,11},{4,5},{5,4},{6,7},{7,6},{8,0},{9,8},{10,2... | collective-permute-start | bytes 49160 | tf_op jit(solution)/shard_map/ppermute | solution.py:46
  19.0 1.7 %collective-permute-start.8 = (bf16[2,32,128]{2,1,0:T(8,128)(2,1)S(1)}, bf16[2,32,128]{2,1,0:T(8,128)(2,1)S(1)}, u32[]{:S(2)}, u32[]{:S(2)}) collective-permute-start(bf16[2,32,128]{2,1,0:T(8,128)(2,1)S(1)} %get-tuple-element.35), channel_id=1, source_target_pairs={{0,12},{1,5},{2,14},{3,7},{4,0},{5,13},{6,2},{7,15},{8,4},{9,1},{1... | collective-permute-start | bytes 49160 | tf_op jit(solution)/shard_map/ppermute | solution.py:46
  20.7 0.8 %collective-permute-start.9 = (bf16[2,32,128]{2,1,0:T(8,128)(2,1)S(1)}, bf16[2,32,128]{2,1,0:T(8,128)(2,1)S(1)}, u32[]{:S(2)}, u32[]{:S(2)}) collective-permute-start(bf16[2,32,128]{2,1,0:T(8,128)(2,1)S(1)} %get-tuple-element.36), channel_id=1, source_target_pairs={{0,8},{1,0},{2,10},{3,2},{4,12},{5,1},{6,14},{7,3},{8,9},{9,13},{1... | collective-permute-start | bytes 49160 | tf_op jit(solution)/shard_map/ppermute | solution.py:46
  21.5 0.9 %collective-permute-done.5 = bf16[2,32,128]{2,1,0:T(8,128)(2,1)S(1)} collective-permute-done((bf16[2,32,128]{2,1,0:T(8,128)(2,1)S(1)}, bf16[2,32,128]{2,1,0:T(8,128)(2,1)S(1)}, u32[]{:S(2)}, u32[]{:S(2)}) %collective-permute-start.5) | collective-permute-done | bytes 16416 | tf_op jit(solution)/shard_map/ppermute | solution.py:46
  22.4 0.2 keep.1
  22.6 0.5 %collective-permute-done.7 = bf16[2,32,128]{2,1,0:T(8,128)(2,1)S(1)} collective-permute-done((bf16[2,32,128]{2,1,0:T(8,128)(2,1)S(1)}, bf16[2,32,128]{2,1,0:T(8,128)(2,1)S(1)}, u32[]{:S(2)}, u32[]{:S(2)}) %collective-permute-start.7) | collective-permute-done | bytes 16416 | tf_op jit(solution)/shard_map/ppermute | solution.py:46
  23.1 0.0 collective-permute-done.8
  23.2 0.0 collective-permute-done.9
  23.2 0.6 %add_bitcast_fusion = f32[2,128,32]{1,2,0:T(8,128)} fusion(f32[2,32,128]{2,1,0:T(8,128)S(1)} %convert_add_fusion, bf16[2,32,128]{2,1,0:T(8,128)(2,1)S(1)} %collective-permute-done.9, pred[]{:T(512)S(6)} %and.58, pred[]{:T(512)S(6)} %and.57), kind=kLoop, calls=%fused_computation.2 | loop fusion | flops 32768 | bytes 81922 | tf_op jit(solution)/shard_map/transpose | solution.py:282
  (16 shorter events, 0.1 us)
Async XLA Ops:
  0.0 5.6 %copy-start.3 = (f32[4,8]{1,0:T(4,128)S(1)}, f32[4,8]{1,0:T(4,128)}, u32[]{:S(2)}) copy-start(f32[4,8]{1,0:T(4,128)} %noise.1) | copy-start | bytes 388
  0.0 15.8 %collective-permute-start.4 = (bf16[2,1024,128]{2,1,0:T(8,128)(2,1)}, bf16[2,1024,128]{2,1,0:T(8,128)(2,1)S(1)}, u32[]{:S(2)}, u32[]{:S(2)}) collective-permute-start(bf16[2,1024,128]{2,1,0:T(8,128)(2,1)} %refs_0_.1), channel_id=1, source_target_pairs={{0,16},{16,0},{1,17},{17,1},{2,18},{18,2},{3,19},{19,3},{4,20},{20... | collective-permute-start | bytes 1572872 | tf_op jit(solution)/shard_map/ppermute | solution.py:29
  3.0 2.6 %copy-start.4 = (s32[128]{0:T(128)S(1)}, s32[128]{0:T(128)}, u32[]{:S(2)}) copy-start(s32[128]{0:T(128)} %param.9) | copy-start | bytes 1540
  3.0 5.0 %collective-permute-start = (bf16[2,32,128]{2,1,0:T(8,128)(2,1)}, bf16[2,32,128]{2,1,0:T(8,128)(2,1)S(1)}, u32[]{:S(2)}, u32[]{:S(2)}) collective-permute-start(bf16[2,32,128]{2,1,0:T(8,128)(2,1)} %bitcast.15), channel_id=1, source_target_pairs={{0,8},{1,9},{2,10},{3,11},{4,12},{5,13},{6,14},{7,15},{8,0},{9,1},... | collective-permute-start | bytes 49160 | tf_op jit(solution)/shard_map/ppermute | solution.py:24
  5.6 1.0 %copy-start = (bf16[2,1024,128]{2,1,0:T(8,128)(2,1)S(1)}, bf16[2,1024,128]{2,1,0:T(8,128)(2,1)}, u32[]{:S(2)}) copy-start(bf16[2,1024,128]{2,1,0:T(8,128)(2,1)} %refs_0_.1) | copy-start | bytes 1572868
  6.6 0.7 %copy-start.2 = (bf16[2,128,32]{1,2,0:T(8,128)(2,1)S(1)}, bf16[2,128,32]{1,2,0:T(8,128)(2,1)}, u32[]{:S(2)}) copy-start(bf16[2,128,32]{1,2,0:T(8,128)(2,1)} %param.6) | copy-start | bytes 49156
  7.3 7.1 %copy-start.1 = (bf16[2,1024,128]{2,1,0:T(8,128)(2,1)S(1)}, bf16[2,1024,128]{2,1,0:T(8,128)(2,1)}, u32[]{:S(2)}) copy-start(bf16[2,1024,128]{2,1,0:T(8,128)(2,1)} %refs_0_.1) | copy-start | bytes 1572868
  8.0 4.3 %collective-permute-start.1 = (bf16[2,2,64,128]{3,2,1,0:T(8,128)(2,1)S(1)}, bf16[2,2,64,128]{3,2,1,0:T(8,128)(2,1)S(1)}, u32[]{:S(2)}, u32[]{:S(2)}) collective-permute-start(bf16[2,2,64,128]{3,2,1,0:T(8,128)(2,1)S(1)} %pad_maximum_fusion), channel_id=1, source_target_pairs={{0,4},{1,5},{2,6},{3,7},{4,0},{5,1},{6,2},{7,3},{8,12},{9,13},{10,... | collective-permute-start | bytes 196616 | tf_op jit(solution)/shard_map/ppermute | solution.py:24
  9.6 4.9 %collective-permute-start.3 = (bf16[2,64,128]{2,1,0:T(8,128)(2,1)S(1)}, bf16[2,64,128]{2,1,0:T(8,128)(2,1)S(1)}, u32[]{:S(2)}, u32[]{:S(2)}) collective-permute-start(bf16[2,64,128]{2,1,0:T(8,128)(2,1)S(1)} %get-tuple-element.25), channel_id=1, source_target_pairs={{0,1},{1,0},{2,3},{3,2},{4,8},{5,9},{6,10},{7,11},{8,4},{9,5},{10,... | collective-permute-start | bytes 98312 | tf_op jit(solution)/shard_map/ppermute | solution.py:38
  12.3 2.1 %copy-start.5 = (s32[4096]{0:T(1024)S(1)}, s32[4096]{0:T(1024)}, u32[]{:S(2)}) copy-start(s32[4096]{0:T(1024)} %param.11) | copy-start | bytes 49156
  12.4 2.1 %copy-start.6 = (f32[16]{0:T(128)S(1)}, f32[16]{0:T(128)}, u32[]{:S(2)}) copy-start(f32[16]{0:T(128)} %kappa.1) | copy-start | bytes 196
  12.4 4.2 %collective-permute-start.2 = (bf16[3,2,32,128]{3,2,1,0:T(8,128)(2,1)S(1)}, bf16[3,2,32,128]{3,2,1,0:T(8,128)(2,1)S(1)}, u32[]{:S(2)}, u32[]{:S(2)}) collective-permute-start(bf16[3,2,32,128]{3,2,1,0:T(8,128)(2,1)S(1)} %slice.13.refs_0_), channel_id=1, source_target_pairs={{0,16},{16,0},{1,17},{17,1},{2,18},{18,2},{3,19},{19,3},{4,20},{20... | collective-permute-start | bytes 147464 | tf_op jit(solution)/shard_map/ppermute | solution.py:29
  12.9 5.5 %collective-permute-start.6 = (bf16[1,2,32,128]{3,2,1,0:T(8,128)(2,1)S(1)}, bf16[1,2,32,128]{3,2,1,0:T(8,128)(2,1)S(1)}, u32[]{:S(2)}, u32[]{:S(2)}) collective-permute-start(bf16[1,2,32,128]{3,2,1,0:T(8,128)(2,1)S(1)} %slice.14.refs_0_), channel_id=1, source_target_pairs={{0,16},{16,0},{1,17},{17,1},{2,18},{18,2},{3,19},{19,3},{4,20},{20... | collective-permute-start | bytes 49160 | tf_op jit(solution)/shard_map/ppermute | solution.py:29
  16.8 5.6 %collective-permute-start.5 = (bf16[2,32,128]{2,1,0:T(8,128)(2,1)S(1)}, bf16[2,32,128]{2,1,0:T(8,128)(2,1)S(1)}, u32[]{:S(2)}, u32[]{:S(2)}) collective-permute-start(bf16[2,32,128]{2,1,0:T(8,128)(2,1)S(1)} %get-tuple-element.28), channel_id=1, source_target_pairs={{0,4},{1,13},{2,6},{3,15},{4,8},{5,9},{6,10},{7,11},{8,12},{9,5},{... | collective-permute-start | bytes 49160 | tf_op jit(solution)/shard_map/ppermute | solution.py:46
  18.5 4.7 %collective-permute-start.7 = (bf16[2,32,128]{2,1,0:T(8,128)(2,1)S(1)}, bf16[2,32,128]{2,1,0:T(8,128)(2,1)S(1)}, u32[]{:S(2)}, u32[]{:S(2)}) collective-permute-start(bf16[2,32,128]{2,1,0:T(8,128)(2,1)S(1)} %get-tuple-element.34), channel_id=1, source_target_pairs={{0,1},{1,9},{2,3},{3,11},{4,5},{5,4},{6,7},{7,6},{8,0},{9,8},{10,2... | collective-permute-start | bytes 49160 | tf_op jit(solution)/shard_map/ppermute | solution.py:46
  19.0 4.1 %collective-permute-start.8 = (bf16[2,32,128]{2,1,0:T(8,128)(2,1)S(1)}, bf16[2,32,128]{2,1,0:T(8,128)(2,1)S(1)}, u32[]{:S(2)}, u32[]{:S(2)}) collective-permute-start(bf16[2,32,128]{2,1,0:T(8,128)(2,1)S(1)} %get-tuple-element.35), channel_id=1, source_target_pairs={{0,12},{1,5},{2,14},{3,7},{4,0},{5,13},{6,2},{7,15},{8,4},{9,1},{1... | collective-permute-start | bytes 49160 | tf_op jit(solution)/shard_map/ppermute | solution.py:46
  20.7 2.5 %collective-permute-start.9 = (bf16[2,32,128]{2,1,0:T(8,128)(2,1)S(1)}, bf16[2,32,128]{2,1,0:T(8,128)(2,1)S(1)}, u32[]{:S(2)}, u32[]{:S(2)}) collective-permute-start(bf16[2,32,128]{2,1,0:T(8,128)(2,1)S(1)} %get-tuple-element.36), channel_id=1, source_target_pairs={{0,8},{1,0},{2,10},{3,2},{4,12},{5,1},{6,14},{7,3},{8,9},{9,13},{1... | collective-permute-start | bytes 49160 | tf_op jit(solution)/shard_map/ppermute | solution.py:46

commit v8 on v7

--- a/solution.py
+++ b/solution.py
@@ -50,10 +50,10 @@
     return lax.dot_general(a, b, (form, ((), ())), preferred_element_type=F32)
 
 
-def chosen(table, index, count, place):
+def chosen(table, index):
     value = jnp.zeros(index.shape, F32)
-    for k in range(count):
-        value = jnp.where(index == k, place(table, k), value)
+    for k in range(table.shape[1]):
+        value = jnp.where(index == k, jnp.broadcast_to(table[:, k : k + 1], index.shape), value)
     return value
 
 
@@ -88,24 +88,21 @@
     held[...] = vector[...]
     facing[...] = green[:, pl.ds(last, REACH)]
     other[...] = green[:, pl.ds(first, REACH)]
-    variance = chosen(noise, station[...], noise.shape[1], lambda t, k: t[freq, k])
+    variance = chosen(noise[pl.ds(freq, 1), :], station[...])
     weight[...] = 1.0 / jnp.sqrt(variance)
 
 
 def halves(full):
     real = full[:LANES, :LANES] + full[LANES:, LANES:]
     imag = full[:LANES, LANES:] - full[LANES:, :LANES]
-    both = jnp.concatenate([real, imag], axis=1)
-    high = both.astype(BF16)
-    return high, (both - high.astype(F32)).astype(BF16)
-
-
-def applied(z, high, low):
-    side = lhs(z)
-    return dot(side, high, ((1,), (1,))) + dot(side, low, ((1,), (1,)))
-
-
-def own_kernel(nfreq, nclass, kappa, coeff, green, facing, other, swept, operator, inverse, first, second):
+    return jnp.concatenate([real, imag], axis=1).astype(BF16)
+
+
+def applied(z, product):
+    return dot(lhs(z), product, ((1,), (1,)))
+
+
+def own_kernel(nfreq, kappa, coeff, green, facing, other, swept, operator, inverse, first, second):
     part = lax.div(lax.axis_index("par"), nfreq)
     cells = green.shape[1]
     blocks = cells // LANES
@@ -113,7 +110,7 @@
     extent = cells + 2 * REACH
 
     def inv(index):
-        return 1.0 / (4.0 + chosen(kappa, index, nclass, lambda t, k: t[k]))
+        return 1.0 / (4.0 + chosen(kappa[...], index))
 
     def column(value):
         return jnp.transpose(jnp.broadcast_to(value, (LANES, LANES)))
@@ -156,11 +153,11 @@
 def cross_kernel(swept, *refs):
     greens, pairs = refs[: len(refs) // 2], refs[len(refs) // 2 :]
     for green, pair in zip(greens, pairs):
-        pair[0], pair[1] = halves(dot(swept[...], planes(green, 0, green.shape[1])))
+        pair[...] = halves(dot(swept[...], planes(green, 0, green.shape[1])))
 
 
 def data_of(nsens, weight, refs):
-    terms = [applied(v[...], p[0], p[1]) for v, p in zip(refs[:nsens], refs[nsens:])]
+    terms = [applied(v[...], p[...]) for v, p in zip(refs[:nsens], refs[nsens:])]
     return weight[...] * sum(terms[1:], terms[0])
 
 
@@ -192,7 +189,6 @@
     nsens = lax.axis_size("sens")
     sensors, rows_dev = probes.shape[1:]
     cells = green_blocks.shape[1]
-    smem = pl.BlockSpec(memory_space=pltpu.SMEM)
     vmem = pl.BlockSpec(memory_space=pltpu.VMEM)
     greens = [turned(green_blocks, "sens", k) for k in range(1, nsens)]
     vector = jnp.transpose(probes, (0, 2, 1))
@@ -207,7 +203,7 @@
             rim,
             rim,
         ],
-        in_specs=[smem] + [vmem] * 3,
+        in_specs=[vmem] * 4,
         out_specs=[vmem] * 4,
         compiler_params=PARAMS,
         cost_estimate=PRIOR,
@@ -226,9 +222,9 @@
     rows = SPLIT * rows_dev
     extent = cells + 2 * REACH
     swept = pl.pallas_call(
-        functools.partial(own_kernel, nfreq, kappa_table.shape[0]),
+        functools.partial(own_kernel, nfreq),
         out_shape=jax.ShapeDtypeStruct((2 * sensors, cells), BF16),
-        in_specs=[smem] + [vmem] * 4,
+        in_specs=[vmem] * 5,
         out_specs=vmem,
         scratch_shapes=[
             pltpu.VMEM((extent, 2 * sensors), BF16),
@@ -239,10 +235,10 @@
         compiler_params=PARAMS,
         cost_estimate=BESIDE,
         name="own",
-    )(kappa_table, coeff_index.reshape(-1, LANES), green_blocks, got, other)
+    )(kappa_table.reshape(1, -1), coeff_index.reshape(-1, LANES), green_blocks, got, other)
     pairs = pl.pallas_call(
         cross_kernel,
-        out_shape=[jax.ShapeDtypeStruct((2, sensors, 2 * sensors), BF16)] * nsens,
+        out_shape=[jax.ShapeDtypeStruct((sensors, 2 * sensors), BF16)] * nsens,
         in_specs=[vmem] * (1 + nsens),
         out_specs=[vmem] * nsens,
         compiler_params=PARAMS,

time: 24 us -> 24 us (level)
  Pallas kernels: 2.73 us -> 1.66 us
  local copies, waits for them, and re-layouts: 1.79 us -> 2.44 us
  waiting for transfers between devices: 4.46 us -> 4.73 us
    unnamed x14, local copies, waits for them, and re-layouts: 1.78 us -> 2.42 us
    pallas_call x1, Pallas kernels: 0.59 us -> 0.08 us  [shards(): pl.pallas_call(functools.partial(prep_kernel, nfreq), out_shape=[jax.Shap...]
    pallas_call x2, Pallas kernels: 1.66 us -> 1.19 us  [the longest x1 0.76 us: shards(): pl.pallas_call(functools.partial(own_kernel, nfreq), out_shape=jax.ShapeD...]
    ppermute x2, waiting for transfers between devices: 2.69 us -> 3.09 us  [swapped(): lax.ppermute(value, axis, [(i, i ^ mask) for i in range(lax.axis_size(axi...]
  transfers between devices with their start and end apart: 10 -> 10, of which waited for: 5 -> 6; matrix products, arithmetic and copies ran while one was open for 0% -> 0% of each run, Pallas kernels for 10% -> 6%
where the time goes in v8:
time: 24 us; the launch traced here: 23.8 us
  starting transfers between devices  14.1 us (59%)
  waiting for transfers between devices  4.73 us (20%)
  local copies, waits for them, and re-layouts  2.44 us (10%)
  Pallas kernels  1.66 us (7%)
  other arithmetic  0.68 us (3%)
    ppermute x3, starting transfers between devices, turned(): lax.ppermute(value, axis, [(i, (i + step) % size) for i in range(size)])  5.06 us
    ppermute x4, starting transfers between devices, routed(): return lax.ppermute(value, axis, pairs)  4.84 us
    ppermute x2, starting transfers between devices, swapped(): lax.ppermute(value, axis, [(i, i ^ mask) for i in range(lax.axis_size(axi...  4.23 us
    ppermute x2, waiting for transfers between devices, swapped(): lax.ppermute(value, axis, [(i, i ^ mask) for i in range(lax.axis_size(axi...  3.09 us
    unnamed x14, local copies, waits for them, and re-layouts  2.42 us
    ppermute x4, waiting for transfers between devices, routed(): return lax.ppermute(value, axis, pairs)  1.44 us
    pallas_call x1, Pallas kernels, shards(): pl.pallas_call(functools.partial(own_kernel, nfreq), out_shape=jax.ShapeD...  0.76 us
    transpose x1, other arithmetic, shards(): return jnp.transpose(keep, (0, 2, 1))  0.63 us
  transfers between devices with their start and end apart: 10, of which 6 were waited for; matrix products, arithmetic and copies ran while one was open for 0% of the time, Pallas kernels for 6%

profile of v8, /device:TPU:0, one launch (start us, length us, event | category | flops | bytes accessed | tf_op | source)
XLA Modules:
  0.0 23.8 jit_solution(14174652214197998404)
XLA Ops:
  0.0 3.0 %collective-permute-start.4 = (bf16[2,1024,128]{2,1,0:T(8,128)(2,1)}, bf16[2,1024,128]{2,1,0:T(8,128)(2,1)S(1)}, u32[]{:S(2)}, u32[]{:S(2)}) collective-permute-start(bf16[2,1024,128]{2,1,0:T(8,128)(2,1)} %refs_0_.1), channel_id=1, source_target_pairs={{0,16},{16,0},{1,17},{17,1},{2,18},{18,2},{3,19},{19,3},{4,20},{20... | collective-permute-start | bytes 1572872 | tf_op jit(solution)/shard_map/ppermute | solution.py:29
  3.0 2.6 %collective-permute-start = (bf16[2,32,128]{2,1,0:T(8,128)(2,1)}, bf16[2,32,128]{2,1,0:T(8,128)(2,1)S(1)}, u32[]{:S(2)}, u32[]{:S(2)}) collective-permute-start(bf16[2,32,128]{2,1,0:T(8,128)(2,1)} %bitcast.16), channel_id=1, source_target_pairs={{0,8},{1,9},{2,10},{3,11},{4,12},{5,13},{6,14},{7,15},{8,0},{9,1},... | collective-permute-start | bytes 49160 | tf_op jit(solution)/shard_map/ppermute | solution.py:24
  5.6 0.0 copy-done.3
  5.6 0.0 copy-done.4
  5.6 1.0 %copy-done = bf16[2,1024,128]{2,1,0:T(8,128)(2,1)S(1)} copy-done((bf16[2,1024,128]{2,1,0:T(8,128)(2,1)S(1)}, bf16[2,1024,128]{2,1,0:T(8,128)(2,1)}, u32[]{:S(2)}) %copy-start) | copy-done | bytes 524312
  6.6 0.7 %copy-done.2 = bf16[2,128,32]{1,2,0:T(8,128)(2,1)S(1)} copy-done((bf16[2,128,32]{1,2,0:T(8,128)(2,1)S(1)}, bf16[2,128,32]{1,2,0:T(8,128)(2,1)}, u32[]{:S(2)}) %copy-start.2) | copy-done | bytes 16408
  7.3 0.1 prep.1
  7.4 0.4 %collective-permute-done = bf16[2,32,128]{2,1,0:T(8,128)(2,1)S(1)} collective-permute-done((bf16[2,32,128]{2,1,0:T(8,128)(2,1)}, bf16[2,32,128]{2,1,0:T(8,128)(2,1)S(1)}, u32[]{:S(2)}, u32[]{:S(2)}) %collective-permute-start) | collective-permute-done | bytes 16416 | tf_op jit(solution)/shard_map/ppermute | solution.py:24
  7.8 1.6 %collective-permute-start.1 = (bf16[2,2,64,128]{3,2,1,0:T(8,128)(2,1)S(1)}, bf16[2,2,64,128]{3,2,1,0:T(8,128)(2,1)S(1)}, u32[]{:S(2)}, u32[]{:S(2)}) collective-permute-start(bf16[2,2,64,128]{3,2,1,0:T(8,128)(2,1)S(1)} %pad_maximum_fusion), channel_id=1, source_target_pairs={{0,4},{1,5},{2,6},{3,7},{4,0},{5,1},{6,2},{7,3},{8,12},{9,13},{10,... | collective-permute-start | bytes 196616 | tf_op jit(solution)/shard_map/ppermute | solution.py:24
  9.5 0.0 collective-permute-start.3
  9.5 2.7 %collective-permute-done.1.facing = bf16[2,2,64,128]{3,2,1,0:T(8,128)(2,1)S(1)} collective-permute-done((bf16[2,2,64,128]{3,2,1,0:T(8,128)(2,1)S(1)}, bf16[2,2,64,128]{3,2,1,0:T(8,128)(2,1)S(1)}, u32[]{:S(2)}, u32[]{:S(2)}) %collective-permute-start.1) | collective-permute-done | bytes 65568 | tf_op jit(solution)/shard_map/ppermute | solution.py:24
  12.2 0.0 copy-start.5
  12.2 0.3 %collective-permute-start.2 = (bf16[3,2,32,128]{3,2,1,0:T(8,128)(2,1)S(1)}, bf16[3,2,32,128]{3,2,1,0:T(8,128)(2,1)S(1)}, u32[]{:S(2)}, u32[]{:S(2)}) collective-permute-start(bf16[3,2,32,128]{3,2,1,0:T(8,128)(2,1)S(1)} %slice.13.refs_0_), channel_id=1, source_target_pairs={{0,16},{16,0},{1,17},{17,1},{2,18},{18,2},{3,19},{19,3},{4,20},{20... | collective-permute-start | bytes 147464 | tf_op jit(solution)/shard_map/ppermute | solution.py:29
  12.6 1.7 %collective-permute-start.6 = (bf16[1,2,32,128]{3,2,1,0:T(8,128)(2,1)S(1)}, bf16[1,2,32,128]{3,2,1,0:T(8,128)(2,1)S(1)}, u32[]{:S(2)}, u32[]{:S(2)}) collective-permute-start(bf16[1,2,32,128]{3,2,1,0:T(8,128)(2,1)S(1)} %slice.14.refs_0_), channel_id=1, source_target_pairs={{0,16},{16,0},{1,17},{17,1},{2,18},{18,2},{3,19},{19,3},{4,20},{20... | collective-permute-start | bytes 49160 | tf_op jit(solution)/shard_map/ppermute | solution.py:29
  14.3 0.0 collective-permute-done.3.other
  14.3 0.6 %copy-done.6 = f32[16]{0:T(128)S(1)} copy-done((f32[16]{0:T(128)S(1)}, f32[16]{0:T(128)}, u32[]{:S(2)}) %copy-start.6) | copy-done | bytes 88
  15.0 0.8 %own.1.swept = bf16[256,1024]{1,0:T(8,128)(2,1)S(1)} custom-call(f32[1,16]{1,0:T(1,128)S(1)} %bitcast.21, s32[32,128]{1,0:T(8,128)S(1)} %bitcast.20, bf16[2,1024,128]{2,1,0:T(8,128)(2,1)S(1)} %copy-done.1, bf16[2,2,64,128]{3,2,1,0:T(8,128)(2,1)S(1)} %collective-permute-done.1.facing, bf16[2,64,128]{2,1,0:T(8,128)(2,1)S(1)} %collective-permute-done.3.other), custom_call_target="tpu_custom_call" | custom-call | flops 575000000 | bytes 1 | tf_op jit(solution)/shard_map/own/pallas_call | solution.py:224
  15.7 0.1 collective-permute-done.4.refs_1_
  15.8 0.4 %cross.1 = (bf16[128,256]{1,0:T(8,128)(2,1)S(1)}, bf16[128,256]{1,0:T(8,128)(2,1)S(1)}) custom-call(bf16[256,1024]{1,0:T(8,128)(2,1)S(1)} %own.1.swept, bf16[2,1024,128]{2,1,0:T(8,128)(2,1)S(1)} %copy-done.1, bf16[2,1024,128]{2,1,0:T(8,128)(2,1)S(1)} %collective-permute-done.4.refs_1_), custom_call_target="tpu_custom_call" | custom-call | flops 1 | bytes 1 | tf_op jit(solution)/shard_map/cross/pallas_call | solution.py:239
  16.2 0.1 collective-permute-done.2.refs_1_
  16.4 0.2 send.1
  16.6 1.8 %collective-permute-start.5 = (bf16[2,32,128]{2,1,0:T(8,128)(2,1)S(1)}, bf16[2,32,128]{2,1,0:T(8,128)(2,1)S(1)}, u32[]{:S(2)}, u32[]{:S(2)}) collective-permute-start(bf16[2,32,128]{2,1,0:T(8,128)(2,1)S(1)} %get-tuple-element.28), channel_id=1, source_target_pairs={{0,4},{1,13},{2,6},{3,15},{4,8},{5,9},{6,10},{7,11},{8,12},{9,5},{... | collective-permute-start | bytes 49160 | tf_op jit(solution)/shard_map/ppermute | solution.py:46
  18.4 0.0 collective-permute-done.6.refs_1_
  18.4 0.5 %collective-permute-start.7 = (bf16[2,32,128]{2,1,0:T(8,128)(2,1)S(1)}, bf16[2,32,128]{2,1,0:T(8,128)(2,1)S(1)}, u32[]{:S(2)}, u32[]{:S(2)}) collective-permute-start(bf16[2,32,128]{2,1,0:T(8,128)(2,1)S(1)} %get-tuple-element.34), channel_id=1, source_target_pairs={{0,1},{1,9},{2,3},{3,11},{4,5},{5,4},{6,7},{7,6},{8,0},{9,8},{10,2... | collective-permute-start | bytes 49160 | tf_op jit(solution)/shard_map/ppermute | solution.py:46
  18.9 1.7 %collective-permute-start.8 = (bf16[2,32,128]{2,1,0:T(8,128)(2,1)S(1)}, bf16[2,32,128]{2,1,0:T(8,128)(2,1)S(1)}, u32[]{:S(2)}, u32[]{:S(2)}) collective-permute-start(bf16[2,32,128]{2,1,0:T(8,128)(2,1)S(1)} %get-tuple-element.35), channel_id=1, source_target_pairs={{0,12},{1,5},{2,14},{3,7},{4,0},{5,13},{6,2},{7,15},{8,4},{9,1},{1... | collective-permute-start | bytes 49160 | tf_op jit(solution)/shard_map/ppermute | solution.py:46
  20.6 0.8 %collective-permute-start.9 = (bf16[2,32,128]{2,1,0:T(8,128)(2,1)S(1)}, bf16[2,32,128]{2,1,0:T(8,128)(2,1)S(1)}, u32[]{:S(2)}, u32[]{:S(2)}) collective-permute-start(bf16[2,32,128]{2,1,0:T(8,128)(2,1)S(1)} %get-tuple-element.36), channel_id=1, source_target_pairs={{0,8},{1,0},{2,10},{3,2},{4,12},{5,1},{6,14},{7,3},{8,9},{9,13},{1... | collective-permute-start | bytes 49160 | tf_op jit(solution)/shard_map/ppermute | solution.py:46
  21.5 0.7 %collective-permute-done.5 = bf16[2,32,128]{2,1,0:T(8,128)(2,1)S(1)} collective-permute-done((bf16[2,32,128]{2,1,0:T(8,128)(2,1)S(1)}, bf16[2,32,128]{2,1,0:T(8,128)(2,1)S(1)}, u32[]{:S(2)}, u32[]{:S(2)}) %collective-permute-start.5) | collective-permute-done | bytes 16416 | tf_op jit(solution)/shard_map/ppermute | solution.py:46
  22.2 0.2 keep.1
  22.4 0.7 %collective-permute-done.7 = bf16[2,32,128]{2,1,0:T(8,128)(2,1)S(1)} collective-permute-done((bf16[2,32,128]{2,1,0:T(8,128)(2,1)S(1)}, bf16[2,32,128]{2,1,0:T(8,128)(2,1)S(1)}, u32[]{:S(2)}, u32[]{:S(2)}) %collective-permute-start.7) | collective-permute-done | bytes 16416 | tf_op jit(solution)/shard_map/ppermute | solution.py:46
  23.1 0.0 collective-permute-done.8
  23.1 0.0 collective-permute-done.9
  23.1 0.6 %add_bitcast_fusion = f32[2,128,32]{1,2,0:T(8,128)} fusion(f32[2,32,128]{2,1,0:T(8,128)S(1)} %convert_add_fusion, bf16[2,32,128]{2,1,0:T(8,128)(2,1)S(1)} %collective-permute-done.9, pred[]{:T(512)S(6)} %and.58, pred[]{:T(512)S(6)} %and.57), kind=kLoop, calls=%fused_computation.2 | loop fusion | flops 32768 | bytes 81922 | tf_op jit(solution)/shard_map/transpose | solution.py:278
  (16 shorter events, 0.1 us)
Async XLA Ops:
  0.0 5.6 %copy-start.3 = (f32[4,8]{1,0:T(4,128)S(1)}, f32[4,8]{1,0:T(4,128)}, u32[]{:S(2)}) copy-start(f32[4,8]{1,0:T(4,128)} %noise.1) | copy-start | bytes 388
  0.0 15.8 %collective-permute-start.4 = (bf16[2,1024,128]{2,1,0:T(8,128)(2,1)}, bf16[2,1024,128]{2,1,0:T(8,128)(2,1)S(1)}, u32[]{:S(2)}, u32[]{:S(2)}) collective-permute-start(bf16[2,1024,128]{2,1,0:T(8,128)(2,1)} %refs_0_.1), channel_id=1, source_target_pairs={{0,16},{16,0},{1,17},{17,1},{2,18},{18,2},{3,19},{19,3},{4,20},{20... | collective-permute-start | bytes 1572872 | tf_op jit(solution)/shard_map/ppermute | solution.py:29
  3.0 2.6 %copy-start.4 = (s32[128]{0:T(128)S(1)}, s32[128]{0:T(128)}, u32[]{:S(2)}) copy-start(s32[128]{0:T(128)} %param.9) | copy-start | bytes 1540
  3.0 4.8 %collective-permute-start = (bf16[2,32,128]{2,1,0:T(8,128)(2,1)}, bf16[2,32,128]{2,1,0:T(8,128)(2,1)S(1)}, u32[]{:S(2)}, u32[]{:S(2)}) collective-permute-start(bf16[2,32,128]{2,1,0:T(8,128)(2,1)} %bitcast.16), channel_id=1, source_target_pairs={{0,8},{1,9},{2,10},{3,11},{4,12},{5,13},{6,14},{7,15},{8,0},{9,1},... | collective-permute-start | bytes 49160 | tf_op jit(solution)/shard_map/ppermute | solution.py:24
  5.6 1.0 %copy-start = (bf16[2,1024,128]{2,1,0:T(8,128)(2,1)S(1)}, bf16[2,1024,128]{2,1,0:T(8,128)(2,1)}, u32[]{:S(2)}) copy-start(bf16[2,1024,128]{2,1,0:T(8,128)(2,1)} %refs_0_.1) | copy-start | bytes 1572868
  6.6 0.7 %copy-start.2 = (bf16[2,128,32]{1,2,0:T(8,128)(2,1)S(1)}, bf16[2,128,32]{1,2,0:T(8,128)(2,1)}, u32[]{:S(2)}) copy-start(bf16[2,128,32]{1,2,0:T(8,128)(2,1)} %param.6) | copy-start | bytes 49156
  7.3 7.0 %copy-start.1 = (bf16[2,1024,128]{2,1,0:T(8,128)(2,1)S(1)}, bf16[2,1024,128]{2,1,0:T(8,128)(2,1)}, u32[]{:S(2)}) copy-start(bf16[2,1024,128]{2,1,0:T(8,128)(2,1)} %refs_0_.1) | copy-start | bytes 1572868
  7.8 4.3 %collective-permute-start.1 = (bf16[2,2,64,128]{3,2,1,0:T(8,128)(2,1)S(1)}, bf16[2,2,64,128]{3,2,1,0:T(8,128)(2,1)S(1)}, u32[]{:S(2)}, u32[]{:S(2)}) collective-permute-start(bf16[2,2,64,128]{3,2,1,0:T(8,128)(2,1)S(1)} %pad_maximum_fusion), channel_id=1, source_target_pairs={{0,4},{1,5},{2,6},{3,7},{4,0},{5,1},{6,2},{7,3},{8,12},{9,13},{10,... | collective-permute-start | bytes 196616 | tf_op jit(solution)/shard_map/ppermute | solution.py:24
  9.5 4.8 %collective-permute-start.3 = (bf16[2,64,128]{2,1,0:T(8,128)(2,1)S(1)}, bf16[2,64,128]{2,1,0:T(8,128)(2,1)S(1)}, u32[]{:S(2)}, u32[]{:S(2)}) collective-permute-start(bf16[2,64,128]{2,1,0:T(8,128)(2,1)S(1)} %get-tuple-element.25), channel_id=1, source_target_pairs={{0,1},{1,0},{2,3},{3,2},{4,8},{5,9},{6,10},{7,11},{8,4},{9,5},{10,... | collective-permute-start | bytes 98312 | tf_op jit(solution)/shard_map/ppermute | solution.py:38
  12.2 2.1 %copy-start.5 = (s32[4096]{0:T(1024)S(1)}, s32[4096]{0:T(1024)}, u32[]{:S(2)}) copy-start(s32[4096]{0:T(1024)} %param.11) | copy-start | bytes 49156
  12.2 4.2 %collective-permute-start.2 = (bf16[3,2,32,128]{3,2,1,0:T(8,128)(2,1)S(1)}, bf16[3,2,32,128]{3,2,1,0:T(8,128)(2,1)S(1)}, u32[]{:S(2)}, u32[]{:S(2)}) collective-permute-start(bf16[3,2,32,128]{3,2,1,0:T(8,128)(2,1)S(1)} %slice.13.refs_0_), channel_id=1, source_target_pairs={{0,16},{16,0},{1,17},{17,1},{2,18},{18,2},{3,19},{19,3},{4,20},{20... | collective-permute-start | bytes 147464 | tf_op jit(solution)/shard_map/ppermute | solution.py:29
  12.6 5.8 %collective-permute-start.6 = (bf16[1,2,32,128]{3,2,1,0:T(8,128)(2,1)S(1)}, bf16[1,2,32,128]{3,2,1,0:T(8,128)(2,1)S(1)}, u32[]{:S(2)}, u32[]{:S(2)}) collective-permute-start(bf16[1,2,32,128]{3,2,1,0:T(8,128)(2,1)S(1)} %slice.14.refs_0_), channel_id=1, source_target_pairs={{0,16},{16,0},{1,17},{17,1},{2,18},{18,2},{3,19},{19,3},{4,20},{20... | collective-permute-start | bytes 49160 | tf_op jit(solution)/shard_map/ppermute | solution.py:29
  14.3 0.7 %copy-start.6 = (f32[16]{0:T(128)S(1)}, f32[16]{0:T(128)}, u32[]{:S(2)}) copy-start(f32[16]{0:T(128)} %param.10) | copy-start | bytes 196
  16.6 5.6 %collective-permute-start.5 = (bf16[2,32,128]{2,1,0:T(8,128)(2,1)S(1)}, bf16[2,32,128]{2,1,0:T(8,128)(2,1)S(1)}, u32[]{:S(2)}, u32[]{:S(2)}) collective-permute-start(bf16[2,32,128]{2,1,0:T(8,128)(2,1)S(1)} %get-tuple-element.28), channel_id=1, source_target_pairs={{0,4},{1,13},{2,6},{3,15},{4,8},{5,9},{6,10},{7,11},{8,12},{9,5},{... | collective-permute-start | bytes 49160 | tf_op jit(solution)/shard_map/ppermute | solution.py:46
  18.4 4.7 %collective-permute-start.7 = (bf16[2,32,128]{2,1,0:T(8,128)(2,1)S(1)}, bf16[2,32,128]{2,1,0:T(8,128)(2,1)S(1)}, u32[]{:S(2)}, u32[]{:S(2)}) collective-permute-start(bf16[2,32,128]{2,1,0:T(8,128)(2,1)S(1)} %get-tuple-element.34), channel_id=1, source_target_pairs={{0,1},{1,9},{2,3},{3,11},{4,5},{5,4},{6,7},{7,6},{8,0},{9,8},{10,2... | collective-permute-start | bytes 49160 | tf_op jit(solution)/shard_map/ppermute | solution.py:46
  18.9 4.1 %collective-permute-start.8 = (bf16[2,32,128]{2,1,0:T(8,128)(2,1)S(1)}, bf16[2,32,128]{2,1,0:T(8,128)(2,1)S(1)}, u32[]{:S(2)}, u32[]{:S(2)}) collective-permute-start(bf16[2,32,128]{2,1,0:T(8,128)(2,1)S(1)} %get-tuple-element.35), channel_id=1, source_target_pairs={{0,12},{1,5},{2,14},{3,7},{4,0},{5,13},{6,2},{7,15},{8,4},{9,1},{1... | collective-permute-start | bytes 49160 | tf_op jit(solution)/shard_map/ppermute | solution.py:46
  20.6 2.5 %collective-permute-start.9 = (bf16[2,32,128]{2,1,0:T(8,128)(2,1)S(1)}, bf16[2,32,128]{2,1,0:T(8,128)(2,1)S(1)}, u32[]{:S(2)}, u32[]{:S(2)}) collective-permute-start(bf16[2,32,128]{2,1,0:T(8,128)(2,1)S(1)} %get-tuple-element.36), channel_id=1, source_target_pairs={{0,8},{1,0},{2,10},{3,2},{4,12},{5,1},{6,14},{7,3},{8,9},{9,13},{1... | collective-permute-start | bytes 49160 | tf_op jit(solution)/shard_map/ppermute | solution.py:46

commit v9 on v8

--- a/solution.py
+++ b/solution.py
@@ -102,7 +102,7 @@
     return dot(lhs(z), product, ((1,), (1,)))
 
 
-def own_kernel(nfreq, kappa, coeff, green, facing, other, swept, operator, inverse, first, second):
+def own_kernel(nfreq, weight, kappa, coeff, green, facing, other, swept, operator, inverse, first, second):
     part = lax.div(lax.axis_index("par"), nfreq)
     cells = green.shape[1]
     blocks = cells // LANES
@@ -129,6 +129,7 @@
     operator[REACH : REACH + cells] = planes(green, 0, cells)
     operator[extent - REACH : extent] = jnp.where(odd, far, near)
 
+    wide = jnp.concatenate([weight[...]] * 2, axis=1)
     hood = stencil()
     none = jnp.zeros((DIP, 2 * LANES), BF16)
     for ref in (first, second):
@@ -147,7 +148,7 @@
         second[DIP + at : DIP + at + LANES] = solved(at, total).astype(BF16)
     for at in range(REACH, REACH + cells, LANES):
         total = operator[at : at + LANES].astype(F32) + dot(hood, second[at : at + LANES + 2 * DIP])
-        swept[:, at - REACH : at - REACH + LANES] = jnp.transpose(solved(at, total)).astype(BF16)
+        swept[:, at - REACH : at - REACH + LANES] = jnp.transpose(wide * solved(at, total)).astype(BF16)
 
 
 def cross_kernel(swept, *refs):
@@ -156,24 +157,24 @@
         pair[...] = halves(dot(swept[...], planes(green, 0, green.shape[1])))
 
 
-def data_of(nsens, weight, refs):
+def data_of(nsens, refs):
     terms = [applied(v[...], p[...]) for v, p in zip(refs[:nsens], refs[nsens:])]
-    return weight[...] * sum(terms[1:], terms[0])
-
-
-def keep_kernel(nsens, weight, *refs):
-    data = data_of(nsens, weight, refs[:-1])
+    return sum(terms[1:], terms[0])
+
+
+def keep_kernel(nsens, *refs):
+    data = data_of(nsens, refs[:-1])
     half = data.shape[0] // 2
     for k in range(2):
         refs[-1][k] = data[k * half : (k + 1) * half]
 
 
-def send_kernel(nfreq, nsens, weight, *refs):
-    refs, (*sends, total) = refs[: 2 * nsens], refs[2 * nsens :]
+def send_kernel(nfreq, nsens, *refs):
+    refs, sends = refs[: 2 * nsens], refs[2 * nsens :]
     par = lax.axis_index("par")
     part, odd = lax.div(par, nfreq), lax.rem(par, 2)
-    total[...] = data_of(nsens, weight, refs)
-    half = total.shape[0] // 2
+    data = data_of(nsens, refs)
+    half = data.shape[0] // 2
     rows = half // (SPLIT - 1)
     for send, step in zip(sends, ROUTES):
         place = 0
@@ -181,7 +182,11 @@
             for p, q in enumerate(route):
                 place = jnp.where((part == p) & (odd == core), PLACE[p ^ max(q, 0)], place)
         for k in range(2):
-            send[k] = total[pl.ds(pl.multiple_of(k * half + place * rows, rows), rows), :].astype(BF16)
+            blocks = [data[k * half + j * rows : k * half + (j + 1) * rows] for j in range(SPLIT - 1)]
+            share = blocks[0]
+            for j, block in enumerate(blocks[1:], 1):
+                share = jnp.where(place == j, block, share)
+            send[k] = share.astype(BF16)
 
 
 def shards(probes, green_blocks, noise_table, station_class, kappa_table, coeff_index):
@@ -224,7 +229,7 @@
     swept = pl.pallas_call(
         functools.partial(own_kernel, nfreq),
         out_shape=jax.ShapeDtypeStruct((2 * sensors, cells), BF16),
-        in_specs=[vmem] * 5,
+        in_specs=[vmem] * 6,
         out_specs=vmem,
         scratch_shapes=[
             pltpu.VMEM((extent, 2 * sensors), BF16),
@@ -235,7 +240,7 @@
         compiler_params=PARAMS,
         cost_estimate=BESIDE,
         name="own",
-    )(kappa_table.reshape(1, -1), coeff_index.reshape(-1, LANES), green_blocks, got, other)
+    )(weight, kappa_table.reshape(1, -1), coeff_index.reshape(-1, LANES), green_blocks, got, other)
     pairs = pl.pallas_call(
         cross_kernel,
         out_shape=[jax.ShapeDtypeStruct((sensors, 2 * sensors), BF16)] * nsens,
@@ -248,24 +253,23 @@
     sends = list(pl.pallas_call(
         functools.partial(send_kernel, nfreq, nsens),
         out_shape=[jax.ShapeDtypeStruct((2, rows_dev, sensors), BF16)] * len(ROUTES),
-        in_specs=[vmem] * (1 + 2 * nsens),
+        in_specs=[vmem] * (2 * nsens),
         out_specs=[vmem] * len(ROUTES),
-        scratch_shapes=[pltpu.VMEM((2 * (rows - rows_dev), sensors), F32)],
         compiler_params=PARAMS,
         name="send",
-    )(weight, given, *rests[0], *pairs))
+    )(given, *rests[0], *pairs))
     sends[2], rests[1] = lax.optimization_barrier((sends[2], rests[1]))
     shares = [routed(send, "par", nfreq, step) for send, step in zip(sends, ROUTES)]
     shares[0], kept = lax.optimization_barrier((shares[0], kept))
     keep = pl.pallas_call(
         functools.partial(keep_kernel, nsens),
         out_shape=jax.ShapeDtypeStruct((2, rows_dev, sensors), F32),
-        in_specs=[vmem] * (1 + 2 * nsens),
+        in_specs=[vmem] * (2 * nsens),
         out_specs=vmem,
         compiler_params=PARAMS,
         cost_estimate=PRIOR,
         name="keep",
-    )(weight, kept, *rests[1], *pairs)
+    )(kept, *rests[1], *pairs)
     par = lax.axis_index("par")
     for step, share in zip(ROUTES, shares):
         share = share.astype(F32)

time: 24 us -> 24 us (level)
  transfers between devices with their start and end apart: 10 -> 10, of which waited for: 6 -> 5; matrix products, arithmetic and copies ran while one was open for 0% -> 0% of each run, Pallas kernels for 6% -> 6%
where the time goes in v9:
time: 24 us; the launch traced here: 23.7 us
  starting transfers between devices  14.1 us (59%)
  waiting for transfers between devices  4.71 us (20%)
  local copies, waits for them, and re-layouts  2.44 us (10%)
  Pallas kernels  1.67 us (7%)
  other arithmetic  0.68 us (3%)
    ppermute x3, starting transfers between devices, turned(): lax.ppermute(value, axis, [(i, (i + step) % size) for i in range(size)])  5.06 us
    ppermute x4, starting transfers between devices, routed(): return lax.ppermute(value, axis, pairs)  4.84 us
    ppermute x2, starting transfers between devices, swapped(): lax.ppermute(value, axis, [(i, i ^ mask) for i in range(lax.axis_size(axi...  4.23 us
    ppermute x2, waiting for transfers between devices, swapped(): lax.ppermute(value, axis, [(i, i ^ mask) for i in range(lax.axis_size(axi...  3.09 us
    unnamed x14, local copies, waits for them, and re-layouts  2.42 us
    ppermute x4, waiting for transfers between devices, routed(): return lax.ppermute(value, axis, pairs)  1.44 us
    pallas_call x1, Pallas kernels, shards(): pl.pallas_call(functools.partial(own_kernel, nfreq), out_shape=jax.ShapeD...  0.78 us
    transpose x1, other arithmetic, shards(): return jnp.transpose(keep, (0, 2, 1))  0.63 us
  transfers between devices with their start and end apart: 10, of which 5 were waited for; matrix products, arithmetic and copies ran while one was open for 0% of the time, Pallas kernels for 6%

profile of v9, /device:TPU:0, one launch (start us, length us, event | category | flops | bytes accessed | tf_op | source)
XLA Modules:
  0.0 23.7 jit_solution(13269939984120959540)
XLA Ops:
  0.0 3.0 %collective-permute-start.4 = (bf16[2,1024,128]{2,1,0:T(8,128)(2,1)}, bf16[2,1024,128]{2,1,0:T(8,128)(2,1)S(1)}, u32[]{:S(2)}, u32[]{:S(2)}) collective-permute-start(bf16[2,1024,128]{2,1,0:T(8,128)(2,1)} %refs_0_.1), channel_id=1, source_target_pairs={{0,16},{16,0},{1,17},{17,1},{2,18},{18,2},{3,19},{19,3},{4,20},{20... | collective-permute-start | bytes 1572872 | tf_op jit(solution)/shard_map/ppermute | solution.py:29
  3.0 2.6 %collective-permute-start = (bf16[2,32,128]{2,1,0:T(8,128)(2,1)}, bf16[2,32,128]{2,1,0:T(8,128)(2,1)S(1)}, u32[]{:S(2)}, u32[]{:S(2)}) collective-permute-start(bf16[2,32,128]{2,1,0:T(8,128)(2,1)} %bitcast.16), channel_id=1, source_target_pairs={{0,8},{1,9},{2,10},{3,11},{4,12},{5,13},{6,14},{7,15},{8,0},{9,1},... | collective-permute-start | bytes 49160 | tf_op jit(solution)/shard_map/ppermute | solution.py:24
  5.6 0.0 copy-done.3
  5.6 1.0 %copy-done = bf16[2,1024,128]{2,1,0:T(8,128)(2,1)S(1)} copy-done((bf16[2,1024,128]{2,1,0:T(8,128)(2,1)S(1)}, bf16[2,1024,128]{2,1,0:T(8,128)(2,1)}, u32[]{:S(2)}) %copy-start) | copy-done | bytes 524312
  6.6 0.7 %copy-done.2 = bf16[2,128,32]{1,2,0:T(8,128)(2,1)S(1)} copy-done((bf16[2,128,32]{1,2,0:T(8,128)(2,1)S(1)}, bf16[2,128,32]{1,2,0:T(8,128)(2,1)}, u32[]{:S(2)}) %copy-start.2) | copy-done | bytes 16408
  7.3 0.1 prep.1
  7.4 0.4 %collective-permute-done = bf16[2,32,128]{2,1,0:T(8,128)(2,1)S(1)} collective-permute-done((bf16[2,32,128]{2,1,0:T(8,128)(2,1)}, bf16[2,32,128]{2,1,0:T(8,128)(2,1)S(1)}, u32[]{:S(2)}, u32[]{:S(2)}) %collective-permute-start) | collective-permute-done | bytes 16416 | tf_op jit(solution)/shard_map/ppermute | solution.py:24
  7.8 1.6 %collective-permute-start.1 = (bf16[2,2,64,128]{3,2,1,0:T(8,128)(2,1)S(1)}, bf16[2,2,64,128]{3,2,1,0:T(8,128)(2,1)S(1)}, u32[]{:S(2)}, u32[]{:S(2)}) collective-permute-start(bf16[2,2,64,128]{3,2,1,0:T(8,128)(2,1)S(1)} %pad_maximum_fusion), channel_id=1, source_target_pairs={{0,4},{1,5},{2,6},{3,7},{4,0},{5,1},{6,2},{7,3},{8,12},{9,13},{10,... | collective-permute-start | bytes 196616 | tf_op jit(solution)/shard_map/ppermute | solution.py:24
  9.5 0.0 collective-permute-start.3
  9.5 2.7 %collective-permute-done.1.facing = bf16[2,2,64,128]{3,2,1,0:T(8,128)(2,1)S(1)} collective-permute-done((bf16[2,2,64,128]{3,2,1,0:T(8,128)(2,1)S(1)}, bf16[2,2,64,128]{3,2,1,0:T(8,128)(2,1)S(1)}, u32[]{:S(2)}, u32[]{:S(2)}) %collective-permute-start.1) | collective-permute-done | bytes 65568 | tf_op jit(solution)/shard_map/ppermute | solution.py:24
  12.2 0.0 copy-start.5
  12.2 0.3 %collective-permute-start.2 = (bf16[3,2,32,128]{3,2,1,0:T(8,128)(2,1)S(1)}, bf16[3,2,32,128]{3,2,1,0:T(8,128)(2,1)S(1)}, u32[]{:S(2)}, u32[]{:S(2)}) collective-permute-start(bf16[3,2,32,128]{3,2,1,0:T(8,128)(2,1)S(1)} %slice.13.refs_0_), channel_id=1, source_target_pairs={{0,16},{16,0},{1,17},{17,1},{2,18},{18,2},{3,19},{19,3},{4,20},{20... | collective-permute-start | bytes 147464 | tf_op jit(solution)/shard_map/ppermute | solution.py:29
  12.6 1.7 %collective-permute-start.6 = (bf16[1,2,32,128]{3,2,1,0:T(8,128)(2,1)S(1)}, bf16[1,2,32,128]{3,2,1,0:T(8,128)(2,1)S(1)}, u32[]{:S(2)}, u32[]{:S(2)}) collective-permute-start(bf16[1,2,32,128]{3,2,1,0:T(8,128)(2,1)S(1)} %slice.14.refs_0_), channel_id=1, source_target_pairs={{0,16},{16,0},{1,17},{17,1},{2,18},{18,2},{3,19},{19,3},{4,20},{20... | collective-permute-start | bytes 49160 | tf_op jit(solution)/shard_map/ppermute | solution.py:29
  14.3 0.0 collective-permute-done.3.other
  14.3 0.0 copy-done.1
  14.3 0.6 %copy-done.6 = f32[16]{0:T(128)S(1)} copy-done((f32[16]{0:T(128)S(1)}, f32[16]{0:T(128)}, u32[]{:S(2)}) %copy-start.6) | copy-done | bytes 88
  15.0 0.8 %own.1.swept = bf16[256,1024]{1,0:T(8,128)(2,1)S(1)} custom-call(f32[1,128]{1,0:T(1,128)S(1)} %get-tuple-element.21.weight, f32[1,16]{1,0:T(1,128)S(1)} %bitcast.21, s32[32,128]{1,0:T(8,128)S(1)} %bitcast.20, bf16[2,1024,128]{2,1,0:T(8,128)(2,1)S(1)} %copy-done.1, bf16[2,2,64,128]{3,2,1,0:T(8,128)(2,1)S(1)} %collective-permute-done.1.facing, ...), custom_call_target="tpu_custom_call" | custom-call | flops 575000000 | bytes 1 | tf_op jit(solution)/shard_map/own/pallas_call | solution.py:229
  15.8 0.0 collective-permute-done.4.refs_1_
  15.8 0.4 %cross.1 = (bf16[128,256]{1,0:T(8,128)(2,1)S(1)}, bf16[128,256]{1,0:T(8,128)(2,1)S(1)}) custom-call(bf16[256,1024]{1,0:T(8,128)(2,1)S(1)} %own.1.swept, bf16[2,1024,128]{2,1,0:T(8,128)(2,1)S(1)} %copy-done.1, bf16[2,1024,128]{2,1,0:T(8,128)(2,1)S(1)} %collective-permute-done.4.refs_1_), custom_call_target="tpu_custom_call" | custom-call | flops 1 | bytes 1 | tf_op jit(solution)/shard_map/cross/pallas_call | solution.py:244
  16.2 0.1 collective-permute-done.2.refs_1_
  16.4 0.2 send.1
  16.6 1.8 %collective-permute-start.5 = (bf16[2,32,128]{2,1,0:T(8,128)(2,1)S(1)}, bf16[2,32,128]{2,1,0:T(8,128)(2,1)S(1)}, u32[]{:S(2)}, u32[]{:S(2)}) collective-permute-start(bf16[2,32,128]{2,1,0:T(8,128)(2,1)S(1)} %get-tuple-element.28), channel_id=1, source_target_pairs={{0,4},{1,13},{2,6},{3,15},{4,8},{5,9},{6,10},{7,11},{8,12},{9,5},{... | collective-permute-start | bytes 49160 | tf_op jit(solution)/shard_map/ppermute | solution.py:46
  18.4 0.0 collective-permute-done.6.refs_1_
  18.4 0.5 %collective-permute-start.7 = (bf16[2,32,128]{2,1,0:T(8,128)(2,1)S(1)}, bf16[2,32,128]{2,1,0:T(8,128)(2,1)S(1)}, u32[]{:S(2)}, u32[]{:S(2)}) collective-permute-start(bf16[2,32,128]{2,1,0:T(8,128)(2,1)S(1)} %get-tuple-element.34), channel_id=1, source_target_pairs={{0,1},{1,9},{2,3},{3,11},{4,5},{5,4},{6,7},{7,6},{8,0},{9,8},{10,2... | collective-permute-start | bytes 49160 | tf_op jit(solution)/shard_map/ppermute | solution.py:46
  18.9 1.7 %collective-permute-start.8 = (bf16[2,32,128]{2,1,0:T(8,128)(2,1)S(1)}, bf16[2,32,128]{2,1,0:T(8,128)(2,1)S(1)}, u32[]{:S(2)}, u32[]{:S(2)}) collective-permute-start(bf16[2,32,128]{2,1,0:T(8,128)(2,1)S(1)} %get-tuple-element.35), channel_id=1, source_target_pairs={{0,12},{1,5},{2,14},{3,7},{4,0},{5,13},{6,2},{7,15},{8,4},{9,1},{1... | collective-permute-start | bytes 49160 | tf_op jit(solution)/shard_map/ppermute | solution.py:46
  20.6 0.8 %collective-permute-start.9 = (bf16[2,32,128]{2,1,0:T(8,128)(2,1)S(1)}, bf16[2,32,128]{2,1,0:T(8,128)(2,1)S(1)}, u32[]{:S(2)}, u32[]{:S(2)}) collective-permute-start(bf16[2,32,128]{2,1,0:T(8,128)(2,1)S(1)} %get-tuple-element.36), channel_id=1, source_target_pairs={{0,8},{1,0},{2,10},{3,2},{4,12},{5,1},{6,14},{7,3},{8,9},{9,13},{1... | collective-permute-start | bytes 49160 | tf_op jit(solution)/shard_map/ppermute | solution.py:46
  21.4 0.7 %collective-permute-done.5 = bf16[2,32,128]{2,1,0:T(8,128)(2,1)S(1)} collective-permute-done((bf16[2,32,128]{2,1,0:T(8,128)(2,1)S(1)}, bf16[2,32,128]{2,1,0:T(8,128)(2,1)S(1)}, u32[]{:S(2)}, u32[]{:S(2)}) %collective-permute-start.5) | collective-permute-done | bytes 16416 | tf_op jit(solution)/shard_map/ppermute | solution.py:46
  22.2 0.2 keep.1
  22.4 0.7 %collective-permute-done.7 = bf16[2,32,128]{2,1,0:T(8,128)(2,1)S(1)} collective-permute-done((bf16[2,32,128]{2,1,0:T(8,128)(2,1)S(1)}, bf16[2,32,128]{2,1,0:T(8,128)(2,1)S(1)}, u32[]{:S(2)}, u32[]{:S(2)}) %collective-permute-start.7) | collective-permute-done | bytes 16416 | tf_op jit(solution)/shard_map/ppermute | solution.py:46
  23.1 0.0 collective-permute-done.8
  23.1 0.0 collective-permute-done.9
  23.1 0.6 %add_bitcast_fusion = f32[2,128,32]{1,2,0:T(8,128)} fusion(f32[2,32,128]{2,1,0:T(8,128)S(1)} %convert_add_fusion, bf16[2,32,128]{2,1,0:T(8,128)(2,1)S(1)} %collective-permute-done.9, pred[]{:T(512)S(6)} %and.58, pred[]{:T(512)S(6)} %and.57), kind=kLoop, calls=%fused_computation.2 | loop fusion | flops 32768 | bytes 81922 | tf_op jit(solution)/shard_map/transpose | solution.py:282
  (16 shorter events, 0.1 us)
Async XLA Ops:
  0.0 5.6 %copy-start.3 = (f32[4,8]{1,0:T(4,128)S(1)}, f32[4,8]{1,0:T(4,128)}, u32[]{:S(2)}) copy-start(f32[4,8]{1,0:T(4,128)} %noise.1) | copy-start | bytes 388
  0.0 15.8 %collective-permute-start.4 = (bf16[2,1024,128]{2,1,0:T(8,128)(2,1)}, bf16[2,1024,128]{2,1,0:T(8,128)(2,1)S(1)}, u32[]{:S(2)}, u32[]{:S(2)}) collective-permute-start(bf16[2,1024,128]{2,1,0:T(8,128)(2,1)} %refs_0_.1), channel_id=1, source_target_pairs={{0,16},{16,0},{1,17},{17,1},{2,18},{18,2},{3,19},{19,3},{4,20},{20... | collective-permute-start | bytes 1572872 | tf_op jit(solution)/shard_map/ppermute | solution.py:29
  3.0 2.6 %copy-start.4 = (s32[128]{0:T(128)S(1)}, s32[128]{0:T(128)}, u32[]{:S(2)}) copy-start(s32[128]{0:T(128)} %param.9) | copy-start | bytes 1540
  3.0 4.8 %collective-permute-start = (bf16[2,32,128]{2,1,0:T(8,128)(2,1)}, bf16[2,32,128]{2,1,0:T(8,128)(2,1)S(1)}, u32[]{:S(2)}, u32[]{:S(2)}) collective-permute-start(bf16[2,32,128]{2,1,0:T(8,128)(2,1)} %bitcast.16), channel_id=1, source_target_pairs={{0,8},{1,9},{2,10},{3,11},{4,12},{5,13},{6,14},{7,15},{8,0},{9,1},... | collective-permute-start | bytes 49160 | tf_op jit(solution)/shard_map/ppermute | solution.py:24
  5.6 1.0 %copy-start = (bf16[2,1024,128]{2,1,0:T(8,128)(2,1)S(1)}, bf16[2,1024,128]{2,1,0:T(8,128)(2,1)}, u32[]{:S(2)}) copy-start(bf16[2,1024,128]{2,1,0:T(8,128)(2,1)} %refs_0_.1) | copy-start | bytes 1572868
  6.6 0.7 %copy-start.2 = (bf16[2,128,32]{1,2,0:T(8,128)(2,1)S(1)}, bf16[2,128,32]{1,2,0:T(8,128)(2,1)}, u32[]{:S(2)}) copy-start(bf16[2,128,32]{1,2,0:T(8,128)(2,1)} %param.6) | copy-start | bytes 49156
  7.3 7.0 %copy-start.1 = (bf16[2,1024,128]{2,1,0:T(8,128)(2,1)S(1)}, bf16[2,1024,128]{2,1,0:T(8,128)(2,1)}, u32[]{:S(2)}) copy-start(bf16[2,1024,128]{2,1,0:T(8,128)(2,1)} %refs_0_.1) | copy-start | bytes 1572868
  7.8 4.3 %collective-permute-start.1 = (bf16[2,2,64,128]{3,2,1,0:T(8,128)(2,1)S(1)}, bf16[2,2,64,128]{3,2,1,0:T(8,128)(2,1)S(1)}, u32[]{:S(2)}, u32[]{:S(2)}) collective-permute-start(bf16[2,2,64,128]{3,2,1,0:T(8,128)(2,1)S(1)} %pad_maximum_fusion), channel_id=1, source_target_pairs={{0,4},{1,5},{2,6},{3,7},{4,0},{5,1},{6,2},{7,3},{8,12},{9,13},{10,... | collective-permute-start | bytes 196616 | tf_op jit(solution)/shard_map/ppermute | solution.py:24
  9.5 4.8 %collective-permute-start.3 = (bf16[2,64,128]{2,1,0:T(8,128)(2,1)S(1)}, bf16[2,64,128]{2,1,0:T(8,128)(2,1)S(1)}, u32[]{:S(2)}, u32[]{:S(2)}) collective-permute-start(bf16[2,64,128]{2,1,0:T(8,128)(2,1)S(1)} %get-tuple-element.25), channel_id=1, source_target_pairs={{0,1},{1,0},{2,3},{3,2},{4,8},{5,9},{6,10},{7,11},{8,4},{9,5},{10,... | collective-permute-start | bytes 98312 | tf_op jit(solution)/shard_map/ppermute | solution.py:38
  12.2 2.1 %copy-start.5 = (s32[4096]{0:T(1024)S(1)}, s32[4096]{0:T(1024)}, u32[]{:S(2)}) copy-start(s32[4096]{0:T(1024)} %param.11) | copy-start | bytes 49156
  12.2 4.2 %collective-permute-start.2 = (bf16[3,2,32,128]{3,2,1,0:T(8,128)(2,1)S(1)}, bf16[3,2,32,128]{3,2,1,0:T(8,128)(2,1)S(1)}, u32[]{:S(2)}, u32[]{:S(2)}) collective-permute-start(bf16[3,2,32,128]{3,2,1,0:T(8,128)(2,1)S(1)} %slice.13.refs_0_), channel_id=1, source_target_pairs={{0,16},{16,0},{1,17},{17,1},{2,18},{18,2},{3,19},{19,3},{4,20},{20... | collective-permute-start | bytes 147464 | tf_op jit(solution)/shard_map/ppermute | solution.py:29
  12.6 5.8 %collective-permute-start.6 = (bf16[1,2,32,128]{3,2,1,0:T(8,128)(2,1)S(1)}, bf16[1,2,32,128]{3,2,1,0:T(8,128)(2,1)S(1)}, u32[]{:S(2)}, u32[]{:S(2)}) collective-permute-start(bf16[1,2,32,128]{3,2,1,0:T(8,128)(2,1)S(1)} %slice.14.refs_0_), channel_id=1, source_target_pairs={{0,16},{16,0},{1,17},{17,1},{2,18},{18,2},{3,19},{19,3},{4,20},{20... | collective-permute-start | bytes 49160 | tf_op jit(solution)/shard_map/ppermute | solution.py:29
  14.3 0.7 %copy-start.6 = (f32[16]{0:T(128)S(1)}, f32[16]{0:T(128)}, u32[]{:S(2)}) copy-start(f32[16]{0:T(128)} %param.10) | copy-start | bytes 196
  16.6 5.6 %collective-permute-start.5 = (bf16[2,32,128]{2,1,0:T(8,128)(2,1)S(1)}, bf16[2,32,128]{2,1,0:T(8,128)(2,1)S(1)}, u32[]{:S(2)}, u32[]{:S(2)}) collective-permute-start(bf16[2,32,128]{2,1,0:T(8,128)(2,1)S(1)} %get-tuple-element.28), channel_id=1, source_target_pairs={{0,4},{1,13},{2,6},{3,15},{4,8},{5,9},{6,10},{7,11},{8,12},{9,5},{... | collective-permute-start | bytes 49160 | tf_op jit(solution)/shard_map/ppermute | solution.py:46
  18.4 4.7 %collective-permute-start.7 = (bf16[2,32,128]{2,1,0:T(8,128)(2,1)S(1)}, bf16[2,32,128]{2,1,0:T(8,128)(2,1)S(1)}, u32[]{:S(2)}, u32[]{:S(2)}) collective-permute-start(bf16[2,32,128]{2,1,0:T(8,128)(2,1)S(1)} %get-tuple-element.34), channel_id=1, source_target_pairs={{0,1},{1,9},{2,3},{3,11},{4,5},{5,4},{6,7},{7,6},{8,0},{9,8},{10,2... | collective-permute-start | bytes 49160 | tf_op jit(solution)/shard_map/ppermute | solution.py:46
  18.9 4.1 %collective-permute-start.8 = (bf16[2,32,128]{2,1,0:T(8,128)(2,1)S(1)}, bf16[2,32,128]{2,1,0:T(8,128)(2,1)S(1)}, u32[]{:S(2)}, u32[]{:S(2)}) collective-permute-start(bf16[2,32,128]{2,1,0:T(8,128)(2,1)S(1)} %get-tuple-element.35), channel_id=1, source_target_pairs={{0,12},{1,5},{2,14},{3,7},{4,0},{5,13},{6,2},{7,15},{8,4},{9,1},{1... | collective-permute-start | bytes 49160 | tf_op jit(solution)/shard_map/ppermute | solution.py:46
  20.6 2.5 %collective-permute-start.9 = (bf16[2,32,128]{2,1,0:T(8,128)(2,1)S(1)}, bf16[2,32,128]{2,1,0:T(8,128)(2,1)S(1)}, u32[]{:S(2)}, u32[]{:S(2)}) collective-permute-start(bf16[2,32,128]{2,1,0:T(8,128)(2,1)S(1)} %get-tuple-element.36), channel_id=1, source_target_pairs={{0,8},{1,0},{2,10},{3,2},{4,12},{5,1},{6,14},{7,3},{8,9},{9,13},{1... | collective-permute-start | bytes 49160 | tf_op jit(solution)/shard_map/ppermute | solution.py:46

commit v10 on v9

--- a/solution.py
+++ b/solution.py
@@ -10,7 +10,7 @@
 SPLIT = 4
 DIP = 32
 LANES = 128
-ROUTES = (((1, 2, 3, 0), (3, 2, 1, 0)), ((-1, -1, 0, -1), (2, -1, -1, -1)), ((3, 0, 1, 2), (1, 3, 0, 2)), ((2, 3, -1, 1), (-1, 0, 3, 1)))
+ROUTES = (((-1, -1, 0, -1), (2, -1, -1, -1)), ((1, 2, 3, 0), (1, 3, 0, 2)), ((3, 0, 1, 2), (3, 2, 1, 0)), ((2, 3, -1, 1), (-1, 0, 3, 1)))
 PLACE = (0, 1, 0, 2)
 REACH = 2 * DIP
 F32 = jnp.float32

time: 24 us -> 23.9 us (level)
  no operation moved by 1% of the time
where the time goes in v10:
time: 23.9 us; the launch traced here: 23.7 us
  starting transfers between devices  14.2 us (59%)
  waiting for transfers between devices  4.51 us (19%)
  local copies, waits for them, and re-layouts  2.44 us (10%)
  Pallas kernels  1.67 us (7%)
  other arithmetic  0.68 us (3%)
    ppermute x3, starting transfers between devices, turned(): lax.ppermute(value, axis, [(i, (i + step) % size) for i in range(size)])  5.06 us
    ppermute x4, starting transfers between devices, routed(): return lax.ppermute(value, axis, pairs)  4.95 us
    ppermute x2, starting transfers between devices, swapped(): lax.ppermute(value, axis, [(i, i ^ mask) for i in range(lax.axis_size(axi...  4.23 us
    ppermute x2, waiting for transfers between devices, swapped(): lax.ppermute(value, axis, [(i, i ^ mask) for i in range(lax.axis_size(axi...  3.09 us
    unnamed x14, local copies, waits for them, and re-layouts  2.42 us
    ppermute x4, waiting for transfers between devices, routed(): return lax.ppermute(value, axis, pairs)  1.23 us
    pallas_call x1, Pallas kernels, shards(): pl.pallas_call(functools.partial(own_kernel, nfreq), out_shape=jax.ShapeD...  0.78 us
    transpose x1, other arithmetic, shards(): return jnp.transpose(keep, (0, 2, 1))  0.62 us
  transfers between devices with their start and end apart: 10, of which 5 were waited for; matrix products, arithmetic and copies ran while one was open for 0% of the time, Pallas kernels for 6%

profile of v10, /device:TPU:0, one launch (start us, length us, event | category | flops | bytes accessed | tf_op | source)
XLA Modules:
  0.0 23.7 jit_solution(15244505975831297565)
XLA Ops:
  0.0 3.0 %collective-permute-start.4 = (bf16[2,1024,128]{2,1,0:T(8,128)(2,1)}, bf16[2,1024,128]{2,1,0:T(8,128)(2,1)S(1)}, u32[]{:S(2)}, u32[]{:S(2)}) collective-permute-start(bf16[2,1024,128]{2,1,0:T(8,128)(2,1)} %refs_0_.1), channel_id=1, source_target_pairs={{0,16},{16,0},{1,17},{17,1},{2,18},{18,2},{3,19},{19,3},{4,20},{20... | collective-permute-start | bytes 1572872 | tf_op jit(solution)/shard_map/ppermute | solution.py:29
  3.0 2.6 %collective-permute-start = (bf16[2,32,128]{2,1,0:T(8,128)(2,1)}, bf16[2,32,128]{2,1,0:T(8,128)(2,1)S(1)}, u32[]{:S(2)}, u32[]{:S(2)}) collective-permute-start(bf16[2,32,128]{2,1,0:T(8,128)(2,1)} %bitcast.16), channel_id=1, source_target_pairs={{0,8},{1,9},{2,10},{3,11},{4,12},{5,13},{6,14},{7,15},{8,0},{9,1},... | collective-permute-start | bytes 49160 | tf_op jit(solution)/shard_map/ppermute | solution.py:24
  5.6 0.0 copy-done.4
  5.6 1.0 %copy-done = bf16[2,1024,128]{2,1,0:T(8,128)(2,1)S(1)} copy-done((bf16[2,1024,128]{2,1,0:T(8,128)(2,1)S(1)}, bf16[2,1024,128]{2,1,0:T(8,128)(2,1)}, u32[]{:S(2)}) %copy-start) | copy-done | bytes 524312
  6.6 0.7 %copy-done.2 = bf16[2,128,32]{1,2,0:T(8,128)(2,1)S(1)} copy-done((bf16[2,128,32]{1,2,0:T(8,128)(2,1)S(1)}, bf16[2,128,32]{1,2,0:T(8,128)(2,1)}, u32[]{:S(2)}) %copy-start.2) | copy-done | bytes 16408
  7.3 0.1 prep.1
  7.4 0.4 %collective-permute-done = bf16[2,32,128]{2,1,0:T(8,128)(2,1)S(1)} collective-permute-done((bf16[2,32,128]{2,1,0:T(8,128)(2,1)}, bf16[2,32,128]{2,1,0:T(8,128)(2,1)S(1)}, u32[]{:S(2)}, u32[]{:S(2)}) %collective-permute-start) | collective-permute-done | bytes 16416 | tf_op jit(solution)/shard_map/ppermute | solution.py:24
  7.8 1.6 %collective-permute-start.1 = (bf16[2,2,64,128]{3,2,1,0:T(8,128)(2,1)S(1)}, bf16[2,2,64,128]{3,2,1,0:T(8,128)(2,1)S(1)}, u32[]{:S(2)}, u32[]{:S(2)}) collective-permute-start(bf16[2,2,64,128]{3,2,1,0:T(8,128)(2,1)S(1)} %pad_maximum_fusion), channel_id=1, source_target_pairs={{0,4},{1,5},{2,6},{3,7},{4,0},{5,1},{6,2},{7,3},{8,12},{9,13},{10,... | collective-permute-start | bytes 196616 | tf_op jit(solution)/shard_map/ppermute | solution.py:24
  9.5 0.0 collective-permute-start.3
  9.5 2.7 %collective-permute-done.1.facing = bf16[2,2,64,128]{3,2,1,0:T(8,128)(2,1)S(1)} collective-permute-done((bf16[2,2,64,128]{3,2,1,0:T(8,128)(2,1)S(1)}, bf16[2,2,64,128]{3,2,1,0:T(8,128)(2,1)S(1)}, u32[]{:S(2)}, u32[]{:S(2)}) %collective-permute-start.1) | collective-permute-done | bytes 65568 | tf_op jit(solution)/shard_map/ppermute | solution.py:24
  12.2 0.0 copy-start.5
  12.2 0.3 %collective-permute-start.2 = (bf16[3,2,32,128]{3,2,1,0:T(8,128)(2,1)S(1)}, bf16[3,2,32,128]{3,2,1,0:T(8,128)(2,1)S(1)}, u32[]{:S(2)}, u32[]{:S(2)}) collective-permute-start(bf16[3,2,32,128]{3,2,1,0:T(8,128)(2,1)S(1)} %slice.13.refs_0_), channel_id=1, source_target_pairs={{0,16},{16,0},{1,17},{17,1},{2,18},{18,2},{3,19},{19,3},{4,20},{20... | collective-permute-start | bytes 147464 | tf_op jit(solution)/shard_map/ppermute | solution.py:29
  12.6 1.7 %collective-permute-start.6 = (bf16[1,2,32,128]{3,2,1,0:T(8,128)(2,1)S(1)}, bf16[1,2,32,128]{3,2,1,0:T(8,128)(2,1)S(1)}, u32[]{:S(2)}, u32[]{:S(2)}) collective-permute-start(bf16[1,2,32,128]{3,2,1,0:T(8,128)(2,1)S(1)} %slice.14.refs_0_), channel_id=1, source_target_pairs={{0,16},{16,0},{1,17},{17,1},{2,18},{18,2},{3,19},{19,3},{4,20},{20... | collective-permute-start | bytes 49160 | tf_op jit(solution)/shard_map/ppermute | solution.py:29
  14.3 0.0 collective-permute-done.3.other
  14.3 0.0 copy-done.5
  14.3 0.6 %copy-done.6 = f32[16]{0:T(128)S(1)} copy-done((f32[16]{0:T(128)S(1)}, f32[16]{0:T(128)}, u32[]{:S(2)}) %copy-start.6) | copy-done | bytes 88
  15.0 0.8 %own.1.swept = bf16[256,1024]{1,0:T(8,128)(2,1)S(1)} custom-call(f32[1,128]{1,0:T(1,128)S(1)} %get-tuple-element.21.weight, f32[1,16]{1,0:T(1,128)S(1)} %bitcast.21, s32[32,128]{1,0:T(8,128)S(1)} %bitcast.20, bf16[2,1024,128]{2,1,0:T(8,128)(2,1)S(1)} %copy-done.1, bf16[2,2,64,128]{3,2,1,0:T(8,128)(2,1)S(1)} %collective-permute-done.1.facing, ...), custom_call_target="tpu_custom_call" | custom-call | flops 575000000 | bytes 1 | tf_op jit(solution)/shard_map/own/pallas_call | solution.py:229
  15.8 0.0 collective-permute-done.4.refs_1_
  15.8 0.4 %cross.1 = (bf16[128,256]{1,0:T(8,128)(2,1)S(1)}, bf16[128,256]{1,0:T(8,128)(2,1)S(1)}) custom-call(bf16[256,1024]{1,0:T(8,128)(2,1)S(1)} %own.1.swept, bf16[2,1024,128]{2,1,0:T(8,128)(2,1)S(1)} %copy-done.1, bf16[2,1024,128]{2,1,0:T(8,128)(2,1)S(1)} %collective-permute-done.4.refs_1_), custom_call_target="tpu_custom_call" | custom-call | flops 1 | bytes 1 | tf_op jit(solution)/shard_map/cross/pallas_call | solution.py:244
  16.2 0.1 collective-permute-done.2.refs_1_
  16.4 0.2 send.1
  16.6 0.1 collective-permute-start.5
  16.7 0.0 collective-permute-done.6.refs_1_
  16.7 1.8 %collective-permute-start.7 = (bf16[2,32,128]{2,1,0:T(8,128)(2,1)S(1)}, bf16[2,32,128]{2,1,0:T(8,128)(2,1)S(1)}, u32[]{:S(2)}, u32[]{:S(2)}) collective-permute-start(bf16[2,32,128]{2,1,0:T(8,128)(2,1)S(1)} %get-tuple-element.34), channel_id=1, source_target_pairs={{0,4},{1,5},{2,6},{3,7},{4,8},{5,13},{6,10},{7,15},{8,12},{9,1},{1... | collective-permute-start | bytes 49160 | tf_op jit(solution)/shard_map/ppermute | solution.py:46
  18.6 2.1 %collective-permute-start.8 = (bf16[2,32,128]{2,1,0:T(8,128)(2,1)S(1)}, bf16[2,32,128]{2,1,0:T(8,128)(2,1)S(1)}, u32[]{:S(2)}, u32[]{:S(2)}) collective-permute-start(bf16[2,32,128]{2,1,0:T(8,128)(2,1)S(1)} %get-tuple-element.35), channel_id=1, source_target_pairs={{0,12},{1,13},{2,14},{3,15},{4,0},{5,9},{6,2},{7,11},{8,4},{9,5},{... | collective-permute-start | bytes 49160 | tf_op jit(solution)/shard_map/ppermute | solution.py:46
  20.6 1.0 %collective-permute-start.9 = (bf16[2,32,128]{2,1,0:T(8,128)(2,1)S(1)}, bf16[2,32,128]{2,1,0:T(8,128)(2,1)S(1)}, u32[]{:S(2)}, u32[]{:S(2)}) collective-permute-start(bf16[2,32,128]{2,1,0:T(8,128)(2,1)S(1)} %get-tuple-element.36), channel_id=1, source_target_pairs={{0,8},{1,0},{2,10},{3,2},{4,12},{5,1},{6,14},{7,3},{8,9},{9,13},{1... | collective-permute-start | bytes 49160 | tf_op jit(solution)/shard_map/ppermute | solution.py:46
  21.6 0.0 collective-permute-done.5
  21.6 0.2 keep.1
  21.8 0.6 %collective-permute-done.7 = bf16[2,32,128]{2,1,0:T(8,128)(2,1)S(1)} collective-permute-done((bf16[2,32,128]{2,1,0:T(8,128)(2,1)S(1)}, bf16[2,32,128]{2,1,0:T(8,128)(2,1)S(1)}, u32[]{:S(2)}, u32[]{:S(2)}) %collective-permute-start.7) | collective-permute-done | bytes 16416 | tf_op jit(solution)/shard_map/ppermute | solution.py:46
  22.4 0.0 collective-permute-done.8
  22.5 0.6 %collective-permute-done.9 = bf16[2,32,128]{2,1,0:T(8,128)(2,1)S(1)} collective-permute-done((bf16[2,32,128]{2,1,0:T(8,128)(2,1)S(1)}, bf16[2,32,128]{2,1,0:T(8,128)(2,1)S(1)}, u32[]{:S(2)}, u32[]{:S(2)}) %collective-permute-start.9) | collective-permute-done | bytes 16416 | tf_op jit(solution)/shard_map/ppermute | solution.py:46
  23.1 0.6 %add_bitcast_fusion = f32[2,128,32]{1,2,0:T(8,128)} fusion(f32[2,32,128]{2,1,0:T(8,128)S(1)} %convert_add_fusion, bf16[2,32,128]{2,1,0:T(8,128)(2,1)S(1)} %collective-permute-done.9, pred[]{:T(512)S(6)} %and.58, pred[]{:T(512)S(6)} %and.57), kind=kLoop, calls=%fused_computation.2 | loop fusion | flops 32768 | bytes 81922 | tf_op jit(solution)/shard_map/transpose | solution.py:282
  (16 shorter events, 0.1 us)
Async XLA Ops:
  0.0 5.6 %copy-start.3 = (f32[4,8]{1,0:T(4,128)S(1)}, f32[4,8]{1,0:T(4,128)}, u32[]{:S(2)}) copy-start(f32[4,8]{1,0:T(4,128)} %noise.1) | copy-start | bytes 388
  0.0 15.8 %collective-permute-start.4 = (bf16[2,1024,128]{2,1,0:T(8,128)(2,1)}, bf16[2,1024,128]{2,1,0:T(8,128)(2,1)S(1)}, u32[]{:S(2)}, u32[]{:S(2)}) collective-permute-start(bf16[2,1024,128]{2,1,0:T(8,128)(2,1)} %refs_0_.1), channel_id=1, source_target_pairs={{0,16},{16,0},{1,17},{17,1},{2,18},{18,2},{3,19},{19,3},{4,20},{20... | collective-permute-start | bytes 1572872 | tf_op jit(solution)/shard_map/ppermute | solution.py:29
  3.0 2.6 %copy-start.4 = (s32[128]{0:T(128)S(1)}, s32[128]{0:T(128)}, u32[]{:S(2)}) copy-start(s32[128]{0:T(128)} %param.9) | copy-start | bytes 1540
  3.0 4.8 %collective-permute-start = (bf16[2,32,128]{2,1,0:T(8,128)(2,1)}, bf16[2,32,128]{2,1,0:T(8,128)(2,1)S(1)}, u32[]{:S(2)}, u32[]{:S(2)}) collective-permute-start(bf16[2,32,128]{2,1,0:T(8,128)(2,1)} %bitcast.16), channel_id=1, source_target_pairs={{0,8},{1,9},{2,10},{3,11},{4,12},{5,13},{6,14},{7,15},{8,0},{9,1},... | collective-permute-start | bytes 49160 | tf_op jit(solution)/shard_map/ppermute | solution.py:24
  5.6 1.0 %copy-start = (bf16[2,1024,128]{2,1,0:T(8,128)(2,1)S(1)}, bf16[2,1024,128]{2,1,0:T(8,128)(2,1)}, u32[]{:S(2)}) copy-start(bf16[2,1024,128]{2,1,0:T(8,128)(2,1)} %refs_0_.1) | copy-start | bytes 1572868
  6.6 0.7 %copy-start.2 = (bf16[2,128,32]{1,2,0:T(8,128)(2,1)S(1)}, bf16[2,128,32]{1,2,0:T(8,128)(2,1)}, u32[]{:S(2)}) copy-start(bf16[2,128,32]{1,2,0:T(8,128)(2,1)} %param.6) | copy-start | bytes 49156
  7.3 7.0 %copy-start.1 = (bf16[2,1024,128]{2,1,0:T(8,128)(2,1)S(1)}, bf16[2,1024,128]{2,1,0:T(8,128)(2,1)}, u32[]{:S(2)}) copy-start(bf16[2,1024,128]{2,1,0:T(8,128)(2,1)} %refs_0_.1) | copy-start | bytes 1572868
  7.8 4.3 %collective-permute-start.1 = (bf16[2,2,64,128]{3,2,1,0:T(8,128)(2,1)S(1)}, bf16[2,2,64,128]{3,2,1,0:T(8,128)(2,1)S(1)}, u32[]{:S(2)}, u32[]{:S(2)}) collective-permute-start(bf16[2,2,64,128]{3,2,1,0:T(8,128)(2,1)S(1)} %pad_maximum_fusion), channel_id=1, source_target_pairs={{0,4},{1,5},{2,6},{3,7},{4,0},{5,1},{6,2},{7,3},{8,12},{9,13},{10,... | collective-permute-start | bytes 196616 | tf_op jit(solution)/shard_map/ppermute | solution.py:24
  9.5 4.8 %collective-permute-start.3 = (bf16[2,64,128]{2,1,0:T(8,128)(2,1)S(1)}, bf16[2,64,128]{2,1,0:T(8,128)(2,1)S(1)}, u32[]{:S(2)}, u32[]{:S(2)}) collective-permute-start(bf16[2,64,128]{2,1,0:T(8,128)(2,1)S(1)} %get-tuple-element.25), channel_id=1, source_target_pairs={{0,1},{1,0},{2,3},{3,2},{4,8},{5,9},{6,10},{7,11},{8,4},{9,5},{10,... | collective-permute-start | bytes 98312 | tf_op jit(solution)/shard_map/ppermute | solution.py:38
  12.2 2.1 %copy-start.5 = (s32[4096]{0:T(1024)S(1)}, s32[4096]{0:T(1024)}, u32[]{:S(2)}) copy-start(s32[4096]{0:T(1024)} %param.11) | copy-start | bytes 49156
  12.2 4.2 %collective-permute-start.2 = (bf16[3,2,32,128]{3,2,1,0:T(8,128)(2,1)S(1)}, bf16[3,2,32,128]{3,2,1,0:T(8,128)(2,1)S(1)}, u32[]{:S(2)}, u32[]{:S(2)}) collective-permute-start(bf16[3,2,32,128]{3,2,1,0:T(8,128)(2,1)S(1)} %slice.13.refs_0_), channel_id=1, source_target_pairs={{0,16},{16,0},{1,17},{17,1},{2,18},{18,2},{3,19},{19,3},{4,20},{20... | collective-permute-start | bytes 147464 | tf_op jit(solution)/shard_map/ppermute | solution.py:29
  12.6 4.1 %collective-permute-start.6 = (bf16[1,2,32,128]{3,2,1,0:T(8,128)(2,1)S(1)}, bf16[1,2,32,128]{3,2,1,0:T(8,128)(2,1)S(1)}, u32[]{:S(2)}, u32[]{:S(2)}) collective-permute-start(bf16[1,2,32,128]{3,2,1,0:T(8,128)(2,1)S(1)} %slice.14.refs_0_), channel_id=1, source_target_pairs={{0,16},{16,0},{1,17},{17,1},{2,18},{18,2},{3,19},{19,3},{4,20},{20... | collective-permute-start | bytes 49160 | tf_op jit(solution)/shard_map/ppermute | solution.py:29
  14.3 0.7 %copy-start.6 = (f32[16]{0:T(128)S(1)}, f32[16]{0:T(128)}, u32[]{:S(2)}) copy-start(f32[16]{0:T(128)} %param.10) | copy-start | bytes 196
  16.6 5.0 %collective-permute-start.5 = (bf16[2,32,128]{2,1,0:T(8,128)(2,1)S(1)}, bf16[2,32,128]{2,1,0:T(8,128)(2,1)S(1)}, u32[]{:S(2)}, u32[]{:S(2)}) collective-permute-start(bf16[2,32,128]{2,1,0:T(8,128)(2,1)S(1)} %get-tuple-element.28), channel_id=1, source_target_pairs={{0,1},{1,9},{2,3},{3,11},{4,5},{5,4},{6,7},{7,6},{8,0},{9,8},{10,2... | collective-permute-start | bytes 49160 | tf_op jit(solution)/shard_map/ppermute | solution.py:46
  16.7 5.7 %collective-permute-start.7 = (bf16[2,32,128]{2,1,0:T(8,128)(2,1)S(1)}, bf16[2,32,128]{2,1,0:T(8,128)(2,1)S(1)}, u32[]{:S(2)}, u32[]{:S(2)}) collective-permute-start(bf16[2,32,128]{2,1,0:T(8,128)(2,1)S(1)} %get-tuple-element.34), channel_id=1, source_target_pairs={{0,4},{1,5},{2,6},{3,7},{4,8},{5,13},{6,10},{7,15},{8,12},{9,1},{1... | collective-permute-start | bytes 49160 | tf_op jit(solution)/shard_map/ppermute | solution.py:46
  18.6 3.9 %collective-permute-start.8 = (bf16[2,32,128]{2,1,0:T(8,128)(2,1)S(1)}, bf16[2,32,128]{2,1,0:T(8,128)(2,1)S(1)}, u32[]{:S(2)}, u32[]{:S(2)}) collective-permute-start(bf16[2,32,128]{2,1,0:T(8,128)(2,1)S(1)} %get-tuple-element.35), channel_id=1, source_target_pairs={{0,12},{1,13},{2,14},{3,15},{4,0},{5,9},{6,2},{7,11},{8,4},{9,5},{... | collective-permute-start | bytes 49160 | tf_op jit(solution)/shard_map/ppermute | solution.py:46
  20.6 2.4 %collective-permute-start.9 = (bf16[2,32,128]{2,1,0:T(8,128)(2,1)S(1)}, bf16[2,32,128]{2,1,0:T(8,128)(2,1)S(1)}, u32[]{:S(2)}, u32[]{:S(2)}) collective-permute-start(bf16[2,32,128]{2,1,0:T(8,128)(2,1)S(1)} %get-tuple-element.36), channel_id=1, source_target_pairs={{0,8},{1,0},{2,10},{3,2},{4,12},{5,1},{6,14},{7,3},{8,9},{9,13},{1... | collective-permute-start | bytes 49160 | tf_op jit(solution)/shard_map/ppermute | solution.py:46

commit v11 on v10

--- a/solution.py
+++ b/solution.py
@@ -258,7 +258,7 @@
         compiler_params=PARAMS,
         name="send",
     )(given, *rests[0], *pairs))
-    sends[2], rests[1] = lax.optimization_barrier((sends[2], rests[1]))
+    sends[1], rests[1] = lax.optimization_barrier((sends[1], rests[1]))
     shares = [routed(send, "par", nfreq, step) for send, step in zip(sends, ROUTES)]
     shares[0], kept = lax.optimization_barrier((shares[0], kept))
     keep = pl.pallas_call(

time: 23.9 us -> 23.9 us (level)
  no operation moved by 1% of the time
where the time goes in v11:
time: 23.9 us; the launch traced here: 23.7 us
  starting transfers between devices  14.2 us (59%)
  waiting for transfers between devices  4.51 us (19%)
  local copies, waits for them, and re-layouts  2.44 us (10%)
  Pallas kernels  1.67 us (7%)
  other arithmetic  0.68 us (3%)
    ppermute x3, starting transfers between devices, turned(): lax.ppermute(value, axis, [(i, (i + step) % size) for i in range(size)])  5.06 us
    ppermute x4, starting transfers between devices, routed(): return lax.ppermute(value, axis, pairs)  4.95 us
    ppermute x2, starting transfers between devices, swapped(): lax.ppermute(value, axis, [(i, i ^ mask) for i in range(lax.axis_size(axi...  4.23 us
    ppermute x2, waiting for transfers between devices, swapped(): lax.ppermute(value, axis, [(i, i ^ mask) for i in range(lax.axis_size(axi...  3.09 us
    unnamed x14, local copies, waits for them, and re-layouts  2.42 us
    ppermute x4, waiting for transfers between devices, routed(): return lax.ppermute(value, axis, pairs)  1.23 us
    pallas_call x1, Pallas kernels, shards(): pl.pallas_call(functools.partial(own_kernel, nfreq), out_shape=jax.ShapeD...  0.78 us
    transpose x1, other arithmetic, shards(): return jnp.transpose(keep, (0, 2, 1))  0.62 us
  transfers between devices with their start and end apart: 10, of which 5 were waited for; matrix products, arithmetic and copies ran while one was open for 0% of the time, Pallas kernels for 6%

profile of v11, /device:TPU:0, one launch (start us, length us, event | category | flops | bytes accessed | tf_op | source)
XLA Modules:
  0.0 23.7 jit_solution(10331161042093459262)
XLA Ops:
  0.0 3.0 %collective-permute-start.4 = (bf16[2,1024,128]{2,1,0:T(8,128)(2,1)}, bf16[2,1024,128]{2,1,0:T(8,128)(2,1)S(1)}, u32[]{:S(2)}, u32[]{:S(2)}) collective-permute-start(bf16[2,1024,128]{2,1,0:T(8,128)(2,1)} %refs_0_.1), channel_id=1, source_target_pairs={{0,16},{16,0},{1,17},{17,1},{2,18},{18,2},{3,19},{19,3},{4,20},{20... | collective-permute-start | bytes 1572872 | tf_op jit(solution)/shard_map/ppermute | solution.py:29
  3.0 2.6 %collective-permute-start = (bf16[2,32,128]{2,1,0:T(8,128)(2,1)}, bf16[2,32,128]{2,1,0:T(8,128)(2,1)S(1)}, u32[]{:S(2)}, u32[]{:S(2)}) collective-permute-start(bf16[2,32,128]{2,1,0:T(8,128)(2,1)} %bitcast.16), channel_id=1, source_target_pairs={{0,8},{1,9},{2,10},{3,11},{4,12},{5,13},{6,14},{7,15},{8,0},{9,1},... | collective-permute-start | bytes 49160 | tf_op jit(solution)/shard_map/ppermute | solution.py:24
  5.6 0.0 copy-done.4
  5.6 1.0 %copy-done = bf16[2,1024,128]{2,1,0:T(8,128)(2,1)S(1)} copy-done((bf16[2,1024,128]{2,1,0:T(8,128)(2,1)S(1)}, bf16[2,1024,128]{2,1,0:T(8,128)(2,1)}, u32[]{:S(2)}) %copy-start) | copy-done | bytes 524312
  6.6 0.7 %copy-done.2 = bf16[2,128,32]{1,2,0:T(8,128)(2,1)S(1)} copy-done((bf16[2,128,32]{1,2,0:T(8,128)(2,1)S(1)}, bf16[2,128,32]{1,2,0:T(8,128)(2,1)}, u32[]{:S(2)}) %copy-start.2) | copy-done | bytes 16408
  7.3 0.1 prep.1
  7.4 0.4 %collective-permute-done = bf16[2,32,128]{2,1,0:T(8,128)(2,1)S(1)} collective-permute-done((bf16[2,32,128]{2,1,0:T(8,128)(2,1)}, bf16[2,32,128]{2,1,0:T(8,128)(2,1)S(1)}, u32[]{:S(2)}, u32[]{:S(2)}) %collective-permute-start) | collective-permute-done | bytes 16416 | tf_op jit(solution)/shard_map/ppermute | solution.py:24
  7.8 1.6 %collective-permute-start.1 = (bf16[2,2,64,128]{3,2,1,0:T(8,128)(2,1)S(1)}, bf16[2,2,64,128]{3,2,1,0:T(8,128)(2,1)S(1)}, u32[]{:S(2)}, u32[]{:S(2)}) collective-permute-start(bf16[2,2,64,128]{3,2,1,0:T(8,128)(2,1)S(1)} %pad_maximum_fusion), channel_id=1, source_target_pairs={{0,4},{1,5},{2,6},{3,7},{4,0},{5,1},{6,2},{7,3},{8,12},{9,13},{10,... | collective-permute-start | bytes 196616 | tf_op jit(solution)/shard_map/ppermute | solution.py:24
  9.5 0.0 collective-permute-start.3
  9.5 2.7 %collective-permute-done.1.facing = bf16[2,2,64,128]{3,2,1,0:T(8,128)(2,1)S(1)} collective-permute-done((bf16[2,2,64,128]{3,2,1,0:T(8,128)(2,1)S(1)}, bf16[2,2,64,128]{3,2,1,0:T(8,128)(2,1)S(1)}, u32[]{:S(2)}, u32[]{:S(2)}) %collective-permute-start.1) | collective-permute-done | bytes 65568 | tf_op jit(solution)/shard_map/ppermute | solution.py:24
  12.2 0.0 copy-start.5
  12.2 0.3 %collective-permute-start.2 = (bf16[3,2,32,128]{3,2,1,0:T(8,128)(2,1)S(1)}, bf16[3,2,32,128]{3,2,1,0:T(8,128)(2,1)S(1)}, u32[]{:S(2)}, u32[]{:S(2)}) collective-permute-start(bf16[3,2,32,128]{3,2,1,0:T(8,128)(2,1)S(1)} %slice.13.refs_0_), channel_id=1, source_target_pairs={{0,16},{16,0},{1,17},{17,1},{2,18},{18,2},{3,19},{19,3},{4,20},{20... | collective-permute-start | bytes 147464 | tf_op jit(solution)/shard_map/ppermute | solution.py:29
  12.6 1.7 %collective-permute-start.6 = (bf16[1,2,32,128]{3,2,1,0:T(8,128)(2,1)S(1)}, bf16[1,2,32,128]{3,2,1,0:T(8,128)(2,1)S(1)}, u32[]{:S(2)}, u32[]{:S(2)}) collective-permute-start(bf16[1,2,32,128]{3,2,1,0:T(8,128)(2,1)S(1)} %slice.14.refs_0_), channel_id=1, source_target_pairs={{0,16},{16,0},{1,17},{17,1},{2,18},{18,2},{3,19},{19,3},{4,20},{20... | collective-permute-start | bytes 49160 | tf_op jit(solution)/shard_map/ppermute | solution.py:29
  14.3 0.0 collective-permute-done.3.other
  14.3 0.0 copy-done.5
  14.3 0.6 %copy-done.6 = f32[16]{0:T(128)S(1)} copy-done((f32[16]{0:T(128)S(1)}, f32[16]{0:T(128)}, u32[]{:S(2)}) %copy-start.6) | copy-done | bytes 88
  15.0 0.8 %own.1.swept = bf16[256,1024]{1,0:T(8,128)(2,1)S(1)} custom-call(f32[1,128]{1,0:T(1,128)S(1)} %get-tuple-element.21.weight, f32[1,16]{1,0:T(1,128)S(1)} %bitcast.21, s32[32,128]{1,0:T(8,128)S(1)} %bitcast.20, bf16[2,1024,128]{2,1,0:T(8,128)(2,1)S(1)} %copy-done.1, bf16[2,2,64,128]{3,2,1,0:T(8,128)(2,1)S(1)} %collective-permute-done.1.facing, ...), custom_call_target="tpu_custom_call" | custom-call | flops 575000000 | bytes 1 | tf_op jit(solution)/shard_map/own/pallas_call | solution.py:229
  15.8 0.0 collective-permute-done.4.refs_1_
  15.8 0.4 %cross.1 = (bf16[128,256]{1,0:T(8,128)(2,1)S(1)}, bf16[128,256]{1,0:T(8,128)(2,1)S(1)}) custom-call(bf16[256,1024]{1,0:T(8,128)(2,1)S(1)} %own.1.swept, bf16[2,1024,128]{2,1,0:T(8,128)(2,1)S(1)} %copy-done.1, bf16[2,1024,128]{2,1,0:T(8,128)(2,1)S(1)} %collective-permute-done.4.refs_1_), custom_call_target="tpu_custom_call" | custom-call | flops 1 | bytes 1 | tf_op jit(solution)/shard_map/cross/pallas_call | solution.py:244
  16.2 0.1 collective-permute-done.2.refs_1_
  16.4 0.2 send.1
  16.6 0.1 collective-permute-start.5
  16.7 0.0 collective-permute-done.6.refs_1_
  16.7 1.8 %collective-permute-start.7 = (bf16[2,32,128]{2,1,0:T(8,128)(2,1)S(1)}, bf16[2,32,128]{2,1,0:T(8,128)(2,1)S(1)}, u32[]{:S(2)}, u32[]{:S(2)}) collective-permute-start(bf16[2,32,128]{2,1,0:T(8,128)(2,1)S(1)} %get-tuple-element.34), channel_id=1, source_target_pairs={{0,4},{1,5},{2,6},{3,7},{4,8},{5,13},{6,10},{7,15},{8,12},{9,1},{1... | collective-permute-start | bytes 49160 | tf_op jit(solution)/shard_map/ppermute | solution.py:46
  18.6 2.1 %collective-permute-start.8 = (bf16[2,32,128]{2,1,0:T(8,128)(2,1)S(1)}, bf16[2,32,128]{2,1,0:T(8,128)(2,1)S(1)}, u32[]{:S(2)}, u32[]{:S(2)}) collective-permute-start(bf16[2,32,128]{2,1,0:T(8,128)(2,1)S(1)} %get-tuple-element.35), channel_id=1, source_target_pairs={{0,12},{1,13},{2,14},{3,15},{4,0},{5,9},{6,2},{7,11},{8,4},{9,5},{... | collective-permute-start | bytes 49160 | tf_op jit(solution)/shard_map/ppermute | solution.py:46
  20.6 1.0 %collective-permute-start.9 = (bf16[2,32,128]{2,1,0:T(8,128)(2,1)S(1)}, bf16[2,32,128]{2,1,0:T(8,128)(2,1)S(1)}, u32[]{:S(2)}, u32[]{:S(2)}) collective-permute-start(bf16[2,32,128]{2,1,0:T(8,128)(2,1)S(1)} %get-tuple-element.36), channel_id=1, source_target_pairs={{0,8},{1,0},{2,10},{3,2},{4,12},{5,1},{6,14},{7,3},{8,9},{9,13},{1... | collective-permute-start | bytes 49160 | tf_op jit(solution)/shard_map/ppermute | solution.py:46
  21.6 0.0 collective-permute-done.5
  21.6 0.2 keep.1
  21.8 0.6 %collective-permute-done.7 = bf16[2,32,128]{2,1,0:T(8,128)(2,1)S(1)} collective-permute-done((bf16[2,32,128]{2,1,0:T(8,128)(2,1)S(1)}, bf16[2,32,128]{2,1,0:T(8,128)(2,1)S(1)}, u32[]{:S(2)}, u32[]{:S(2)}) %collective-permute-start.7) | collective-permute-done | bytes 16416 | tf_op jit(solution)/shard_map/ppermute | solution.py:46
  22.4 0.0 collective-permute-done.8
  22.5 0.6 %collective-permute-done.9 = bf16[2,32,128]{2,1,0:T(8,128)(2,1)S(1)} collective-permute-done((bf16[2,32,128]{2,1,0:T(8,128)(2,1)S(1)}, bf16[2,32,128]{2,1,0:T(8,128)(2,1)S(1)}, u32[]{:S(2)}, u32[]{:S(2)}) %collective-permute-start.9) | collective-permute-done | bytes 16416 | tf_op jit(solution)/shard_map/ppermute | solution.py:46
  23.1 0.6 %add_bitcast_fusion = f32[2,128,32]{1,2,0:T(8,128)} fusion(f32[2,32,128]{2,1,0:T(8,128)S(1)} %convert_add_fusion, bf16[2,32,128]{2,1,0:T(8,128)(2,1)S(1)} %collective-permute-done.9, pred[]{:T(512)S(6)} %and.58, pred[]{:T(512)S(6)} %and.57), kind=kLoop, calls=%fused_computation.2 | loop fusion | flops 32768 | bytes 81922 | tf_op jit(solution)/shard_map/transpose | solution.py:282
  (16 shorter events, 0.1 us)
Async XLA Ops:
  0.0 5.6 %copy-start.3 = (f32[4,8]{1,0:T(4,128)S(1)}, f32[4,8]{1,0:T(4,128)}, u32[]{:S(2)}) copy-start(f32[4,8]{1,0:T(4,128)} %noise.1) | copy-start | bytes 388
  0.0 15.8 %collective-permute-start.4 = (bf16[2,1024,128]{2,1,0:T(8,128)(2,1)}, bf16[2,1024,128]{2,1,0:T(8,128)(2,1)S(1)}, u32[]{:S(2)}, u32[]{:S(2)}) collective-permute-start(bf16[2,1024,128]{2,1,0:T(8,128)(2,1)} %refs_0_.1), channel_id=1, source_target_pairs={{0,16},{16,0},{1,17},{17,1},{2,18},{18,2},{3,19},{19,3},{4,20},{20... | collective-permute-start | bytes 1572872 | tf_op jit(solution)/shard_map/ppermute | solution.py:29
  3.0 2.6 %copy-start.4 = (s32[128]{0:T(128)S(1)}, s32[128]{0:T(128)}, u32[]{:S(2)}) copy-start(s32[128]{0:T(128)} %param.9) | copy-start | bytes 1540
  3.0 4.8 %collective-permute-start = (bf16[2,32,128]{2,1,0:T(8,128)(2,1)}, bf16[2,32,128]{2,1,0:T(8,128)(2,1)S(1)}, u32[]{:S(2)}, u32[]{:S(2)}) collective-permute-start(bf16[2,32,128]{2,1,0:T(8,128)(2,1)} %bitcast.16), channel_id=1, source_target_pairs={{0,8},{1,9},{2,10},{3,11},{4,12},{5,13},{6,14},{7,15},{8,0},{9,1},... | collective-permute-start | bytes 49160 | tf_op jit(solution)/shard_map/ppermute | solution.py:24
  5.6 1.0 %copy-start = (bf16[2,1024,128]{2,1,0:T(8,128)(2,1)S(1)}, bf16[2,1024,128]{2,1,0:T(8,128)(2,1)}, u32[]{:S(2)}) copy-start(bf16[2,1024,128]{2,1,0:T(8,128)(2,1)} %refs_0_.1) | copy-start | bytes 1572868
  6.6 0.7 %copy-start.2 = (bf16[2,128,32]{1,2,0:T(8,128)(2,1)S(1)}, bf16[2,128,32]{1,2,0:T(8,128)(2,1)}, u32[]{:S(2)}) copy-start(bf16[2,128,32]{1,2,0:T(8,128)(2,1)} %param.6) | copy-start | bytes 49156
  7.3 7.0 %copy-start.1 = (bf16[2,1024,128]{2,1,0:T(8,128)(2,1)S(1)}, bf16[2,1024,128]{2,1,0:T(8,128)(2,1)}, u32[]{:S(2)}) copy-start(bf16[2,1024,128]{2,1,0:T(8,128)(2,1)} %refs_0_.1) | copy-start | bytes 1572868
  7.8 4.3 %collective-permute-start.1 = (bf16[2,2,64,128]{3,2,1,0:T(8,128)(2,1)S(1)}, bf16[2,2,64,128]{3,2,1,0:T(8,128)(2,1)S(1)}, u32[]{:S(2)}, u32[]{:S(2)}) collective-permute-start(bf16[2,2,64,128]{3,2,1,0:T(8,128)(2,1)S(1)} %pad_maximum_fusion), channel_id=1, source_target_pairs={{0,4},{1,5},{2,6},{3,7},{4,0},{5,1},{6,2},{7,3},{8,12},{9,13},{10,... | collective-permute-start | bytes 196616 | tf_op jit(solution)/shard_map/ppermute | solution.py:24
  9.5 4.8 %collective-permute-start.3 = (bf16[2,64,128]{2,1,0:T(8,128)(2,1)S(1)}, bf16[2,64,128]{2,1,0:T(8,128)(2,1)S(1)}, u32[]{:S(2)}, u32[]{:S(2)}) collective-permute-start(bf16[2,64,128]{2,1,0:T(8,128)(2,1)S(1)} %get-tuple-element.25), channel_id=1, source_target_pairs={{0,1},{1,0},{2,3},{3,2},{4,8},{5,9},{6,10},{7,11},{8,4},{9,5},{10,... | collective-permute-start | bytes 98312 | tf_op jit(solution)/shard_map/ppermute | solution.py:38
  12.2 2.1 %copy-start.5 = (s32[4096]{0:T(1024)S(1)}, s32[4096]{0:T(1024)}, u32[]{:S(2)}) copy-start(s32[4096]{0:T(1024)} %param.11) | copy-start | bytes 49156
  12.2 4.2 %collective-permute-start.2 = (bf16[3,2,32,128]{3,2,1,0:T(8,128)(2,1)S(1)}, bf16[3,2,32,128]{3,2,1,0:T(8,128)(2,1)S(1)}, u32[]{:S(2)}, u32[]{:S(2)}) collective-permute-start(bf16[3,2,32,128]{3,2,1,0:T(8,128)(2,1)S(1)} %slice.13.refs_0_), channel_id=1, source_target_pairs={{0,16},{16,0},{1,17},{17,1},{2,18},{18,2},{3,19},{19,3},{4,20},{20... | collective-permute-start | bytes 147464 | tf_op jit(solution)/shard_map/ppermute | solution.py:29
  12.6 4.1 %collective-permute-start.6 = (bf16[1,2,32,128]{3,2,1,0:T(8,128)(2,1)S(1)}, bf16[1,2,32,128]{3,2,1,0:T(8,128)(2,1)S(1)}, u32[]{:S(2)}, u32[]{:S(2)}) collective-permute-start(bf16[1,2,32,128]{3,2,1,0:T(8,128)(2,1)S(1)} %slice.14.refs_0_), channel_id=1, source_target_pairs={{0,16},{16,0},{1,17},{17,1},{2,18},{18,2},{3,19},{19,3},{4,20},{20... | collective-permute-start | bytes 49160 | tf_op jit(solution)/shard_map/ppermute | solution.py:29
  14.3 0.7 %copy-start.6 = (f32[16]{0:T(128)S(1)}, f32[16]{0:T(128)}, u32[]{:S(2)}) copy-start(f32[16]{0:T(128)} %param.10) | copy-start | bytes 196
  16.6 5.0 %collective-permute-start.5 = (bf16[2,32,128]{2,1,0:T(8,128)(2,1)S(1)}, bf16[2,32,128]{2,1,0:T(8,128)(2,1)S(1)}, u32[]{:S(2)}, u32[]{:S(2)}) collective-permute-start(bf16[2,32,128]{2,1,0:T(8,128)(2,1)S(1)} %get-tuple-element.28), channel_id=1, source_target_pairs={{0,1},{1,9},{2,3},{3,11},{4,5},{5,4},{6,7},{7,6},{8,0},{9,8},{10,2... | collective-permute-start | bytes 49160 | tf_op jit(solution)/shard_map/ppermute | solution.py:46
  16.7 5.7 %collective-permute-start.7 = (bf16[2,32,128]{2,1,0:T(8,128)(2,1)S(1)}, bf16[2,32,128]{2,1,0:T(8,128)(2,1)S(1)}, u32[]{:S(2)}, u32[]{:S(2)}) collective-permute-start(bf16[2,32,128]{2,1,0:T(8,128)(2,1)S(1)} %get-tuple-element.34), channel_id=1, source_target_pairs={{0,4},{1,5},{2,6},{3,7},{4,8},{5,13},{6,10},{7,15},{8,12},{9,1},{1... | collective-permute-start | bytes 49160 | tf_op jit(solution)/shard_map/ppermute | solution.py:46
  18.6 3.9 %collective-permute-start.8 = (bf16[2,32,128]{2,1,0:T(8,128)(2,1)S(1)}, bf16[2,32,128]{2,1,0:T(8,128)(2,1)S(1)}, u32[]{:S(2)}, u32[]{:S(2)}) collective-permute-start(bf16[2,32,128]{2,1,0:T(8,128)(2,1)S(1)} %get-tuple-element.35), channel_id=1, source_target_pairs={{0,12},{1,13},{2,14},{3,15},{4,0},{5,9},{6,2},{7,11},{8,4},{9,5},{... | collective-permute-start | bytes 49160 | tf_op jit(solution)/shard_map/ppermute | solution.py:46
  20.6 2.4 %collective-permute-start.9 = (bf16[2,32,128]{2,1,0:T(8,128)(2,1)S(1)}, bf16[2,32,128]{2,1,0:T(8,128)(2,1)S(1)}, u32[]{:S(2)}, u32[]{:S(2)}) collective-permute-start(bf16[2,32,128]{2,1,0:T(8,128)(2,1)S(1)} %get-tuple-element.36), channel_id=1, source_target_pairs={{0,8},{1,0},{2,10},{3,2},{4,12},{5,1},{6,14},{7,3},{8,9},{9,13},{1... | collective-permute-start | bytes 49160 | tf_op jit(solution)/shard_map/ppermute | solution.py:46

commit v12 on v11

--- a/solution.py
+++ b/solution.py
@@ -258,7 +258,7 @@
         compiler_params=PARAMS,
         name="send",
     )(given, *rests[0], *pairs))
-    sends[1], rests[1] = lax.optimization_barrier((sends[1], rests[1]))
+    sends[3], rests[1] = lax.optimization_barrier((sends[3], rests[1]))
     shares = [routed(send, "par", nfreq, step) for send, step in zip(sends, ROUTES)]
     shares[0], kept = lax.optimization_barrier((shares[0], kept))
     keep = pl.pallas_call(

time: 23.9 us -> 23.9 us (level)
  no operation moved by 1% of the time
where the time goes in v12:
time: 23.9 us; the launch traced here: 23.7 us
  starting transfers between devices  14.2 us (59%)
  waiting for transfers between devices  4.51 us (19%)
  local copies, waits for them, and re-layouts  2.44 us (10%)
  Pallas kernels  1.67 us (7%)
  other arithmetic  0.68 us (3%)
    ppermute x3, starting transfers between devices, turned(): lax.ppermute(value, axis, [(i, (i + step) % size) for i in range(size)])  5.06 us
    ppermute x4, starting transfers between devices, routed(): return lax.ppermute(value, axis, pairs)  4.95 us
    ppermute x2, starting transfers between devices, swapped(): lax.ppermute(value, axis, [(i, i ^ mask) for i in range(lax.axis_size(axi...  4.23 us
    ppermute x2, waiting for transfers between devices, swapped(): lax.ppermute(value, axis, [(i, i ^ mask) for i in range(lax.axis_size(axi...  3.09 us
    unnamed x14, local copies, waits for them, and re-layouts  2.42 us
    ppermute x4, waiting for transfers between devices, routed(): return lax.ppermute(value, axis, pairs)  1.23 us
    pallas_call x1, Pallas kernels, shards(): pl.pallas_call(functools.partial(own_kernel, nfreq), out_shape=jax.ShapeD...  0.78 us
    transpose x1, other arithmetic, shards(): return jnp.transpose(keep, (0, 2, 1))  0.62 us
  transfers between devices with their start and end apart: 10, of which 5 were waited for; matrix products, arithmetic and copies ran while one was open for 0% of the time, Pallas kernels for 6%

profile of v12, /device:TPU:0, one launch (start us, length us, event | category | flops | bytes accessed | tf_op | source)
XLA Modules:
  0.0 23.7 jit_solution(5303087248891551885)
XLA Ops:
  0.0 3.0 %collective-permute-start.4 = (bf16[2,1024,128]{2,1,0:T(8,128)(2,1)}, bf16[2,1024,128]{2,1,0:T(8,128)(2,1)S(1)}, u32[]{:S(2)}, u32[]{:S(2)}) collective-permute-start(bf16[2,1024,128]{2,1,0:T(8,128)(2,1)} %refs_0_.1), channel_id=1, source_target_pairs={{0,16},{16,0},{1,17},{17,1},{2,18},{18,2},{3,19},{19,3},{4,20},{20... | collective-permute-start | bytes 1572872 | tf_op jit(solution)/shard_map/ppermute | solution.py:29
  3.0 2.6 %collective-permute-start = (bf16[2,32,128]{2,1,0:T(8,128)(2,1)}, bf16[2,32,128]{2,1,0:T(8,128)(2,1)S(1)}, u32[]{:S(2)}, u32[]{:S(2)}) collective-permute-start(bf16[2,32,128]{2,1,0:T(8,128)(2,1)} %bitcast.16), channel_id=1, source_target_pairs={{0,8},{1,9},{2,10},{3,11},{4,12},{5,13},{6,14},{7,15},{8,0},{9,1},... | collective-permute-start | bytes 49160 | tf_op jit(solution)/shard_map/ppermute | solution.py:24
  5.6 0.0 copy-done.4
  5.6 1.0 %copy-done = bf16[2,1024,128]{2,1,0:T(8,128)(2,1)S(1)} copy-done((bf16[2,1024,128]{2,1,0:T(8,128)(2,1)S(1)}, bf16[2,1024,128]{2,1,0:T(8,128)(2,1)}, u32[]{:S(2)}) %copy-start) | copy-done | bytes 524312
  6.6 0.7 %copy-done.2 = bf16[2,128,32]{1,2,0:T(8,128)(2,1)S(1)} copy-done((bf16[2,128,32]{1,2,0:T(8,128)(2,1)S(1)}, bf16[2,128,32]{1,2,0:T(8,128)(2,1)}, u32[]{:S(2)}) %copy-start.2) | copy-done | bytes 16408
  7.3 0.1 prep.1
  7.4 0.4 %collective-permute-done = bf16[2,32,128]{2,1,0:T(8,128)(2,1)S(1)} collective-permute-done((bf16[2,32,128]{2,1,0:T(8,128)(2,1)}, bf16[2,32,128]{2,1,0:T(8,128)(2,1)S(1)}, u32[]{:S(2)}, u32[]{:S(2)}) %collective-permute-start) | collective-permute-done | bytes 16416 | tf_op jit(solution)/shard_map/ppermute | solution.py:24
  7.8 1.6 %collective-permute-start.1 = (bf16[2,2,64,128]{3,2,1,0:T(8,128)(2,1)S(1)}, bf16[2,2,64,128]{3,2,1,0:T(8,128)(2,1)S(1)}, u32[]{:S(2)}, u32[]{:S(2)}) collective-permute-start(bf16[2,2,64,128]{3,2,1,0:T(8,128)(2,1)S(1)} %pad_maximum_fusion), channel_id=1, source_target_pairs={{0,4},{1,5},{2,6},{3,7},{4,0},{5,1},{6,2},{7,3},{8,12},{9,13},{10,... | collective-permute-start | bytes 196616 | tf_op jit(solution)/shard_map/ppermute | solution.py:24
  9.5 0.0 collective-permute-start.3
  9.5 2.7 %collective-permute-done.1.facing = bf16[2,2,64,128]{3,2,1,0:T(8,128)(2,1)S(1)} collective-permute-done((bf16[2,2,64,128]{3,2,1,0:T(8,128)(2,1)S(1)}, bf16[2,2,64,128]{3,2,1,0:T(8,128)(2,1)S(1)}, u32[]{:S(2)}, u32[]{:S(2)}) %collective-permute-start.1) | collective-permute-done | bytes 65568 | tf_op jit(solution)/shard_map/ppermute | solution.py:24
  12.2 0.0 copy-start.5
  12.2 0.3 %collective-permute-start.2 = (bf16[3,2,32,128]{3,2,1,0:T(8,128)(2,1)S(1)}, bf16[3,2,32,128]{3,2,1,0:T(8,128)(2,1)S(1)}, u32[]{:S(2)}, u32[]{:S(2)}) collective-permute-start(bf16[3,2,32,128]{3,2,1,0:T(8,128)(2,1)S(1)} %slice.13.refs_0_), channel_id=1, source_target_pairs={{0,16},{16,0},{1,17},{17,1},{2,18},{18,2},{3,19},{19,3},{4,20},{20... | collective-permute-start | bytes 147464 | tf_op jit(solution)/shard_map/ppermute | solution.py:29
  12.6 1.7 %collective-permute-start.6 = (bf16[1,2,32,128]{3,2,1,0:T(8,128)(2,1)S(1)}, bf16[1,2,32,128]{3,2,1,0:T(8,128)(2,1)S(1)}, u32[]{:S(2)}, u32[]{:S(2)}) collective-permute-start(bf16[1,2,32,128]{3,2,1,0:T(8,128)(2,1)S(1)} %slice.14.refs_0_), channel_id=1, source_target_pairs={{0,16},{16,0},{1,17},{17,1},{2,18},{18,2},{3,19},{19,3},{4,20},{20... | collective-permute-start | bytes 49160 | tf_op jit(solution)/shard_map/ppermute | solution.py:29
  14.3 0.0 collective-permute-done.3.other
  14.3 0.0 copy-done.5
  14.3 0.6 %copy-done.6 = f32[16]{0:T(128)S(1)} copy-done((f32[16]{0:T(128)S(1)}, f32[16]{0:T(128)}, u32[]{:S(2)}) %copy-start.6) | copy-done | bytes 88
  15.0 0.8 %own.1.swept = bf16[256,1024]{1,0:T(8,128)(2,1)S(1)} custom-call(f32[1,128]{1,0:T(1,128)S(1)} %get-tuple-element.21.weight, f32[1,16]{1,0:T(1,128)S(1)} %bitcast.21, s32[32,128]{1,0:T(8,128)S(1)} %bitcast.20, bf16[2,1024,128]{2,1,0:T(8,128)(2,1)S(1)} %copy-done.1, bf16[2,2,64,128]{3,2,1,0:T(8,128)(2,1)S(1)} %collective-permute-done.1.facing, ...), custom_call_target="tpu_custom_call" | custom-call | flops 575000000 | bytes 1 | tf_op jit(solution)/shard_map/own/pallas_call | solution.py:229
  15.8 0.0 collective-permute-done.4.refs_1_
  15.8 0.4 %cross.1 = (bf16[128,256]{1,0:T(8,128)(2,1)S(1)}, bf16[128,256]{1,0:T(8,128)(2,1)S(1)}) custom-call(bf16[256,1024]{1,0:T(8,128)(2,1)S(1)} %own.1.swept, bf16[2,1024,128]{2,1,0:T(8,128)(2,1)S(1)} %copy-done.1, bf16[2,1024,128]{2,1,0:T(8,128)(2,1)S(1)} %collective-permute-done.4.refs_1_), custom_call_target="tpu_custom_call" | custom-call | flops 1 | bytes 1 | tf_op jit(solution)/shard_map/cross/pallas_call | solution.py:244
  16.2 0.1 collective-permute-done.2.refs_1_
  16.4 0.2 send.1
  16.6 0.1 collective-permute-start.5
  16.7 0.0 collective-permute-done.6.refs_1_
  16.7 1.8 %collective-permute-start.7 = (bf16[2,32,128]{2,1,0:T(8,128)(2,1)S(1)}, bf16[2,32,128]{2,1,0:T(8,128)(2,1)S(1)}, u32[]{:S(2)}, u32[]{:S(2)}) collective-permute-start(bf16[2,32,128]{2,1,0:T(8,128)(2,1)S(1)} %get-tuple-element.34), channel_id=1, source_target_pairs={{0,4},{1,5},{2,6},{3,7},{4,8},{5,13},{6,10},{7,15},{8,12},{9,1},{1... | collective-permute-start | bytes 49160 | tf_op jit(solution)/shard_map/ppermute | solution.py:46
  18.6 2.1 %collective-permute-start.8 = (bf16[2,32,128]{2,1,0:T(8,128)(2,1)S(1)}, bf16[2,32,128]{2,1,0:T(8,128)(2,1)S(1)}, u32[]{:S(2)}, u32[]{:S(2)}) collective-permute-start(bf16[2,32,128]{2,1,0:T(8,128)(2,1)S(1)} %get-tuple-element.35), channel_id=1, source_target_pairs={{0,12},{1,13},{2,14},{3,15},{4,0},{5,9},{6,2},{7,11},{8,4},{9,5},{... | collective-permute-start | bytes 49160 | tf_op jit(solution)/shard_map/ppermute | solution.py:46
  20.6 1.0 %collective-permute-start.9 = (bf16[2,32,128]{2,1,0:T(8,128)(2,1)S(1)}, bf16[2,32,128]{2,1,0:T(8,128)(2,1)S(1)}, u32[]{:S(2)}, u32[]{:S(2)}) collective-permute-start(bf16[2,32,128]{2,1,0:T(8,128)(2,1)S(1)} %get-tuple-element.36), channel_id=1, source_target_pairs={{0,8},{1,0},{2,10},{3,2},{4,12},{5,1},{6,14},{7,3},{8,9},{9,13},{1... | collective-permute-start | bytes 49160 | tf_op jit(solution)/shard_map/ppermute | solution.py:46
  21.6 0.0 collective-permute-done.5
  21.6 0.2 keep.1
  21.8 0.6 %collective-permute-done.7 = bf16[2,32,128]{2,1,0:T(8,128)(2,1)S(1)} collective-permute-done((bf16[2,32,128]{2,1,0:T(8,128)(2,1)S(1)}, bf16[2,32,128]{2,1,0:T(8,128)(2,1)S(1)}, u32[]{:S(2)}, u32[]{:S(2)}) %collective-permute-start.7) | collective-permute-done | bytes 16416 | tf_op jit(solution)/shard_map/ppermute | solution.py:46
  22.4 0.0 collective-permute-done.8
  22.5 0.6 %collective-permute-done.9 = bf16[2,32,128]{2,1,0:T(8,128)(2,1)S(1)} collective-permute-done((bf16[2,32,128]{2,1,0:T(8,128)(2,1)S(1)}, bf16[2,32,128]{2,1,0:T(8,128)(2,1)S(1)}, u32[]{:S(2)}, u32[]{:S(2)}) %collective-permute-start.9) | collective-permute-done | bytes 16416 | tf_op jit(solution)/shard_map/ppermute | solution.py:46
  23.1 0.6 %add_bitcast_fusion = f32[2,128,32]{1,2,0:T(8,128)} fusion(f32[2,32,128]{2,1,0:T(8,128)S(1)} %convert_add_fusion, bf16[2,32,128]{2,1,0:T(8,128)(2,1)S(1)} %collective-permute-done.9, pred[]{:T(512)S(6)} %and.58, pred[]{:T(512)S(6)} %and.57), kind=kLoop, calls=%fused_computation.2 | loop fusion | flops 32768 | bytes 81922 | tf_op jit(solution)/shard_map/transpose | solution.py:282
  (16 shorter events, 0.1 us)
Async XLA Ops:
  0.0 5.6 %copy-start.3 = (f32[4,8]{1,0:T(4,128)S(1)}, f32[4,8]{1,0:T(4,128)}, u32[]{:S(2)}) copy-start(f32[4,8]{1,0:T(4,128)} %noise.1) | copy-start | bytes 388
  0.0 15.8 %collective-permute-start.4 = (bf16[2,1024,128]{2,1,0:T(8,128)(2,1)}, bf16[2,1024,128]{2,1,0:T(8,128)(2,1)S(1)}, u32[]{:S(2)}, u32[]{:S(2)}) collective-permute-start(bf16[2,1024,128]{2,1,0:T(8,128)(2,1)} %refs_0_.1), channel_id=1, source_target_pairs={{0,16},{16,0},{1,17},{17,1},{2,18},{18,2},{3,19},{19,3},{4,20},{20... | collective-permute-start | bytes 1572872 | tf_op jit(solution)/shard_map/ppermute | solution.py:29
  3.0 2.6 %copy-start.4 = (s32[128]{0:T(128)S(1)}, s32[128]{0:T(128)}, u32[]{:S(2)}) copy-start(s32[128]{0:T(128)} %param.9) | copy-start | bytes 1540
  3.0 4.8 %collective-permute-start = (bf16[2,32,128]{2,1,0:T(8,128)(2,1)}, bf16[2,32,128]{2,1,0:T(8,128)(2,1)S(1)}, u32[]{:S(2)}, u32[]{:S(2)}) collective-permute-start(bf16[2,32,128]{2,1,0:T(8,128)(2,1)} %bitcast.16), channel_id=1, source_target_pairs={{0,8},{1,9},{2,10},{3,11},{4,12},{5,13},{6,14},{7,15},{8,0},{9,1},... | collective-permute-start | bytes 49160 | tf_op jit(solution)/shard_map/ppermute | solution.py:24
  5.6 1.0 %copy-start = (bf16[2,1024,128]{2,1,0:T(8,128)(2,1)S(1)}, bf16[2,1024,128]{2,1,0:T(8,128)(2,1)}, u32[]{:S(2)}) copy-start(bf16[2,1024,128]{2,1,0:T(8,128)(2,1)} %refs_0_.1) | copy-start | bytes 1572868
  6.6 0.7 %copy-start.2 = (bf16[2,128,32]{1,2,0:T(8,128)(2,1)S(1)}, bf16[2,128,32]{1,2,0:T(8,128)(2,1)}, u32[]{:S(2)}) copy-start(bf16[2,128,32]{1,2,0:T(8,128)(2,1)} %param.6) | copy-start | bytes 49156
  7.3 7.0 %copy-start.1 = (bf16[2,1024,128]{2,1,0:T(8,128)(2,1)S(1)}, bf16[2,1024,128]{2,1,0:T(8,128)(2,1)}, u32[]{:S(2)}) copy-start(bf16[2,1024,128]{2,1,0:T(8,128)(2,1)} %refs_0_.1) | copy-start | bytes 1572868
  7.8 4.3 %collective-permute-start.1 = (bf16[2,2,64,128]{3,2,1,0:T(8,128)(2,1)S(1)}, bf16[2,2,64,128]{3,2,1,0:T(8,128)(2,1)S(1)}, u32[]{:S(2)}, u32[]{:S(2)}) collective-permute-start(bf16[2,2,64,128]{3,2,1,0:T(8,128)(2,1)S(1)} %pad_maximum_fusion), channel_id=1, source_target_pairs={{0,4},{1,5},{2,6},{3,7},{4,0},{5,1},{6,2},{7,3},{8,12},{9,13},{10,... | collective-permute-start | bytes 196616 | tf_op jit(solution)/shard_map/ppermute | solution.py:24
  9.5 4.8 %collective-permute-start.3 = (bf16[2,64,128]{2,1,0:T(8,128)(2,1)S(1)}, bf16[2,64,128]{2,1,0:T(8,128)(2,1)S(1)}, u32[]{:S(2)}, u32[]{:S(2)}) collective-permute-start(bf16[2,64,128]{2,1,0:T(8,128)(2,1)S(1)} %get-tuple-element.25), channel_id=1, source_target_pairs={{0,1},{1,0},{2,3},{3,2},{4,8},{5,9},{6,10},{7,11},{8,4},{9,5},{10,... | collective-permute-start | bytes 98312 | tf_op jit(solution)/shard_map/ppermute | solution.py:38
  12.2 2.1 %copy-start.5 = (s32[4096]{0:T(1024)S(1)}, s32[4096]{0:T(1024)}, u32[]{:S(2)}) copy-start(s32[4096]{0:T(1024)} %param.11) | copy-start | bytes 49156
  12.2 4.2 %collective-permute-start.2 = (bf16[3,2,32,128]{3,2,1,0:T(8,128)(2,1)S(1)}, bf16[3,2,32,128]{3,2,1,0:T(8,128)(2,1)S(1)}, u32[]{:S(2)}, u32[]{:S(2)}) collective-permute-start(bf16[3,2,32,128]{3,2,1,0:T(8,128)(2,1)S(1)} %slice.13.refs_0_), channel_id=1, source_target_pairs={{0,16},{16,0},{1,17},{17,1},{2,18},{18,2},{3,19},{19,3},{4,20},{20... | collective-permute-start | bytes 147464 | tf_op jit(solution)/shard_map/ppermute | solution.py:29
  12.6 4.1 %collective-permute-start.6 = (bf16[1,2,32,128]{3,2,1,0:T(8,128)(2,1)S(1)}, bf16[1,2,32,128]{3,2,1,0:T(8,128)(2,1)S(1)}, u32[]{:S(2)}, u32[]{:S(2)}) collective-permute-start(bf16[1,2,32,128]{3,2,1,0:T(8,128)(2,1)S(1)} %slice.14.refs_0_), channel_id=1, source_target_pairs={{0,16},{16,0},{1,17},{17,1},{2,18},{18,2},{3,19},{19,3},{4,20},{20... | collective-permute-start | bytes 49160 | tf_op jit(solution)/shard_map/ppermute | solution.py:29
  14.3 0.7 %copy-start.6 = (f32[16]{0:T(128)S(1)}, f32[16]{0:T(128)}, u32[]{:S(2)}) copy-start(f32[16]{0:T(128)} %param.10) | copy-start | bytes 196
  16.6 5.0 %collective-permute-start.5 = (bf16[2,32,128]{2,1,0:T(8,128)(2,1)S(1)}, bf16[2,32,128]{2,1,0:T(8,128)(2,1)S(1)}, u32[]{:S(2)}, u32[]{:S(2)}) collective-permute-start(bf16[2,32,128]{2,1,0:T(8,128)(2,1)S(1)} %get-tuple-element.28), channel_id=1, source_target_pairs={{0,1},{1,9},{2,3},{3,11},{4,5},{5,4},{6,7},{7,6},{8,0},{9,8},{10,2... | collective-permute-start | bytes 49160 | tf_op jit(solution)/shard_map/ppermute | solution.py:46
  16.7 5.7 %collective-permute-start.7 = (bf16[2,32,128]{2,1,0:T(8,128)(2,1)S(1)}, bf16[2,32,128]{2,1,0:T(8,128)(2,1)S(1)}, u32[]{:S(2)}, u32[]{:S(2)}) collective-permute-start(bf16[2,32,128]{2,1,0:T(8,128)(2,1)S(1)} %get-tuple-element.34), channel_id=1, source_target_pairs={{0,4},{1,5},{2,6},{3,7},{4,8},{5,13},{6,10},{7,15},{8,12},{9,1},{1... | collective-permute-start | bytes 49160 | tf_op jit(solution)/shard_map/ppermute | solution.py:46
  18.6 3.9 %collective-permute-start.8 = (bf16[2,32,128]{2,1,0:T(8,128)(2,1)S(1)}, bf16[2,32,128]{2,1,0:T(8,128)(2,1)S(1)}, u32[]{:S(2)}, u32[]{:S(2)}) collective-permute-start(bf16[2,32,128]{2,1,0:T(8,128)(2,1)S(1)} %get-tuple-element.35), channel_id=1, source_target_pairs={{0,12},{1,13},{2,14},{3,15},{4,0},{5,9},{6,2},{7,11},{8,4},{9,5},{... | collective-permute-start | bytes 49160 | tf_op jit(solution)/shard_map/ppermute | solution.py:46
  20.6 2.4 %collective-permute-start.9 = (bf16[2,32,128]{2,1,0:T(8,128)(2,1)S(1)}, bf16[2,32,128]{2,1,0:T(8,128)(2,1)S(1)}, u32[]{:S(2)}, u32[]{:S(2)}) collective-permute-start(bf16[2,32,128]{2,1,0:T(8,128)(2,1)S(1)} %get-tuple-element.36), channel_id=1, source_target_pairs={{0,8},{1,0},{2,10},{3,2},{4,12},{5,1},{6,14},{7,3},{8,9},{9,13},{1... | collective-permute-start | bytes 49160 | tf_op jit(solution)/shard_map/ppermute | solution.py:46
